TPU v7x, 32 devices: a whole 2x2x4 slice. The times are simulated.
32 devices in a mesh: pool: 4 (over y, core), tgt: 8 (over z, x).
Axes of the slice: x: 2, y: 2, z: 4, core: 2. Of those that a mesh axis runs over, the one named last changes fastest.
Arguments:
- pool_grads: bfloat16 [8192, 16384], P('pool', 'tgt'), may hold values from -6 to 6
- target_grads: bfloat16 [512, 16384], P('pool', 'tgt'), may hold values from -6 to 6
- precond: bfloat16 [32, 512, 512], P('tgt'), as said below
- active: int32 [4, 16], replicated, may hold values from 0 to 31, as said below
Outputs:
- scores: float32 [8192, 512], P(('pool', 'tgt'))
Inputs may be any that keep to these rules, and one draw needn't show every extreme that they name: `active`: each row lists 16 distinct blocks; rows 2k and 2k + 1 together list every block exactly once. `precond`: each block is symmetric with a positive diagonal.
All inputs are finite; a program needn't handle non-finite values.
Results may differ from a plain program's by a relative error of at most 0.0029.
Values may be sent and summed in bfloat16 or wider, within the bound.
No kernel may reach another device: no remote copies, remote signals or barrier semaphores. Data moves between devices by JAX's collectives and lax.ppermute only.
A program may use at most 64 MiB of HBM per device.

v0:
```python
import jax
import jax.numpy as jnp
from jax import lax
from jax.sharding import PartitionSpec as P

PROWS = 128


def local(pool_grads, target_grads, precond, active):
    blocks_here = precond.shape[0]
    bsize = precond.shape[1]
    panels = active.shape[0]
    scale = (active.shape[1] * bsize) ** (-0.5)
    first = lax.axis_index("tgt") * blocks_here
    owned = first + jnp.arange(blocks_here, dtype=jnp.int32)
    mask = jnp.sum((active[:, :, None] == owned[None, None, :]).astype(jnp.float32), axis=1)
    whole = lax.all_gather(target_grads, "pool", axis=0, tiled=True)
    count = whole.shape[0]
    panel_of = jnp.arange(count, dtype=jnp.int32) // PROWS
    onehot = (panel_of[:, None] == jnp.arange(panels, dtype=jnp.int32)[None, :]).astype(jnp.float32)
    row_mask = jnp.dot(onehot, mask)
    shaped = whole.reshape(count, blocks_here, bsize)
    product = jnp.einsum("rbi,bij->rbj", shaped, precond, preferred_element_type=jnp.float32)
    product = product * row_mask[:, :, None] * scale
    conditioned = product.astype(jnp.bfloat16).reshape(count, blocks_here * bsize)
    return lax.psum_scatter(
        lax.dot_general(
            pool_grads, conditioned, (((1,), (1,)), ((), ())), preferred_element_type=jnp.float32
        ),
        "tgt",
        scatter_dimension=0,
        tiled=True,
    )


def solution(mesh):
    return jax.shard_map(
        local,
        mesh=mesh,
        in_specs=(P("pool", "tgt"), P("pool", "tgt"), P("tgt", None, None), P()),
        out_specs=P(("pool", "tgt"), None),
        check_vma=False,
    )
```

profile of v0, /device:TPU:0, one launch (start us, length us, event | category | flops | bytes accessed | tf_op | source)
XLA Modules:
  0.0 144.4 jit_solution(2317878927838466790)
XLA Ops:
  6.5 0.0 copy-start
  6.5 0.0 all-gather.2.cloned.1.call-start
  6.5 2.2 %copy.11 = bf16[128,2048]{0,1:T(8,128)(2,1)} copy(bf16[128,2048]{1,0:T(8,128)(2,1)} %param.5) | data formatting | bytes 1048576 | tf_op args[1]
  8.7 0.0 all-gather.2.cloned.1.call-update
  8.8 0.0 reduce-scatter.2.cloned.1.call-start
  8.8 0.8 convert_reduce_fusion
  9.7 0.3 fusion.2
  9.9 24.6 %all-gather.2.cloned.1.call-done = bf16[512,2048]{0,1:T(8,128)(2,1)} async-done(((bf16[128,2048]{0,1:T(8,128)(2,1)}), bf16[512,2048]{0,1:T(8,128)(2,1)}) %all-gather.2.cloned.1.call-update) | async-done | bytes 2097168 | tf_op jit(solution)/shard_map/all_gather | solution.py:17
  34.5 0.0 copy-done
  34.5 2.9 %fusion.1 = bf16[512,4,512]{0,2,1:T(8,128)(2,1)S(1)} fusion(bf16[4,512,512]{2,1,0:T(8,128)(2,1)S(1)} %copy-done, bf16[512,4,512]{0,2,1:T(8,128)(2,1)} %bitcast.15, f32[512,4]{0,1:T(4,128)S(1)} %fusion.2), kind=kOutput, calls=%fused_computation.2 | convolution fusion | flops 1076887552 | bytes 6299648 | tf_op jit(solution)/shard_map/rbi,bij->rbj/dot_general | solution.py:23
  37.4 9.6 %convolution_bitcast_fusion = f32[2048,512]{0,1:T(8,128)} fusion(bf16[512,2048]{0,1:T(8,128)(2,1)S(1)} %bitcast.16, bf16[2048,2048]{1,0:T(8,128)(2,1)} %param.4), kind=kOutput, calls=%fused_computation.3 | convolution fusion | flops 4294967296 | bytes 14680064 | tf_op jit(solution)/shard_map/dot_general | solution.py:27
  47.1 0.0 reduce-scatter.2.cloned.1.call-update
  47.1 88.5 %reduce-scatter.2.cloned.1.call-done = f32[256,512]{0,1:T(8,128)} async-done(((f32[2048,512]{0,1:T(8,128)}), f32[256,512]{0,1:T(8,128)}) %reduce-scatter.2.cloned.1.call-update) | async-done | bytes 524304 | tf_op jit(solution)/shard_map/reduce_scatter | solution.py:26
  135.5 2.0 %copy.14 = f32[256,512]{1,0:T(8,128)} copy(f32[256,512]{0,1:T(8,128)} %reduce-scatter.2.cloned.1.call-done) | data formatting | bytes 1048576 | tf_op jit(solution)/shard_map/reduce_scatter | solution.py:26
  (2 shorter events, 0.0 us)
Async XLA Ops:
  6.5 28.0 %copy-start = (bf16[4,512,512]{2,1,0:T(8,128)(2,1)S(1)}, bf16[4,512,512]{2,1,0:T(8,128)(2,1)}, u32[]{:S(2)}) copy-start(bf16[4,512,512]{2,1,0:T(8,128)(2,1)} %param.6) | copy-start | bytes 6291460
  6.5 28.0 %all-gather.2.cloned.1.call-start = ((), (), s32[]{:S(2)}) async-start(), calls=%async_computation.1 | async-start | bytes 2621440 | tf_op jit(solution)/shard_map/all_gather | solution.py:17
  8.8 126.8 %reduce-scatter.2.cloned.1.call-start = ((), (), s32[]{:S(2)}) async-start(), calls=%async_computation.2 | async-start | bytes 4718592 | tf_op jit(solution)/shard_map/reduce_scatter | solution.py:26
Sparse Core Ops, SparseCore 0:
  8.9 25.5 all-gather.1
  47.2 88.2 reduce-scatter.1
where the time goes:
time: 145 us; the launch traced here: 144 us
  waiting for transfers between devices  113 us (78%)
  between operations  13.4 us (9%)
  matrix products  12.8 us (9%)
  local copies, waits for them, and re-layouts  4.23 us (3%)
    reduce_scatter x1, waiting for transfers between devices, local(): lax.psum_scatter(lax.dot_general(pool_grads, conditioned, (((1,), (1,)),...  88.5 us
    all_gather x1, waiting for transfers between devices, local(): whole = lax.all_gather(target_grads, 'pool', axis=0, tiled=True)  24.6 us
    dot_general x1, matrix products, local(): lax.dot_general(pool_grads, conditioned, (((1,), (1,)), ((), ())), prefer...  9.62 us
    dot_general x1, matrix products, local(): jnp.einsum('rbi,bij->rbj', shaped, precond, preferred_element_type=jnp.fl...  2.92 us
  transfers between devices with their start and end apart: 2, of which 2 were waited for; matrix products, arithmetic and copies ran while one was open for 1% of the time, Pallas kernels for 0%

commit v1 on v0

v1 whole, which is shorter than its diff:
```python
import functools

import jax
import jax.numpy as jnp
from jax import lax
from jax.experimental import pallas as pl
from jax.experimental.pallas import tpu as pltpu
from jax.sharding import PartitionSpec as P

PROWS = 128
F32, BF16 = jnp.float32, jnp.bfloat16
VMEM = pl.BlockSpec(memory_space=pltpu.VMEM)


def call(body, outs, *args, flops=0, mib=20, scratch=()):
    return pl.pallas_call(
        body,
        in_specs=[VMEM] * len(args),
        out_specs=[VMEM] * len(outs),
        out_shape=[jax.ShapeDtypeStruct(shape, dtype) for shape, dtype in outs],
        scratch_shapes=list(scratch),
        compiler_params=pltpu.CompilerParams(vmem_limit_bytes=mib * 2**20),
        cost_estimate=pl.CostEstimate(flops=flops, bytes_accessed=0, transcendentals=0),
    )(*args)


def listed(active, panel, block):
    rows = lax.broadcasted_iota(jnp.int32, active.shape, 0)
    return jnp.max(((active == block) & (rows == panel)).astype(jnp.int32))


def place(group):
    return lax.axis_index("tgt"), lax.axis_index("pool") // group


def near_kernel(group, scale, active, own, sib, pre, right, half):
    j, panel = place(group)
    core = panel & 1
    blocks, bs, _ = pre.shape
    depth = blocks // 2
    table = active[...]
    for b in range(blocks):
        even = listed(table, panel - core, j * blocks + b) == 1
        columns = slice(b * bs, (b + 1) * bs)
        mine = even == (core == 0)
        rows = jnp.where(mine, own[:, columns], sib[:, columns])
        product = jnp.dot(rows, pre[b], preferred_element_type=F32)
        value = (product * scale).T.astype(BF16)
        spread(right, value, even, b, bs)

        @pl.when(core == b // depth)
        def _():
            half[(b % depth) * bs : (b % depth + 1) * bs, :] = value


def spread(right, value, even, b, bs):
    zero = jnp.zeros_like(value)
    right[b * bs : (b + 1) * bs, :PROWS] = jnp.where(even, value, zero)
    right[b * bs : (b + 1) * bs, PROWS:] = jnp.where(even, zero, value)


def scores(pool, right, parts, j, send_a, keep_a, send_c, keep_c):
    rows = pool.shape[0] // parts
    low, high = j & 1, (j >> 1) & 1
    for da in (1, 0):
        for dc in (1, 0):
            for i in range(parts // 4):
                at = (i << 2) | ((high ^ dc) << 1) | (low ^ da)
                start = pl.multiple_of(at * rows, rows)
                value = jnp.dot(pool[pl.ds(start, rows), :], right[...], preferred_element_type=F32)
                out_a, out_c = (send_a if da else keep_a), (send_c if dc else keep_c)
                out_a[(i << 1) | (high ^ dc)] = value[:, :PROWS].astype(out_a.dtype)
                out_c[(i << 1) | (low ^ da)] = value[:, PROWS:].astype(out_c.dtype)


def scores_near_kernel(parts, pool, right, *outs):
    scores(pool, right, parts, lax.axis_index("tgt"), *outs)


def scores_far_kernel(parts, group, blocks, bs, active, pool, mine, other, *rest):
    outs, right = rest[:-1], rest[-1]
    j, panel = place(group)
    core = panel & 1
    depth = blocks // 2
    far = (panel ^ 2) - core
    table = active[...]
    for b in range(blocks):
        here = slice((b % depth) * bs, (b % depth + 1) * bs)
        value = jnp.where(core == b // depth, mine[here, :], other[here, :])
        spread(right, value, listed(table, far, j * blocks + b) == 1, b, bs)
    scores(pool, right, parts, j, *outs)


def halve_kernel(bit, count, *refs):
    keeps, gots, (send, keep) = refs[:count], refs[count : 2 * count], refs[2 * count :]
    value = (lax.axis_index("tgt") >> bit) & 1
    for i in range(send.shape[0]):
        for c in range(count):
            width = keeps[c].shape[2]
            columns = slice(c * width, (c + 1) * width)
            away, home = 2 * i + 1 - value, 2 * i + value
            send[i, :, columns] = (keeps[c][away] + gots[c][away].astype(F32)).astype(BF16)
            keep[i, :, columns] = keeps[c][home] + gots[c][home].astype(F32)


def halve(keeps, gots, bit):
    n, rows, width = keeps[0].shape
    shape = (n // 2, rows, width * len(keeps))
    return call(
        functools.partial(halve_kernel, bit, len(keeps)), [(shape, BF16), (shape, F32)], *keeps, *gots
    )


def last_kernel(group, near, near_got, far, far_got, out):
    _, panel = place(group)
    pair = panel >> 1
    width = near.shape[2]
    first, second = near[0] + near_got[0].astype(F32), far[0] + far_got[0].astype(F32)
    swapped = pair == 1
    out[:, :width] = jnp.where(swapped, second, first)
    out[:, width:] = jnp.where(swapped, first, second)


def local(tgt_size, pool_size, pool, target, pre, active):
    blocks, bs, _ = pre.shape
    scale = (active.shape[1] * bs) ** (-0.5)
    group = PROWS // target.shape[0]
    m, k = pool.shape
    part = m // tgt_size
    pool = pltpu.with_memory_space_constraint(pool, pltpu.VMEM)
    if group == 1:
        own = target
    else:
        groups = [list(range(g, g + group)) for g in range(0, pool_size, group)]
        own = lax.all_gather(target, "pool", axis=0, tiled=True, axis_index_groups=groups)

    def swap(x, axis, step):
        size = {"tgt": tgt_size, "pool": pool_size}[axis]
        return lax.ppermute(x, axis, [(i, i ^ step) for i in range(size)])

    sibling = swap(own, "pool", group)
    right, half = call(
        functools.partial(near_kernel, group, scale),
        [((k, 2 * PROWS), BF16), ((k // 2, PROWS), BF16)],
        active, own, sibling, pre, flops=2 * PROWS * k * bs,
    )
    mine = swap(half, "pool", 2 * group)
    other = swap(mine, "pool", group)
    shape = (tgt_size // 2, part, PROWS)
    outs = [(shape, BF16), (shape, F32)] * 2
    flops = 4 * m * k * PROWS

    def first_steps(send_a, keep_a, send_c, keep_c):
        got_a, got_c = swap(send_a, "tgt", 1), swap(send_c, "tgt", 2)
        send_a, keep_a = halve([keep_a], [got_a], 1)
        send_c, keep_c = halve([keep_c], [got_c], 0)
        got_a, got_c = swap(send_a, "tgt", 2), swap(send_c, "tgt", 1)
        bit = 2
        send, keep = halve([keep_a, keep_c], [got_a, got_c], bit)
        while send.shape[0] > 1:
            got = swap(send, "tgt", 1 << bit)
            bit += 1
            send, keep = halve([keep], [got], bit)
        return keep, swap(send, "tgt", 1 << bit)

    near = first_steps(*call(functools.partial(scores_near_kernel, tgt_size), outs, pool, right, flops=flops))
    far = first_steps(
        *call(
            functools.partial(scores_far_kernel, tgt_size, group, blocks, bs),
            outs, active, pool, mine, other, flops=flops, scratch=[pltpu.VMEM((k, 2 * PROWS), BF16)],
        )
    )
    out = ((part, 4 * PROWS), F32)
    return call(functools.partial(last_kernel, group), [out], *near, *far)[0]


def solution(mesh):
    return jax.shard_map(
        functools.partial(local, mesh.shape["tgt"], mesh.shape["pool"]),
        mesh=mesh,
        in_specs=(P("pool", "tgt"), P("pool", "tgt"), P("tgt", None, None), P()),
        out_specs=P(("pool", "tgt"), None),
        check_vma=False,
    )
```

time: 145 us -> 57.1 us (0.39)
  waiting for transfers between devices: 113 us -> 22.1 us
  starting transfers between devices: 0.04 us -> 19.8 us
  between operations: 13.4 us -> 0.07 us
  matrix products: 12.8 us -> 0 us
  Pallas kernels: 0 us -> 8.08 us
  local copies, waits for them, and re-layouts: 4.23 us -> 6.7 us
    reduce_scatter x1 -> x0, waiting for transfers between devices: 88.5 us -> none  [local(): lax.psum_scatter(lax.dot_general(pool_grads, conditioned, (((1,), (1,)),...]
    all_gather x1 -> x0, waiting for transfers between devices: 24.6 us -> none  [local(): whole = lax.all_gather(target_grads, 'pool', axis=0, tiled=True)]
    ppermute x0 -> x13, waiting for transfers between devices: none -> 22.1 us  [swap(): return lax.ppermute(x, axis, [(i, i ^ step) for i in range(size)])]
    ppermute x0 -> x13, starting transfers between devices: none -> 19.8 us  [swap(): return lax.ppermute(x, axis, [(i, i ^ step) for i in range(size)])]
    dot_general x3 -> x0, matrix products: 12.8 us -> none  [the longest x1 9.62 us: local(): lax.dot_general(pool_grads, conditioned, (((1,), (1,)), ((), ())), prefer...]
    pallas_call x0 -> x10, Pallas kernels: none -> 8.08 us  [call(): pl.pallas_call(body, in_specs=[VMEM] * len(args), out_specs=[VMEM] * len(...]
    unnamed x3 -> x10, local copies, waits for them, and re-layouts: 2.19 us -> 6.7 us
    reduce_scatter x1 -> x0, local copies, waits for them, and re-layouts: 2.04 us -> none  [local(): lax.psum_scatter(lax.dot_general(pool_grads, conditioned, (((1,), (1,)),...]
  transfers between devices with their start and end apart: 2 -> 13, of which waited for: 2 -> 7; matrix products, arithmetic and copies ran while one was open for 1% -> 0% of each run, Pallas kernels for 0% -> 9%
where the time goes in v1:
time: 57.1 us; the launch traced here: 56.8 us
  waiting for transfers between devices  22.1 us (39%)
  starting transfers between devices  19.8 us (35%)
  Pallas kernels  8.08 us (14%)
  local copies, waits for them, and re-layouts  6.7 us (12%)
    ppermute x13, waiting for transfers between devices, swap(): return lax.ppermute(x, axis, [(i, i ^ step) for i in range(size)])  22.1 us
    ppermute x13, starting transfers between devices, swap(): return lax.ppermute(x, axis, [(i, i ^ step) for i in range(size)])  19.8 us
    pallas_call x10, Pallas kernels, call(): pl.pallas_call(body, in_specs=[VMEM] * len(args), out_specs=[VMEM] * len(...  8.08 us
    unnamed x10, local copies, waits for them, and re-layouts  6.7 us
  transfers between devices with their start and end apart: 13, of which 7 were waited for; matrix products, arithmetic and copies ran while one was open for 0% of the time, Pallas kernels for 9%

profile of v1, /device:TPU:0, one launch (start us, length us, event | category | flops | bytes accessed | tf_op | source)
XLA Modules:
  0.0 56.8 jit_solution(15697942697798608496)
XLA Ops:
  0.5 1.7 %collective-permute-done.sib = bf16[128,2048]{1,0:T(8,128)(2,1)S(1)} collective-permute-done((bf16[128,2048]{1,0:T(8,128)(2,1)}, bf16[128,2048]{1,0:T(8,128)(2,1)S(1)}, u32[]{:S(2)}, u32[]{:S(2)}) %collective-permute-start) | collective-permute-done | bytes 524320 | tf_op jit(solution)/shard_map/ppermute | solution.py:139
  2.2 1.6 %copy-done.2 = bf16[4,512,512]{2,1,0:T(8,128)(2,1)S(1)} copy-done((bf16[4,512,512]{2,1,0:T(8,128)(2,1)S(1)}, bf16[4,512,512]{2,1,0:T(8,128)(2,1)}, u32[]{:S(2)}) %copy-start.2) | copy-done | bytes 2097176
  3.8 1.0 %copy-done.3 = bf16[128,2048]{1,0:T(8,128)(2,1)S(1)} copy-done((bf16[128,2048]{1,0:T(8,128)(2,1)S(1)}, bf16[128,2048]{1,0:T(8,128)(2,1)}, u32[]{:S(2)}) %copy-start.3) | copy-done | bytes 524312
  4.8 0.7 %copy-done.4 = s32[4,16]{1,0:T(4,128)S(1)} copy-done((s32[4,16]{1,0:T(4,128)S(1)}, s32[4,16]{1,0:T(4,128)}, u32[]{:S(2)}) %copy-start.4) | copy-done | bytes 280
  5.5 2.0 %shard_map.46 = (bf16[2048,256]{1,0:T(8,128)(2,1)S(1)}, bf16[1024,128]{1,0:T(8,128)(2,1)S(1)}) custom-call(s32[4,16]{1,0:T(4,128)S(1)} %copy-done.4, bf16[128,2048]{1,0:T(8,128)(2,1)S(1)} %copy-done.3, bf16[128,2048]{1,0:T(8,128)(2,1)S(1)} %collective-permute-done.sib, bf16[4,512,512]{2,1,0:T(8,128)(2,1)S(1)} %copy-done.2), custom_call_target="tpu_custom_call" | custom-call | flops 268435456 | tf_op jit(solution)/shard_map/pallas_call | solution.py:16
  7.5 3.0 %collective-permute-start.6 = (bf16[1024,128]{1,0:T(8,128)(2,1)S(1)}, bf16[1024,128]{1,0:T(8,128)(2,1)S(1)}, u32[]{:S(2)}, u32[]{:S(2)}) collective-permute-start(bf16[1024,128]{1,0:T(8,128)(2,1)S(1)} %get-tuple-element.38), channel_id=1, source_target_pairs={{0,16},{8,24},{16,0},{24,8},{1,17},{9,25},{17,1},{25,9},{2,18},{10... | collective-permute-start | bytes 786440 | tf_op jit(solution)/shard_map/ppermute | solution.py:139
  10.4 6.6 %collective-permute-done.6.mine = bf16[1024,128]{1,0:T(8,128)(2,1)S(1)} collective-permute-done((bf16[1024,128]{1,0:T(8,128)(2,1)S(1)}, bf16[1024,128]{1,0:T(8,128)(2,1)S(1)}, u32[]{:S(2)}, u32[]{:S(2)}) %collective-permute-start.6) | collective-permute-done | bytes 262176 | tf_op jit(solution)/shard_map/ppermute | solution.py:139
  17.1 3.4 %copy-done = bf16[2048,2048]{1,0:T(8,128)(2,1)S(1)} copy-done((bf16[2048,2048]{1,0:T(8,128)(2,1)S(1)}, bf16[2048,2048]{1,0:T(8,128)(2,1)}, u32[]{:S(2)}) %copy-start) | copy-done | bytes 8388632
  20.4 2.3 %shard_map.47 = (bf16[4,256,128]{2,1,0:T(8,128)(2,1)S(1)}, f32[4,256,128]{2,1,0:T(8,128)S(1)}, bf16[4,256,128]{2,1,0:T(8,128)(2,1)S(1)}, f32[4,256,128]{2,1,0:T(8,128)S(1)}) custom-call(bf16[2048,2048]{1,0:T(8,128)(2,1)S(1)} %copy-done, bf16[2048,256]{1,0:T(8,128)(2,1)S(1)} %get-tuple-element.27.right), custom_call_target="tpu_custom_call" | custom-call | flops 2147483648 | tf_op jit(solution)/shard_map/pallas_call | solution.py:16
  22.8 1.8 %collective-permute-start.1 = (bf16[4,256,128]{2,1,0:T(8,128)(2,1)S(1)}, bf16[4,256,128]{2,1,0:T(8,128)(2,1)S(1)}, u32[]{:S(2)}, u32[]{:S(2)}) collective-permute-start(bf16[4,256,128]{2,1,0:T(8,128)(2,1)S(1)} %get-tuple-element.29), channel_id=1, source_target_pairs={{0,1},{1,0},{2,3},{3,2},{4,5},{5,4},{6,7},{7,6},{8,9},{9,8},{10,11... | collective-permute-start | bytes 786440 | tf_op jit(solution)/shard_map/ppermute | solution.py:139
  24.6 1.6 %collective-permute-start.2 = (bf16[4,256,128]{2,1,0:T(8,128)(2,1)S(1)}, bf16[4,256,128]{2,1,0:T(8,128)(2,1)S(1)}, u32[]{:S(2)}, u32[]{:S(2)}) collective-permute-start(bf16[4,256,128]{2,1,0:T(8,128)(2,1)S(1)} %get-tuple-element.32), channel_id=1, source_target_pairs={{0,2},{1,3},{2,0},{3,1},{4,6},{5,7},{6,4},{7,5},{8,10},{9,11},{10,... | collective-permute-start | bytes 786440 | tf_op jit(solution)/shard_map/ppermute | solution.py:139
  26.1 2.6 %shard_map.51 = (bf16[4,256,128]{2,1,0:T(8,128)(2,1)S(1)}, f32[4,256,128]{2,1,0:T(8,128)S(1)}, bf16[4,256,128]{2,1,0:T(8,128)(2,1)S(1)}, f32[4,256,128]{2,1,0:T(8,128)S(1)}) custom-call(s32[4,16]{1,0:T(4,128)S(1)} %copy-done.4, bf16[2048,2048]{1,0:T(8,128)(2,1)S(1)} %copy-done.1, bf16[1024,128]{1,0:T(8,128)(2,1)S(1)} %collective-permute-done.6.mine, ...), custom_call_target="tpu_custom_call" | custom-call | flops 2147483648 | tf_op jit(solution)/shard_map/pallas_call | solution.py:16
  29.8 1.9 %collective-permute-done.1.refs_1_ = bf16[4,256,128]{2,1,0:T(8,128)(2,1)S(1)} collective-permute-done((bf16[4,256,128]{2,1,0:T(8,128)(2,1)S(1)}, bf16[4,256,128]{2,1,0:T(8,128)(2,1)S(1)}, u32[]{:S(2)}, u32[]{:S(2)}) %collective-permute-start.1) | collective-permute-done | bytes 262176 | tf_op jit(solution)/shard_map/ppermute | solution.py:139
  31.7 2.1 %collective-permute-start.3 = (bf16[2,256,128]{2,1,0:T(8,128)(2,1)S(1)}, bf16[2,256,128]{2,1,0:T(8,128)(2,1)S(1)}, u32[]{:S(2)}, u32[]{:S(2)}) collective-permute-start(bf16[2,256,128]{2,1,0:T(8,128)(2,1)S(1)} %get-tuple-element.34), channel_id=1, source_target_pairs={{0,2},{1,3},{2,0},{3,1},{4,6},{5,7},{6,4},{7,5},{8,10},{9,11},{10,... | collective-permute-start | bytes 393224 | tf_op jit(solution)/shard_map/ppermute | solution.py:139
  33.9 1.5 %collective-permute-start.4 = (bf16[2,256,128]{2,1,0:T(8,128)(2,1)S(1)}, bf16[2,256,128]{2,1,0:T(8,128)(2,1)S(1)}, u32[]{:S(2)}, u32[]{:S(2)}) collective-permute-start(bf16[2,256,128]{2,1,0:T(8,128)(2,1)S(1)} %get-tuple-element.35), channel_id=1, source_target_pairs={{0,1},{1,0},{2,3},{3,2},{4,5},{5,4},{6,7},{7,6},{8,9},{9,8},{10,11... | collective-permute-start | bytes 393224 | tf_op jit(solution)/shard_map/ppermute | solution.py:139
  35.5 2.5 %collective-permute-done.8.refs_1_ = bf16[4,256,128]{2,1,0:T(8,128)(2,1)S(1)} collective-permute-done((bf16[4,256,128]{2,1,0:T(8,128)(2,1)S(1)}, bf16[4,256,128]{2,1,0:T(8,128)(2,1)S(1)}, u32[]{:S(2)}, u32[]{:S(2)}) %collective-permute-start.8) | collective-permute-done | bytes 262176 | tf_op jit(solution)/shard_map/ppermute | solution.py:139
  38.1 1.4 %collective-permute-start.10 = (bf16[2,256,128]{2,1,0:T(8,128)(2,1)S(1)}, bf16[2,256,128]{2,1,0:T(8,128)(2,1)S(1)}, u32[]{:S(2)}, u32[]{:S(2)}) collective-permute-start(bf16[2,256,128]{2,1,0:T(8,128)(2,1)S(1)} %get-tuple-element.45), channel_id=1, source_target_pairs={{0,2},{1,3},{2,0},{3,1},{4,6},{5,7},{6,4},{7,5},{8,10},{9,11},{10,... | collective-permute-start | bytes 393224 | tf_op jit(solution)/shard_map/ppermute | solution.py:139
  39.6 1.5 %collective-permute-start.11 = (bf16[2,256,128]{2,1,0:T(8,128)(2,1)S(1)}, bf16[2,256,128]{2,1,0:T(8,128)(2,1)S(1)}, u32[]{:S(2)}, u32[]{:S(2)}) collective-permute-start(bf16[2,256,128]{2,1,0:T(8,128)(2,1)S(1)} %get-tuple-element.46), channel_id=1, source_target_pairs={{0,1},{1,0},{2,3},{3,2},{4,5},{5,4},{6,7},{7,6},{8,9},{9,8},{10,11... | collective-permute-start | bytes 393224 | tf_op jit(solution)/shard_map/ppermute | solution.py:139
  41.1 1.0 %collective-permute-done.3.refs_2_ = bf16[2,256,128]{2,1,0:T(8,128)(2,1)S(1)} collective-permute-done((bf16[2,256,128]{2,1,0:T(8,128)(2,1)S(1)}, bf16[2,256,128]{2,1,0:T(8,128)(2,1)S(1)}, u32[]{:S(2)}, u32[]{:S(2)}) %collective-permute-start.3) | collective-permute-done | bytes 131104 | tf_op jit(solution)/shard_map/ppermute | solution.py:139
  42.2 2.7 %collective-permute-start.5 = (bf16[1,256,256]{2,1,0:T(8,128)(2,1)S(1)}, bf16[1,256,256]{2,1,0:T(8,128)(2,1)S(1)}, u32[]{:S(2)}, u32[]{:S(2)}) collective-permute-start(bf16[1,256,256]{2,1,0:T(8,128)(2,1)S(1)} %get-tuple-element.37), channel_id=1, source_target_pairs={{0,4},{1,5},{2,6},{3,7},{4,0},{5,1},{6,2},{7,3},{8,12},{9,13},{10,... | collective-permute-start | bytes 393224 | tf_op jit(solution)/shard_map/ppermute | solution.py:139
  44.9 2.8 %collective-permute-start.12 = (bf16[1,256,256]{2,1,0:T(8,128)(2,1)S(1)}, bf16[1,256,256]{2,1,0:T(8,128)(2,1)S(1)}, u32[]{:S(2)}, u32[]{:S(2)}) collective-permute-start(bf16[1,256,256]{2,1,0:T(8,128)(2,1)S(1)} %get-tuple-element.48), channel_id=1, source_target_pairs={{0,4},{1,5},{2,6},{3,7},{4,0},{5,1},{6,2},{7,3},{8,12},{9,13},{10,... | collective-permute-start | bytes 393224 | tf_op jit(solution)/shard_map/ppermute | solution.py:139
  47.7 6.7 %collective-permute-done.5.near_got = bf16[1,256,256]{2,1,0:T(8,128)(2,1)S(1)} collective-permute-done((bf16[1,256,256]{2,1,0:T(8,128)(2,1)S(1)}, bf16[1,256,256]{2,1,0:T(8,128)(2,1)S(1)}, u32[]{:S(2)}, u32[]{:S(2)}) %collective-permute-start.5) | collective-permute-done | bytes 131104 | tf_op jit(solution)/shard_map/ppermute | solution.py:139
  54.3 1.6 %collective-permute-done.12.far_got = bf16[1,256,256]{2,1,0:T(8,128)(2,1)S(1)} collective-permute-done((bf16[1,256,256]{2,1,0:T(8,128)(2,1)S(1)}, bf16[1,256,256]{2,1,0:T(8,128)(2,1)S(1)}, u32[]{:S(2)}, u32[]{:S(2)}) %collective-permute-start.12) | collective-permute-done | bytes 131104 | tf_op jit(solution)/shard_map/ppermute | solution.py:139
  56.0 0.9 %shard_map.55 = f32[256,512]{1,0:T(8,128)} custom-call(f32[1,256,256]{2,1,0:T(8,128)S(1)} %get-tuple-element.36.near, bf16[1,256,256]{2,1,0:T(8,128)(2,1)S(1)} %collective-permute-done.5.near_got, f32[1,256,256]{2,1,0:T(8,128)S(1)} %get-tuple-element.47.far, bf16[1,256,256]{2,1,0:T(8,128)(2,1)S(1)} %collective-permute-done.12.far_got), custom_call_target="tpu_custom_call" | custom-call | tf_op jit(solution)/shard_map/pallas_call | solution.py:16
  (22 shorter events, 1.8 us)
Async XLA Ops:
  0.0 2.2 %collective-permute-start = (bf16[128,2048]{1,0:T(8,128)(2,1)}, bf16[128,2048]{1,0:T(8,128)(2,1)S(1)}, u32[]{:S(2)}, u32[]{:S(2)}) collective-permute-start(bf16[128,2048]{1,0:T(8,128)(2,1)} %own.1), channel_id=1, source_target_pairs={{0,8},{8,0},{16,24},{24,16},{1,9},{9,1},{17,25},{25,17},{2,10},{10... | collective-permute-start | bytes 1572872 | tf_op jit(solution)/shard_map/ppermute | solution.py:139
  2.2 1.6 %copy-start.2 = (bf16[4,512,512]{2,1,0:T(8,128)(2,1)S(1)}, bf16[4,512,512]{2,1,0:T(8,128)(2,1)}, u32[]{:S(2)}) copy-start(bf16[4,512,512]{2,1,0:T(8,128)(2,1)} %pre.1) | copy-start | bytes 6291460
  3.8 1.0 %copy-start.3 = (bf16[128,2048]{1,0:T(8,128)(2,1)S(1)}, bf16[128,2048]{1,0:T(8,128)(2,1)}, u32[]{:S(2)}) copy-start(bf16[128,2048]{1,0:T(8,128)(2,1)} %own.1) | copy-start | bytes 1572868
  4.8 0.7 %copy-start.4 = (s32[4,16]{1,0:T(4,128)S(1)}, s32[4,16]{1,0:T(4,128)}, u32[]{:S(2)}) copy-start(s32[4,16]{1,0:T(4,128)} %active.3) | copy-start | bytes 772
  7.5 9.6 %collective-permute-start.6 = (bf16[1024,128]{1,0:T(8,128)(2,1)S(1)}, bf16[1024,128]{1,0:T(8,128)(2,1)S(1)}, u32[]{:S(2)}, u32[]{:S(2)}) collective-permute-start(bf16[1024,128]{1,0:T(8,128)(2,1)S(1)} %get-tuple-element.38), channel_id=1, source_target_pairs={{0,16},{8,24},{16,0},{24,8},{1,17},{9,25},{17,1},{25,9},{2,18},{10... | collective-permute-start | bytes 786440 | tf_op jit(solution)/shard_map/ppermute | solution.py:139
  17.0 9.1 %collective-permute-start.7 = (bf16[1024,128]{1,0:T(8,128)(2,1)S(1)}, bf16[1024,128]{1,0:T(8,128)(2,1)S(1)}, u32[]{:S(2)}, u32[]{:S(2)}) collective-permute-start(bf16[1024,128]{1,0:T(8,128)(2,1)S(1)} %collective-permute-done.6.mine), channel_id=1, source_target_pairs={{0,8},{8,0},{16,24},{24,16},{1,9},{9,1},{17,25},{25,17},{2,10},{10... | collective-permute-start | bytes 786440 | tf_op jit(solution)/shard_map/ppermute | solution.py:139
  17.0 3.4 %copy-start = (bf16[2048,2048]{1,0:T(8,128)(2,1)S(1)}, bf16[2048,2048]{1,0:T(8,128)(2,1)}, u32[]{:S(2)}) copy-start(bf16[2048,2048]{1,0:T(8,128)(2,1)} %pool.3) | copy-start | bytes 25165828
  20.4 5.7 %copy-start.1 = (bf16[2048,2048]{1,0:T(8,128)(2,1)S(1)}, bf16[2048,2048]{1,0:T(8,128)(2,1)}, u32[]{:S(2)}) copy-start(bf16[2048,2048]{1,0:T(8,128)(2,1)} %pool.3) | copy-start | bytes 25165828
  22.8 8.9 %collective-permute-start.1 = (bf16[4,256,128]{2,1,0:T(8,128)(2,1)S(1)}, bf16[4,256,128]{2,1,0:T(8,128)(2,1)S(1)}, u32[]{:S(2)}, u32[]{:S(2)}) collective-permute-start(bf16[4,256,128]{2,1,0:T(8,128)(2,1)S(1)} %get-tuple-element.29), channel_id=1, source_target_pairs={{0,1},{1,0},{2,3},{3,2},{4,5},{5,4},{6,7},{7,6},{8,9},{9,8},{10,11... | collective-permute-start | bytes 786440 | tf_op jit(solution)/shard_map/ppermute | solution.py:139
  24.6 9.3 %collective-permute-start.2 = (bf16[4,256,128]{2,1,0:T(8,128)(2,1)S(1)}, bf16[4,256,128]{2,1,0:T(8,128)(2,1)S(1)}, u32[]{:S(2)}, u32[]{:S(2)}) collective-permute-start(bf16[4,256,128]{2,1,0:T(8,128)(2,1)S(1)} %get-tuple-element.32), channel_id=1, source_target_pairs={{0,2},{1,3},{2,0},{3,1},{4,6},{5,7},{6,4},{7,5},{8,10},{9,11},{10,... | collective-permute-start | bytes 786440 | tf_op jit(solution)/shard_map/ppermute | solution.py:139
  28.8 9.2 %collective-permute-start.8 = (bf16[4,256,128]{2,1,0:T(8,128)(2,1)S(1)}, bf16[4,256,128]{2,1,0:T(8,128)(2,1)S(1)}, u32[]{:S(2)}, u32[]{:S(2)}) collective-permute-start(bf16[4,256,128]{2,1,0:T(8,128)(2,1)S(1)} %get-tuple-element.40), channel_id=1, source_target_pairs={{0,1},{1,0},{2,3},{3,2},{4,5},{5,4},{6,7},{7,6},{8,9},{9,8},{10,11... | collective-permute-start | bytes 786440 | tf_op jit(solution)/shard_map/ppermute | solution.py:139
  29.4 10.1 %collective-permute-start.9 = (bf16[4,256,128]{2,1,0:T(8,128)(2,1)S(1)}, bf16[4,256,128]{2,1,0:T(8,128)(2,1)S(1)}, u32[]{:S(2)}, u32[]{:S(2)}) collective-permute-start(bf16[4,256,128]{2,1,0:T(8,128)(2,1)S(1)} %get-tuple-element.43), channel_id=1, source_target_pairs={{0,2},{1,3},{2,0},{3,1},{4,6},{5,7},{6,4},{7,5},{8,10},{9,11},{10,... | collective-permute-start | bytes 786440 | tf_op jit(solution)/shard_map/ppermute | solution.py:139
  31.7 10.4 %collective-permute-start.3 = (bf16[2,256,128]{2,1,0:T(8,128)(2,1)S(1)}, bf16[2,256,128]{2,1,0:T(8,128)(2,1)S(1)}, u32[]{:S(2)}, u32[]{:S(2)}) collective-permute-start(bf16[2,256,128]{2,1,0:T(8,128)(2,1)S(1)} %get-tuple-element.34), channel_id=1, source_target_pairs={{0,2},{1,3},{2,0},{3,1},{4,6},{5,7},{6,4},{7,5},{8,10},{9,11},{10,... | collective-permute-start | bytes 393224 | tf_op jit(solution)/shard_map/ppermute | solution.py:139
  33.9 8.2 %collective-permute-start.4 = (bf16[2,256,128]{2,1,0:T(8,128)(2,1)S(1)}, bf16[2,256,128]{2,1,0:T(8,128)(2,1)S(1)}, u32[]{:S(2)}, u32[]{:S(2)}) collective-permute-start(bf16[2,256,128]{2,1,0:T(8,128)(2,1)S(1)} %get-tuple-element.35), channel_id=1, source_target_pairs={{0,1},{1,0},{2,3},{3,2},{4,5},{5,4},{6,7},{7,6},{8,9},{9,8},{10,11... | collective-permute-start | bytes 393224 | tf_op jit(solution)/shard_map/ppermute | solution.py:139
  38.1 6.8 %collective-permute-start.10 = (bf16[2,256,128]{2,1,0:T(8,128)(2,1)S(1)}, bf16[2,256,128]{2,1,0:T(8,128)(2,1)S(1)}, u32[]{:S(2)}, u32[]{:S(2)}) collective-permute-start(bf16[2,256,128]{2,1,0:T(8,128)(2,1)S(1)} %get-tuple-element.45), channel_id=1, source_target_pairs={{0,2},{1,3},{2,0},{3,1},{4,6},{5,7},{6,4},{7,5},{8,10},{9,11},{10,... | collective-permute-start | bytes 393224 | tf_op jit(solution)/shard_map/ppermute | solution.py:139
  39.6 5.3 %collective-permute-start.11 = (bf16[2,256,128]{2,1,0:T(8,128)(2,1)S(1)}, bf16[2,256,128]{2,1,0:T(8,128)(2,1)S(1)}, u32[]{:S(2)}, u32[]{:S(2)}) collective-permute-start(bf16[2,256,128]{2,1,0:T(8,128)(2,1)S(1)} %get-tuple-element.46), channel_id=1, source_target_pairs={{0,1},{1,0},{2,3},{3,2},{4,5},{5,4},{6,7},{7,6},{8,9},{9,8},{10,11... | collective-permute-start | bytes 393224 | tf_op jit(solution)/shard_map/ppermute | solution.py:139
  42.2 12.1 %collective-permute-start.5 = (bf16[1,256,256]{2,1,0:T(8,128)(2,1)S(1)}, bf16[1,256,256]{2,1,0:T(8,128)(2,1)S(1)}, u32[]{:S(2)}, u32[]{:S(2)}) collective-permute-start(bf16[1,256,256]{2,1,0:T(8,128)(2,1)S(1)} %get-tuple-element.37), channel_id=1, source_target_pairs={{0,4},{1,5},{2,6},{3,7},{4,0},{5,1},{6,2},{7,3},{8,12},{9,13},{10,... | collective-permute-start | bytes 393224 | tf_op jit(solution)/shard_map/ppermute | solution.py:139
  44.9 11.1 %collective-permute-start.12 = (bf16[1,256,256]{2,1,0:T(8,128)(2,1)S(1)}, bf16[1,256,256]{2,1,0:T(8,128)(2,1)S(1)}, u32[]{:S(2)}, u32[]{:S(2)}) collective-permute-start(bf16[1,256,256]{2,1,0:T(8,128)(2,1)S(1)} %get-tuple-element.48), channel_id=1, source_target_pairs={{0,4},{1,5},{2,6},{3,7},{4,0},{5,1},{6,2},{7,3},{8,12},{9,13},{10,... | collective-permute-start | bytes 393224 | tf_op jit(solution)/shard_map/ppermute | solution.py:139

commit v2 on v0

v2 whole, which is shorter than its diff:
```python
import functools

import jax
import jax.numpy as jnp
from jax import lax
from jax.experimental import pallas as pl
from jax.experimental.pallas import tpu as pltpu
from jax.sharding import PartitionSpec as P

PROWS = 128
F32, BF16 = jnp.float32, jnp.bfloat16
VMEM = pl.BlockSpec(memory_space=pltpu.VMEM)


def call(body, outs, *args, flops=0, mib=24, copies=0, far=(), kind=pltpu.VMEM):
    args = [pltpu.with_memory_space_constraint(x, pltpu.HBM) if n in far else x for n, x in enumerate(args)]
    specs = [pl.BlockSpec(memory_space=pltpu.HBM if n in far else pltpu.VMEM) for n in range(len(args))]
    return pl.pallas_call(
        body,
        in_specs=specs,
        out_specs=[VMEM] * len(outs),
        out_shape=[kind(shape, dtype) for shape, dtype in outs],
        scratch_shapes=[pltpu.SemaphoreType.DMA((copies,))] if copies else [],
        compiler_params=pltpu.CompilerParams(vmem_limit_bytes=mib * 2**20),
        cost_estimate=pl.CostEstimate(flops=flops, bytes_accessed=0, transcendentals=0),
    )(*args)


def copy_kernel(x, *rest):
    rest[-1][...] = x[...]


def after(x, *others, flops=0):
    return call(copy_kernel, [(x.shape, x.dtype)], x, *others, flops=flops)[0]


def place(group):
    return lax.axis_index("tgt"), lax.axis_index("pool") // group


def load(pairs, sems):
    copies = [pltpu.make_async_copy(src, dst, sems.at[n]) for n, (src, dst) in enumerate(pairs)]
    for copy in copies:
        copy.start()
    return copies


def order_of(parts, core):
    bits = list(range(parts.bit_length() - 1))
    return ([0, 1, 2] if core == 0 else [1, 0, 2]) + bits[3:]


def pick(core, values):
    return jnp.where(core == 1, values[1], values[0])


def row_block(parts, group, n):
    j, panel = place(group)
    away, away2, i = n < parts // 2, n % (parts // 2) < parts // 4, n % (parts // 4)
    at = []
    for core in range(2):
        first, second, *left = order_of(parts, core)
        value = (((j >> first) & 1) ^ away) << first | (((j >> second) & 1) ^ away2) << second
        for t, bit in enumerate(sorted(left)):
            value = value | ((i >> t) & 1) << bit
        at.append(value)
    return pick(panel & 1, at)


def rows_of(pool, parts, group, first, held):
    rows = pool.shape[0] // parts
    pairs = []
    for n in range(held.shape[0]):
        start = pl.multiple_of(row_block(parts, group, first + n) * rows, rows)
        pairs.append((pool.at[pl.ds(start, rows), :], held.at[n]))
    return pairs


def load_kernel(parts, group, blocks, pool, active, target, pre, table, target_v, pre_v, even, one, sems):
    copies = load([(active, table), (target, target_v), (pre, pre_v), *rows_of(pool, parts, group, 0, one)], sems)
    j, panel = place(group)
    base = panel - (panel & 1)
    copies[0].wait()
    shape = (even.shape[0], table.shape[1])
    n = lax.broadcasted_iota(jnp.int32, shape, 0)
    near, far = table[pl.ds(base, 1), :], table[pl.ds(base ^ 2, 1), :]
    listed = jnp.where(n < blocks, jnp.broadcast_to(near, shape), jnp.broadcast_to(far, shape))
    hits = (listed == j * blocks + n % blocks).astype(jnp.int32)
    even[...] = jnp.broadcast_to(jnp.max(hits, axis=1, keepdims=True), even.shape)
    for copy in copies[1:]:
        copy.wait()


def select_kernel(group, blocks, bs, evens, own, sib, rows, half):
    core = place(group)[1] & 1
    depth = blocks // 2
    for b in range(blocks):
        columns = slice(b * bs, (b + 1) * bs)
        value = jnp.where(evens[b : b + 1, :] != core, own[:, columns], sib[:, columns])
        rows[:, columns] = value

        @pl.when(core == b // depth)
        def _():
            half[:, (b % depth) * bs : (b % depth + 1) * bs] = value


def condition(scale, pre, even, rows_at, right):
    blocks, bs, _ = pre.shape
    for b in range(blocks):
        product = jnp.dot(rows_at(b), pre[b], preferred_element_type=F32)
        value = (product * scale).T.astype(BF16)
        listed, zero = even[b : b + 1, :PROWS] == 1, jnp.zeros_like(value)
        right[b * bs : (b + 1) * bs, :PROWS] = jnp.where(listed, value, zero)
        right[b * bs : (b + 1) * bs, PROWS:] = jnp.where(listed, zero, value)


def near_send_kernel(parts, group, scale, pool, evens, rows, pre, one, right, two, send, sems):
    copies = load(rows_of(pool, parts, group, parts // 4, two), sems)
    bs = pre.shape[1]
    condition(scale, pre, evens[: pre.shape[0], :], lambda b: rows[:, b * bs : (b + 1) * bs], right)
    scores([one], right, send)
    for copy in copies:
        copy.wait()


def far_send_kernel(group, scale, evens, mine, other, pre, one, *rest):
    right, send = rest[-2:]
    core = place(group)[1] & 1
    blocks, bs, _ = pre.shape
    depth = blocks // 2

    def rows_at(b):
        columns = slice((b % depth) * bs, (b % depth + 1) * bs)
        return jnp.where(core == b // depth, mine[:, columns], other[:, columns])

    condition(scale, pre, evens[blocks : 2 * blocks, :], rows_at, right)
    scores([one], right, send)


def scores(helds, right, *outs):
    for held, out in zip(helds, outs):
        for n in range(held.shape[0]):
            out[n] = jnp.dot(held[n], right[...], preferred_element_type=F32).astype(out.dtype)


def scores_kernel(held, right, *rest):
    scores([held], right, rest[-1])


def keep_kernel(three, four, right, *rest):
    scores([three, four], right, *rest[-2:])


def near_keep_kernel(parts, group, pool, right, _, keep, keep2, three, four, sems):
    copies = load(
        rows_of(pool, parts, group, parts // 2, three)
        + rows_of(pool, parts, group, parts // 2 + parts // 4, four), sems
    )
    for copy in copies:
        copy.wait()
    scores([three, four], right, keep, keep2)


def add_kernel(keep, got, *rest):
    rest[-1][...] = (keep[...] + got[...].astype(F32)).astype(BF16)


def halve_kernel(parts, group, step, gots, keep, *rest):
    send, home = rest[-2:]
    j, panel = place(group)
    bits = [sorted(order_of(parts, core)[2:])[step - 2] for core in range(2)]
    value = (j >> pick(panel & 1, bits)) & 1
    for i in range(send.shape[0]):
        for out, at in ((send, 2 * i + 1 - value), (home, 2 * i + value)):
            total = keep[at]
            for got in rest[:gots]:
                total = total + got[at].astype(F32)
            out[i] = total.astype(out.dtype)


def total_kernel(keep, got, *rest):
    rest[-1][...] = keep[0] + got[0].astype(F32)


def last_kernel(group, near, keep, got, out):
    pair = place(group)[1] >> 1
    width = near.shape[1]
    far = keep[0] + got[0].astype(F32)
    out[:, :width] = jnp.where(pair == 1, far, near[...])
    out[:, width:] = jnp.where(pair == 1, near[...], far)


def local(tgt_size, pool_size, pool, target, pre, active):
    blocks, bs, _ = pre.shape
    scale = (active.shape[1] * bs) ** (-0.5)
    group = PROWS // target.shape[0]
    m, k = pool.shape
    parts, part = tgt_size, m // tgt_size
    if group == 1:
        own = target
    else:
        groups = [list(range(g, g + group)) for g in range(0, pool_size, group)]
        own = lax.all_gather(target, "pool", axis=0, tiled=True, axis_index_groups=groups)

    def swap(x, axis, step):
        size = {"tgt": tgt_size, "pool": pool_size}[axis]
        return lax.ppermute(x, axis, [(i, i ^ step) for i in range(size)])

    sibling = swap(own, "pool", group)
    quarter = ((parts // 4, part, k), BF16)
    _, own_v, pre_v, evens, one = call(
        functools.partial(load_kernel, parts, group, blocks),
        [(active.shape, active.dtype), (own.shape, BF16), (pre.shape, BF16), ((2 * blocks, bs), active.dtype), quarter],
        pool, active, own, pre, copies=3 + parts // 4, far=(0, 1, 2, 3),
    )
    rows, half = call(
        functools.partial(select_kernel, group, blocks, bs), [((PROWS, k), BF16), ((PROWS, k // 2), BF16)],
        evens, own_v, sibling,
    )
    mine = swap(half, "pool", 2 * group)
    shape = (parts // 4, part, 2 * PROWS)
    right_out = ((k, 2 * PROWS), BF16)
    flops = 30 * m * k * PROWS

    def exchange(x, step):
        pairs = []
        for p in range(pool_size):
            bit = order_of(parts, (p // group) & 1)
            bit = bit[step] if step < 2 else sorted(bit[2:])[step - 2]
            pairs += [(p * parts + j, p * parts + (j ^ (1 << bit))) for j in range(parts)]
        return lax.ppermute(x, ("pool", "tgt"), pairs)

    def add(keep, got, *others):
        return call(add_kernel, [(shape, BF16)], keep, got, *others)[0]

    def rest(keep, gots, *others):
        step = 2
        while True:
            half_shape = (keep.shape[0] // 2,) + keep.shape[1:]
            send, keep = call(
                functools.partial(halve_kernel, parts, group, step, len(gots)),
                [(half_shape, BF16), (half_shape, F32)], keep, *gots, *others,
            )
            others, gots = (), [exchange(send, step)]
            step += 1
            if keep.shape[0] == 1:
                return keep, gots[0]

    right, two, send = call(
        functools.partial(near_send_kernel, parts, group, scale), [right_out, quarter, (shape, BF16)],
        pool, evens, rows, pre_v, one, flops=0, copies=parts // 4, far=(0,),
    )
    got = exchange(send, 0)
    send2 = call(scores_kernel, [(shape, BF16)], two, right, send)[0]
    got2 = exchange(send2, 0)
    keep, keep2, three, four = call(
        functools.partial(near_keep_kernel, parts, group), [(shape, F32)] * 2 + [quarter] * 2,
        pool, right, send2, flops=0, copies=parts // 2, far=(0,),
    )
    mine = after(mine, keep, flops=10**11)
    other = swap(mine, "pool", group)
    right, far_send = call(
        functools.partial(far_send_kernel, group, scale), [right_out, (shape, BF16)],
        evens, mine, other, pre_v, one, flops=0,
    )
    far_got = exchange(far_send, 0)
    far_send2 = call(scores_kernel, [(shape, BF16)], two, right, far_send)[0]
    far_got2 = exchange(far_send2, 0)
    got3 = exchange(add(keep, got), 1)
    far_keep, far_keep2 = call(keep_kernel, [(shape, F32)] * 2, three, four, right, flops=0)
    near = rest(keep2, [got2, got3], far_keep)
    near_total = call(total_kernel, [((part, 2 * PROWS), F32)], *near, far_got2, flops=10**11)[0]
    far_got3 = exchange(add(far_keep, far_got, near[0]), 1)
    far = rest(far_keep2, [far_got2, far_got3], near_total)
    out = ((part, 4 * PROWS), F32)
    return call(functools.partial(last_kernel, group), [out], near_total, *far, kind=jax.ShapeDtypeStruct)[0]


def solution(mesh):
    return jax.shard_map(
        functools.partial(local, mesh.shape["tgt"], mesh.shape["pool"]),
        mesh=mesh,
        in_specs=(P("pool", "tgt"), P("pool", "tgt"), P("tgt", None, None), P()),
        out_specs=P(("pool", "tgt"), None),
        check_vma=False,
    )
```

time: 145 us -> 43.3 us (0.30)
  waiting for transfers between devices: 113 us -> 14.8 us
  starting transfers between devices: 0.04 us -> 14.6 us
  Pallas kernels: 0 us -> 13.7 us
  between operations: 13.4 us -> 0.12 us
  matrix products: 12.8 us -> 0 us
  local copies, waits for them, and re-layouts: 4.23 us -> 0 us
    reduce_scatter x1 -> x0, waiting for transfers between devices: 88.5 us -> none  [local(): lax.psum_scatter(lax.dot_general(pool_grads, conditioned, (((1,), (1,)),...]
    all_gather x1 -> x0, waiting for transfers between devices: 24.6 us -> none  [local(): whole = lax.all_gather(target_grads, 'pool', axis=0, tiled=True)]
    ppermute x0 -> x11, waiting for transfers between devices: none -> 14.8 us  [the longest x8 14.8 us: exchange(): return lax.ppermute(x, ('pool', 'tgt'), pairs)]
    ppermute x0 -> x11, starting transfers between devices: none -> 14.6 us  [the longest x8 11.4 us: exchange(): return lax.ppermute(x, ('pool', 'tgt'), pairs)]
    pallas_call x0 -> x15, Pallas kernels: none -> 13.7 us  [call(): pl.pallas_call(body, in_specs=specs, out_specs=[VMEM] * len(outs), out_sh...]
    dot_general x3 -> x0, matrix products: 12.8 us -> none  [the longest x1 9.62 us: local(): lax.dot_general(pool_grads, conditioned, (((1,), (1,)), ((), ())), prefer...]
    unnamed x3 -> x0, local copies, waits for them, and re-layouts: 2.19 us -> none
    reduce_scatter x1 -> x0, local copies, waits for them, and re-layouts: 2.04 us -> none  [local(): lax.psum_scatter(lax.dot_general(pool_grads, conditioned, (((1,), (1,)),...]
  transfers between devices with their start and end apart: 2 -> 11, of which waited for: 2 -> 5; matrix products, arithmetic and copies ran while one was open for 1% -> 0% of each run, Pallas kernels for 0% -> 29%
where the time goes in v2:
time: 43.3 us; the launch traced here: 43.2 us
  waiting for transfers between devices  14.8 us (34%)
  starting transfers between devices  14.6 us (34%)
  Pallas kernels  13.7 us (32%)
    ppermute x8, waiting for transfers between devices, exchange(): return lax.ppermute(x, ('pool', 'tgt'), pairs)  14.8 us
    pallas_call x15, Pallas kernels, call(): pl.pallas_call(body, in_specs=specs, out_specs=[VMEM] * len(outs), out_sh...  13.7 us
    ppermute x8, starting transfers between devices, exchange(): return lax.ppermute(x, ('pool', 'tgt'), pairs)  11.4 us
    ppermute x3, starting transfers between devices, swap(): return lax.ppermute(x, axis, [(i, i ^ step) for i in range(size)])  3.13 us
  transfers between devices with their start and end apart: 11, of which 5 were waited for; matrix products, arithmetic and copies ran while one was open for 0% of the time, Pallas kernels for 29%

profile of v2, /device:TPU:0, one launch (start us, length us, event | category | flops | bytes accessed | tf_op | source)
XLA Modules:
  0.0 43.2 jit_solution(3430912144140745197)
XLA Ops:
  0.0 0.5 %collective-permute-start = (bf16[128,2048]{1,0:T(8,128)(2,1)}, bf16[128,2048]{1,0:T(8,128)(2,1)S(1)}, u32[]{:S(2)}, u32[]{:S(2)}) collective-permute-start(bf16[128,2048]{1,0:T(8,128)(2,1)} %target.1), channel_id=1, source_target_pairs={{0,8},{8,0},{16,24},{24,16},{1,9},{9,1},{17,25},{25,17},{2,10},{10... | collective-permute-start | bytes 1572872 | tf_op jit(solution)/shard_map/ppermute | solution.py:207
  0.5 3.0 %shard_map.46 = (s32[4,16]{1,0:T(4,128)}, bf16[128,2048]{1,0:T(8,128)(2,1)S(1)}, bf16[4,512,512]{2,1,0:T(8,128)(2,1)S(1)}, s32[8,512]{1,0:T(8,128)S(1)}, bf16[2,256,2048]{2,1,0:T(8,128)(2,1)S(1)}) custom-call(bf16[2048,2048]{1,0:T(8,128)(2,1)} %pool.5, s32[4,16]{1,0:T(4,128)} %active.1, bf16[128,2048]{1,0:T(8,128)(2,1)} %target.1, bf16[4,512,512]{2,1,0:T(8,128)(2,1)} %pre.1), custom_call_target="tpu_custom_call" | custom-call | tf_op jit(solution)/shard_map/pallas_call | solution.py:18
  3.4 0.1 shard_map.47
  3.5 2.6 %collective-permute-start.4 = (bf16[128,1024]{1,0:T(8,128)(2,1)S(1)}, bf16[128,1024]{1,0:T(8,128)(2,1)S(1)}, u32[]{:S(2)}, u32[]{:S(2)}) collective-permute-start(bf16[128,1024]{1,0:T(8,128)(2,1)S(1)} %get-tuple-element.38), channel_id=1, source_target_pairs={{0,16},{8,24},{16,0},{24,8},{1,17},{9,25},{17,1},{25,9},{2,18},{10... | collective-permute-start | bytes 786440 | tf_op jit(solution)/shard_map/ppermute | solution.py:207
  6.1 2.4 %shard_map.48 = (bf16[2048,256]{1,0:T(8,128)(2,1)S(1)}, bf16[2,256,2048]{2,1,0:T(8,128)(2,1)S(1)}, bf16[2,256,256]{2,1,0:T(8,128)(2,1)S(1)}) custom-call(bf16[2048,2048]{1,0:T(8,128)(2,1)} %pool.5, s32[8,512]{1,0:T(8,128)S(1)} %get-tuple-element.26.evens, bf16[128,2048]{1,0:T(8,128)(2,1)S(1)} %get-tuple-element.28.rows, ...), custom_call_target="tpu_custom_call" | custom-call | tf_op jit(solution)/shard_map/pallas_call | solution.py:18
  8.5 1.6 %collective-permute-start.2 = (bf16[2,256,256]{2,1,0:T(8,128)(2,1)S(1)}, bf16[2,256,256]{2,1,0:T(8,128)(2,1)S(1)}, u32[]{:S(2)}, u32[]{:S(2)}) collective-permute-start(bf16[2,256,256]{2,1,0:T(8,128)(2,1)S(1)} %get-tuple-element.33.rest_0_), channel_id=1, source_target_pairs={{0,1},{1,0},{2,3},{3,2},{4,5},{5,4},{6,7},{7,6},{8,10},{9,11},{10,... | collective-permute-start | bytes 786440 | tf_op jit(solution)/shard_map/ppermute | solution.py:231
  10.1 0.7 %shard_map.49._ = bf16[2,256,256]{2,1,0:T(8,128)(2,1)S(1)} custom-call(bf16[2,256,2048]{2,1,0:T(8,128)(2,1)S(1)} %get-tuple-element.32.held, bf16[2048,256]{1,0:T(8,128)(2,1)S(1)} %get-tuple-element.31.right, bf16[2,256,256]{2,1,0:T(8,128)(2,1)S(1)} %get-tuple-element.33.rest_0_), custom_call_target="tpu_custom_call" | custom-call | tf_op jit(solution)/shard_map/pallas_call | solution.py:18
  10.8 3.5 %shard_map.50 = (f32[2,256,256]{2,1,0:T(8,128)S(1)}, f32[2,256,256]{2,1,0:T(8,128)S(1)}, bf16[2,256,2048]{2,1,0:T(8,128)(2,1)S(1)}, bf16[2,256,2048]{2,1,0:T(8,128)(2,1)S(1)}) custom-call(bf16[2048,2048]{1,0:T(8,128)(2,1)} %pool.5, bf16[2048,256]{1,0:T(8,128)(2,1)S(1)} %get-tuple-element.31.right, bf16[2,256,256]{2,1,0:T(8,128)(2,1)S(1)} %shard_map.49._), custom_call_target="tpu_custom_call" | custom-call | tf_op jit(solution)/shard_map/pallas_call | solution.py:18
  14.4 1.5 %collective-permute-start.1 = (bf16[2,256,256]{2,1,0:T(8,128)(2,1)S(1)}, bf16[2,256,256]{2,1,0:T(8,128)(2,1)S(1)}, u32[]{:S(2)}, u32[]{:S(2)}) collective-permute-start(bf16[2,256,256]{2,1,0:T(8,128)(2,1)S(1)} %shard_map.49._), channel_id=1, source_target_pairs={{0,1},{1,0},{2,3},{3,2},{4,5},{5,4},{6,7},{7,6},{8,10},{9,11},{10,... | collective-permute-start | bytes 786440 | tf_op jit(solution)/shard_map/ppermute | solution.py:231
  15.9 0.7 %collective-permute-start.3 = (bf16[2,256,256]{2,1,0:T(8,128)(2,1)S(1)}, bf16[2,256,256]{2,1,0:T(8,128)(2,1)S(1)}, u32[]{:S(2)}, u32[]{:S(2)}) collective-permute-start(bf16[2,256,256]{2,1,0:T(8,128)(2,1)S(1)} %shard_map.51), channel_id=1, source_target_pairs={{0,2},{1,3},{2,0},{3,1},{4,6},{5,7},{6,4},{7,5},{8,9},{9,8},{10,11... | collective-permute-start | bytes 786440 | tf_op jit(solution)/shard_map/ppermute | solution.py:231
  16.7 1.0 %shard_map.53 = (bf16[2048,256]{1,0:T(8,128)(2,1)S(1)}, bf16[2,256,256]{2,1,0:T(8,128)(2,1)S(1)}) custom-call(s32[8,512]{1,0:T(8,128)S(1)} %get-tuple-element.26.evens, bf16[128,1024]{1,0:T(8,128)(2,1)S(1)} %shard_map.52.mine, bf16[128,1024]{1,0:T(8,128)(2,1)S(1)} %collective-permute-done.5.other, bf16[4,512,512]{2,1,0:T(8,128)(2,1)S(1)} %get-tuple-element.29.pre, ...), custom_call_target="tpu_custom_call" | custom-call | tf_op jit(solution)/shard_map/pallas_call | solution.py:18
  17.7 1.6 %collective-permute-start.8 = (bf16[2,256,256]{2,1,0:T(8,128)(2,1)S(1)}, bf16[2,256,256]{2,1,0:T(8,128)(2,1)S(1)}, u32[]{:S(2)}, u32[]{:S(2)}) collective-permute-start(bf16[2,256,256]{2,1,0:T(8,128)(2,1)S(1)} %get-tuple-element.43.rest_0_), channel_id=1, source_target_pairs={{0,1},{1,0},{2,3},{3,2},{4,5},{5,4},{6,7},{7,6},{8,10},{9,11},{10,... | collective-permute-start | bytes 786440 | tf_op jit(solution)/shard_map/ppermute | solution.py:231
  19.2 0.7 %shard_map.56 = bf16[2,256,256]{2,1,0:T(8,128)(2,1)S(1)} custom-call(bf16[2,256,2048]{2,1,0:T(8,128)(2,1)S(1)} %get-tuple-element.32.held, bf16[2048,256]{1,0:T(8,128)(2,1)S(1)} %get-tuple-element.39.right, bf16[2,256,256]{2,1,0:T(8,128)(2,1)S(1)} %get-tuple-element.43.rest_0_), custom_call_target="tpu_custom_call" | custom-call | tf_op jit(solution)/shard_map/pallas_call | solution.py:18
  20.0 0.6 %collective-permute-start.7 = (bf16[2,256,256]{2,1,0:T(8,128)(2,1)S(1)}, bf16[2,256,256]{2,1,0:T(8,128)(2,1)S(1)}, u32[]{:S(2)}, u32[]{:S(2)}) collective-permute-start(bf16[2,256,256]{2,1,0:T(8,128)(2,1)S(1)} %shard_map.56), channel_id=1, source_target_pairs={{0,1},{1,0},{2,3},{3,2},{4,5},{5,4},{6,7},{7,6},{8,10},{9,11},{10,... | collective-permute-start | bytes 786440 | tf_op jit(solution)/shard_map/ppermute | solution.py:231
  20.5 1.2 %shard_map.54 = (f32[2,256,256]{2,1,0:T(8,128)S(1)}, f32[2,256,256]{2,1,0:T(8,128)S(1)}) custom-call(bf16[2,256,2048]{2,1,0:T(8,128)(2,1)S(1)} %get-tuple-element.36.three, bf16[2,256,2048]{2,1,0:T(8,128)(2,1)S(1)} %get-tuple-element.37.four, bf16[2048,256]{1,0:T(8,128)(2,1)S(1)} %get-tuple-element.39.right), custom_call_target="tpu_custom_call" | custom-call | tf_op jit(solution)/shard_map/pallas_call | solution.py:18
  21.8 1.0 %collective-permute-done.1.rest_0_ = bf16[2,256,256]{2,1,0:T(8,128)(2,1)S(1)} collective-permute-done((bf16[2,256,256]{2,1,0:T(8,128)(2,1)S(1)}, bf16[2,256,256]{2,1,0:T(8,128)(2,1)S(1)}, u32[]{:S(2)}, u32[]{:S(2)}) %collective-permute-start.1) | collective-permute-done | bytes 262176 | tf_op jit(solution)/shard_map/ppermute | solution.py:231
  22.8 2.5 %collective-permute-done.3.rest_1_ = bf16[2,256,256]{2,1,0:T(8,128)(2,1)S(1)} collective-permute-done((bf16[2,256,256]{2,1,0:T(8,128)(2,1)S(1)}, bf16[2,256,256]{2,1,0:T(8,128)(2,1)S(1)}, u32[]{:S(2)}, u32[]{:S(2)}) %collective-permute-start.3) | collective-permute-done | bytes 262176 | tf_op jit(solution)/shard_map/ppermute | solution.py:231
  25.3 2.7 %collective-permute-start.6 = (bf16[1,256,256]{2,1,0:T(8,128)(2,1)S(1)}, bf16[1,256,256]{2,1,0:T(8,128)(2,1)S(1)}, u32[]{:S(2)}, u32[]{:S(2)}) collective-permute-start(bf16[1,256,256]{2,1,0:T(8,128)(2,1)S(1)} %get-tuple-element.42), channel_id=1, source_target_pairs={{0,4},{1,5},{2,6},{3,7},{4,0},{5,1},{6,2},{7,3},{8,12},{9,13},{10,... | collective-permute-start | bytes 393224 | tf_op jit(solution)/shard_map/ppermute | solution.py:231
  28.0 0.7 %collective-permute-start.9 = (bf16[2,256,256]{2,1,0:T(8,128)(2,1)S(1)}, bf16[2,256,256]{2,1,0:T(8,128)(2,1)S(1)}, u32[]{:S(2)}, u32[]{:S(2)}) collective-permute-start(bf16[2,256,256]{2,1,0:T(8,128)(2,1)S(1)} %shard_map.58), channel_id=1, source_target_pairs={{0,2},{1,3},{2,0},{3,1},{4,6},{5,7},{6,4},{7,5},{8,9},{9,8},{10,11... | collective-permute-start | bytes 786440 | tf_op jit(solution)/shard_map/ppermute | solution.py:231
  28.7 5.0 %collective-permute-done.6.got = bf16[1,256,256]{2,1,0:T(8,128)(2,1)S(1)} collective-permute-done((bf16[1,256,256]{2,1,0:T(8,128)(2,1)S(1)}, bf16[1,256,256]{2,1,0:T(8,128)(2,1)S(1)}, u32[]{:S(2)}, u32[]{:S(2)}) %collective-permute-start.6) | collective-permute-done | bytes 131104 | tf_op jit(solution)/shard_map/ppermute | solution.py:231
  33.8 1.1 %collective-permute-done.9.rest_1_ = bf16[2,256,256]{2,1,0:T(8,128)(2,1)S(1)} collective-permute-done((bf16[2,256,256]{2,1,0:T(8,128)(2,1)S(1)}, bf16[2,256,256]{2,1,0:T(8,128)(2,1)S(1)}, u32[]{:S(2)}, u32[]{:S(2)}) %collective-permute-start.9) | collective-permute-done | bytes 262176 | tf_op jit(solution)/shard_map/ppermute | solution.py:231
  35.0 2.1 %collective-permute-start.10 = (bf16[1,256,256]{2,1,0:T(8,128)(2,1)S(1)}, bf16[1,256,256]{2,1,0:T(8,128)(2,1)S(1)}, u32[]{:S(2)}, u32[]{:S(2)}) collective-permute-start(bf16[1,256,256]{2,1,0:T(8,128)(2,1)S(1)} %get-tuple-element.46), channel_id=1, source_target_pairs={{0,4},{1,5},{2,6},{3,7},{4,0},{5,1},{6,2},{7,3},{8,12},{9,13},{10,... | collective-permute-start | bytes 393224 | tf_op jit(solution)/shard_map/ppermute | solution.py:231
  37.1 5.2 %collective-permute-done.10.got = bf16[1,256,256]{2,1,0:T(8,128)(2,1)S(1)} collective-permute-done((bf16[1,256,256]{2,1,0:T(8,128)(2,1)S(1)}, bf16[1,256,256]{2,1,0:T(8,128)(2,1)S(1)}, u32[]{:S(2)}, u32[]{:S(2)}) %collective-permute-start.10) | collective-permute-done | bytes 131104 | tf_op jit(solution)/shard_map/ppermute | solution.py:231
  42.3 0.9 %shard_map.60 = f32[256,512]{1,0:T(8,128)} custom-call(f32[256,256]{1,0:T(8,128)S(1)} %shard_map.57.rest_2_.near, f32[1,256,256]{2,1,0:T(8,128)S(1)} %get-tuple-element.45.keep, bf16[1,256,256]{2,1,0:T(8,128)(2,1)S(1)} %collective-permute-done.10.got), custom_call_target="tpu_custom_call" | custom-call | tf_op jit(solution)/shard_map/pallas_call | solution.py:18
  (13 shorter events, 0.4 us)
Async XLA Ops:
  0.0 3.4 %collective-permute-start = (bf16[128,2048]{1,0:T(8,128)(2,1)}, bf16[128,2048]{1,0:T(8,128)(2,1)S(1)}, u32[]{:S(2)}, u32[]{:S(2)}) collective-permute-start(bf16[128,2048]{1,0:T(8,128)(2,1)} %target.1), channel_id=1, source_target_pairs={{0,8},{8,0},{16,24},{24,16},{1,9},{9,1},{17,25},{25,17},{2,10},{10... | collective-permute-start | bytes 1572872 | tf_op jit(solution)/shard_map/ppermute | solution.py:207
  3.5 10.7 %collective-permute-start.4 = (bf16[128,1024]{1,0:T(8,128)(2,1)S(1)}, bf16[128,1024]{1,0:T(8,128)(2,1)S(1)}, u32[]{:S(2)}, u32[]{:S(2)}) collective-permute-start(bf16[128,1024]{1,0:T(8,128)(2,1)S(1)} %get-tuple-element.38), channel_id=1, source_target_pairs={{0,16},{8,24},{16,0},{24,8},{1,17},{9,25},{17,1},{25,9},{2,18},{10... | collective-permute-start | bytes 786440 | tf_op jit(solution)/shard_map/ppermute | solution.py:207
  8.5 7.4 %collective-permute-start.2 = (bf16[2,256,256]{2,1,0:T(8,128)(2,1)S(1)}, bf16[2,256,256]{2,1,0:T(8,128)(2,1)S(1)}, u32[]{:S(2)}, u32[]{:S(2)}) collective-permute-start(bf16[2,256,256]{2,1,0:T(8,128)(2,1)S(1)} %get-tuple-element.33.rest_0_), channel_id=1, source_target_pairs={{0,1},{1,0},{2,3},{3,2},{4,5},{5,4},{6,7},{7,6},{8,10},{9,11},{10,... | collective-permute-start | bytes 786440 | tf_op jit(solution)/shard_map/ppermute | solution.py:231
  14.3 2.4 %collective-permute-start.5 = (bf16[128,1024]{1,0:T(8,128)(2,1)S(1)}, bf16[128,1024]{1,0:T(8,128)(2,1)S(1)}, u32[]{:S(2)}, u32[]{:S(2)}) collective-permute-start(bf16[128,1024]{1,0:T(8,128)(2,1)S(1)} %shard_map.52.mine), channel_id=1, source_target_pairs={{0,8},{8,0},{16,24},{24,16},{1,9},{9,1},{17,25},{25,17},{2,10},{10... | collective-permute-start | bytes 786440 | tf_op jit(solution)/shard_map/ppermute | solution.py:207
  14.4 8.4 %collective-permute-start.1 = (bf16[2,256,256]{2,1,0:T(8,128)(2,1)S(1)}, bf16[2,256,256]{2,1,0:T(8,128)(2,1)S(1)}, u32[]{:S(2)}, u32[]{:S(2)}) collective-permute-start(bf16[2,256,256]{2,1,0:T(8,128)(2,1)S(1)} %shard_map.49._), channel_id=1, source_target_pairs={{0,1},{1,0},{2,3},{3,2},{4,5},{5,4},{6,7},{7,6},{8,10},{9,11},{10,... | collective-permute-start | bytes 786440 | tf_op jit(solution)/shard_map/ppermute | solution.py:231
  15.9 9.3 %collective-permute-start.3 = (bf16[2,256,256]{2,1,0:T(8,128)(2,1)S(1)}, bf16[2,256,256]{2,1,0:T(8,128)(2,1)S(1)}, u32[]{:S(2)}, u32[]{:S(2)}) collective-permute-start(bf16[2,256,256]{2,1,0:T(8,128)(2,1)S(1)} %shard_map.51), channel_id=1, source_target_pairs={{0,2},{1,3},{2,0},{3,1},{4,6},{5,7},{6,4},{7,5},{8,9},{9,8},{10,11... | collective-permute-start | bytes 786440 | tf_op jit(solution)/shard_map/ppermute | solution.py:231
  17.7 10.3 %collective-permute-start.8 = (bf16[2,256,256]{2,1,0:T(8,128)(2,1)S(1)}, bf16[2,256,256]{2,1,0:T(8,128)(2,1)S(1)}, u32[]{:S(2)}, u32[]{:S(2)}) collective-permute-start(bf16[2,256,256]{2,1,0:T(8,128)(2,1)S(1)} %get-tuple-element.43.rest_0_), channel_id=1, source_target_pairs={{0,1},{1,0},{2,3},{3,2},{4,5},{5,4},{6,7},{7,6},{8,10},{9,11},{10,... | collective-permute-start | bytes 786440 | tf_op jit(solution)/shard_map/ppermute | solution.py:231
  20.0 13.8 %collective-permute-start.7 = (bf16[2,256,256]{2,1,0:T(8,128)(2,1)S(1)}, bf16[2,256,256]{2,1,0:T(8,128)(2,1)S(1)}, u32[]{:S(2)}, u32[]{:S(2)}) collective-permute-start(bf16[2,256,256]{2,1,0:T(8,128)(2,1)S(1)} %shard_map.56), channel_id=1, source_target_pairs={{0,1},{1,0},{2,3},{3,2},{4,5},{5,4},{6,7},{7,6},{8,10},{9,11},{10,... | collective-permute-start | bytes 786440 | tf_op jit(solution)/shard_map/ppermute | solution.py:231
  25.3 8.5 %collective-permute-start.6 = (bf16[1,256,256]{2,1,0:T(8,128)(2,1)S(1)}, bf16[1,256,256]{2,1,0:T(8,128)(2,1)S(1)}, u32[]{:S(2)}, u32[]{:S(2)}) collective-permute-start(bf16[1,256,256]{2,1,0:T(8,128)(2,1)S(1)} %get-tuple-element.42), channel_id=1, source_target_pairs={{0,4},{1,5},{2,6},{3,7},{4,0},{5,1},{6,2},{7,3},{8,12},{9,13},{10,... | collective-permute-start | bytes 393224 | tf_op jit(solution)/shard_map/ppermute | solution.py:231
  28.0 6.9 %collective-permute-start.9 = (bf16[2,256,256]{2,1,0:T(8,128)(2,1)S(1)}, bf16[2,256,256]{2,1,0:T(8,128)(2,1)S(1)}, u32[]{:S(2)}, u32[]{:S(2)}) collective-permute-start(bf16[2,256,256]{2,1,0:T(8,128)(2,1)S(1)} %shard_map.58), channel_id=1, source_target_pairs={{0,2},{1,3},{2,0},{3,1},{4,6},{5,7},{6,4},{7,5},{8,9},{9,8},{10,11... | collective-permute-start | bytes 786440 | tf_op jit(solution)/shard_map/ppermute | solution.py:231
  35.0 7.3 %collective-permute-start.10 = (bf16[1,256,256]{2,1,0:T(8,128)(2,1)S(1)}, bf16[1,256,256]{2,1,0:T(8,128)(2,1)S(1)}, u32[]{:S(2)}, u32[]{:S(2)}) collective-permute-start(bf16[1,256,256]{2,1,0:T(8,128)(2,1)S(1)} %get-tuple-element.46), channel_id=1, source_target_pairs={{0,4},{1,5},{2,6},{3,7},{4,0},{5,1},{6,2},{7,3},{8,12},{9,13},{10,... | collective-permute-start | bytes 393224 | tf_op jit(solution)/shard_map/ppermute | solution.py:231

commit v3 on v2

--- a/solution.py
+++ b/solution.py
@@ -26,12 +26,15 @@
     )(*args)
 
 
-def copy_kernel(x, *rest):
-    rest[-1][...] = x[...]
-
-
-def after(x, *others, flops=0):
-    return call(copy_kernel, [(x.shape, x.dtype)], x, *others, flops=flops)[0]
+def split_kernel(pieces, x, *rest):
+    width = x.shape[1] // pieces
+    for n, out in enumerate(rest[-pieces:]):
+        out[...] = x[:, n * width : (n + 1) * width]
+
+
+def split_after(x, pieces, *others, flops=0):
+    outs = [((x.shape[0], x.shape[1] // pieces), x.dtype)] * pieces
+    return call(functools.partial(split_kernel, pieces), outs, x, *others, flops=flops)
 
 
 def place(group):
@@ -67,17 +70,8 @@
     return pick(panel & 1, at)
 
 
-def rows_of(pool, parts, group, first, held):
-    rows = pool.shape[0] // parts
-    pairs = []
-    for n in range(held.shape[0]):
-        start = pl.multiple_of(row_block(parts, group, first + n) * rows, rows)
-        pairs.append((pool.at[pl.ds(start, rows), :], held.at[n]))
-    return pairs
-
-
-def load_kernel(parts, group, blocks, pool, active, target, pre, table, target_v, pre_v, even, one, sems):
-    copies = load([(active, table), (target, target_v), (pre, pre_v), *rows_of(pool, parts, group, 0, one)], sems)
+def load_kernel(group, blocks, active, target, pre, table, target_v, pre_v, even, sems):
+    copies = load([(active, table), (target, target_v), (pre, pre_v)], sems)
     j, panel = place(group)
     base = panel - (panel & 1)
     copies[0].wait()
@@ -114,51 +108,36 @@
         right[b * bs : (b + 1) * bs, PROWS:] = jnp.where(listed, zero, value)
 
 
-def near_send_kernel(parts, group, scale, pool, evens, rows, pre, one, right, two, send, sems):
-    copies = load(rows_of(pool, parts, group, parts // 4, two), sems)
+def near_send_kernel(parts, group, scale, pool, evens, rows, pre, right, send):
     bs = pre.shape[1]
     condition(scale, pre, evens[: pre.shape[0], :], lambda b: rows[:, b * bs : (b + 1) * bs], right)
-    scores([one], right, send)
-    for copy in copies:
-        copy.wait()
-
-
-def far_send_kernel(group, scale, evens, mine, other, pre, one, *rest):
+    scores(parts, group, 0, pool, right, send)
+
+
+def far_send_kernel(parts, group, scale, pool, evens, pre, *rest):
     right, send = rest[-2:]
     core = place(group)[1] & 1
     blocks, bs, _ = pre.shape
     depth = blocks // 2
 
     def rows_at(b):
-        columns = slice((b % depth) * bs, (b % depth + 1) * bs)
-        return jnp.where(core == b // depth, mine[:, columns], other[:, columns])
+        return jnp.where(core == b // depth, rest[b % depth][...], rest[depth + b % depth][...])
 
     condition(scale, pre, evens[blocks : 2 * blocks, :], rows_at, right)
-    scores([one], right, send)
-
-
-def scores(helds, right, *outs):
-    for held, out in zip(helds, outs):
-        for n in range(held.shape[0]):
-            out[n] = jnp.dot(held[n], right[...], preferred_element_type=F32).astype(out.dtype)
-
-
-def scores_kernel(held, right, *rest):
-    scores([held], right, rest[-1])
-
-
-def keep_kernel(three, four, right, *rest):
-    scores([three, four], right, *rest[-2:])
-
-
-def near_keep_kernel(parts, group, pool, right, _, keep, keep2, three, four, sems):
-    copies = load(
-        rows_of(pool, parts, group, parts // 2, three)
-        + rows_of(pool, parts, group, parts // 2 + parts // 4, four), sems
-    )
-    for copy in copies:
-        copy.wait()
-    scores([three, four], right, keep, keep2)
+    scores(parts, group, 0, pool, right, send)
+
+
+def scores(parts, group, quarter, pool, right, out):
+    count, rows = out.shape[:2]
+    for n in range(count):
+        start = pl.multiple_of(row_block(parts, group, quarter * count + n) * rows, rows)
+        value = jnp.dot(pool[pl.ds(start, rows), :], right[...], preferred_element_type=F32)
+        out[n] = value.astype(out.dtype)
+
+
+def scores_kernel(parts, group, quarters, pool, right, *rest):
+    for quarter, out in zip(quarters, rest[-len(quarters) :]):
+        scores(parts, group, quarter, pool, right, out)
 
 
 def add_kernel(keep, got, *rest):
@@ -207,11 +186,11 @@
         return lax.ppermute(x, axis, [(i, i ^ step) for i in range(size)])
 
     sibling = swap(own, "pool", group)
-    quarter = ((parts // 4, part, k), BF16)
-    _, own_v, pre_v, evens, one = call(
-        functools.partial(load_kernel, parts, group, blocks),
-        [(active.shape, active.dtype), (own.shape, BF16), (pre.shape, BF16), ((2 * blocks, bs), active.dtype), quarter],
-        pool, active, own, pre, copies=3 + parts // 4, far=(0, 1, 2, 3),
+    pool = pltpu.with_memory_space_constraint(pool, pltpu.VMEM)
+    _, own_v, pre_v, evens = call(
+        functools.partial(load_kernel, group, blocks),
+        [(active.shape, active.dtype), (own.shape, BF16), (pre.shape, BF16), ((2 * blocks, bs), active.dtype)],
+        active, own, pre, copies=3, far=(0, 1, 2), flops=5*10**9,
     )
     rows, half = call(
         functools.partial(select_kernel, group, blocks, bs), [((PROWS, k), BF16), ((PROWS, k // 2), BF16)],
@@ -246,28 +225,30 @@
             if keep.shape[0] == 1:
                 return keep, gots[0]
 
-    right, two, send = call(
-        functools.partial(near_send_kernel, parts, group, scale), [right_out, quarter, (shape, BF16)],
-        pool, evens, rows, pre_v, one, flops=0, copies=parts // 4, far=(0,),
+    right, send = call(
+        functools.partial(near_send_kernel, parts, group, scale), [right_out, (shape, BF16)],
+        pool, evens, rows, pre_v, flops=0,
     )
     got = exchange(send, 0)
-    send2 = call(scores_kernel, [(shape, BF16)], two, right, send)[0]
+
+    def more(quarters, dtype, right, *others, flops=0):
+        body = functools.partial(scores_kernel, parts, group, quarters)
+        return call(body, [(shape, dtype)] * len(quarters), pool, right, *others, flops=flops)
+
+    send2 = more([1], BF16, right, send, flops=0)[0]
     got2 = exchange(send2, 0)
-    keep, keep2, three, four = call(
-        functools.partial(near_keep_kernel, parts, group), [(shape, F32)] * 2 + [quarter] * 2,
-        pool, right, send2, flops=0, copies=parts // 2, far=(0,),
-    )
-    mine = after(mine, keep, flops=10**11)
-    other = swap(mine, "pool", group)
+    keep, keep2 = more([2, 3], F32, right, send2, flops=0)
+    mine = split_after(mine, blocks // 2, keep, flops=0)
+    other = [swap(piece, "pool", group) for piece in mine]
     right, far_send = call(
-        functools.partial(far_send_kernel, group, scale), [right_out, (shape, BF16)],
-        evens, mine, other, pre_v, one, flops=0,
+        functools.partial(far_send_kernel, parts, group, scale), [right_out, (shape, BF16)],
+        pool, evens, pre_v, *mine, *other, flops=0,
     )
     far_got = exchange(far_send, 0)
-    far_send2 = call(scores_kernel, [(shape, BF16)], two, right, far_send)[0]
+    far_send2 = more([1], BF16, right, far_send, got2)[0]
     far_got2 = exchange(far_send2, 0)
     got3 = exchange(add(keep, got), 1)
-    far_keep, far_keep2 = call(keep_kernel, [(shape, F32)] * 2, three, four, right, flops=0)
+    far_keep, far_keep2 = more([2, 3], F32, right, flops=0)
     near = rest(keep2, [got2, got3], far_keep)
     near_total = call(total_kernel, [((part, 2 * PROWS), F32)], *near, far_got2, flops=10**11)[0]
     far_got3 = exchange(add(far_keep, far_got, near[0]), 1)

time: 43.3 us -> 39.8 us (0.919)
  Pallas kernels: 13.7 us -> 9.68 us
  starting transfers between devices: 14.6 us -> 17.4 us
  waiting for transfers between devices: 14.8 us -> 12.4 us
    ppermute x8, waiting for transfers between devices: 14.8 us -> 10.6 us  [exchange(): return lax.ppermute(x, ('pool', 'tgt'), pairs)]
    pallas_call x15, Pallas kernels: 13.7 us -> 9.68 us  [call(): pl.pallas_call(body, in_specs=specs, out_specs=[VMEM] * len(outs), out_sh...]
    ppermute x8, starting transfers between devices: 11.4 us -> 13.8 us  [exchange(): return lax.ppermute(x, ('pool', 'tgt'), pairs)]
    ppermute x3 -> x4, waiting for transfers between devices: 0.01 us -> 1.83 us  [swap(): return lax.ppermute(x, axis, [(i, i ^ step) for i in range(size)])]
    ppermute x3 -> x4, starting transfers between devices: 3.13 us -> 3.6 us  [swap(): return lax.ppermute(x, axis, [(i, i ^ step) for i in range(size)])]
  transfers between devices with their start and end apart: 11 -> 12, of which waited for: 5 -> 5; matrix products, arithmetic and copies ran while one was open for 0% -> 0% of each run, Pallas kernels for 29% -> 22%
where the time goes in v3:
time: 39.8 us; the launch traced here: 39.6 us
  starting transfers between devices  17.4 us (44%)
  waiting for transfers between devices  12.4 us (31%)
  Pallas kernels  9.68 us (24%)
    ppermute x8, starting transfers between devices, exchange(): return lax.ppermute(x, ('pool', 'tgt'), pairs)  13.8 us
    ppermute x8, waiting for transfers between devices, exchange(): return lax.ppermute(x, ('pool', 'tgt'), pairs)  10.6 us
    pallas_call x15, Pallas kernels, call(): pl.pallas_call(body, in_specs=specs, out_specs=[VMEM] * len(outs), out_sh...  9.68 us
    ppermute x4, starting transfers between devices, swap(): return lax.ppermute(x, axis, [(i, i ^ step) for i in range(size)])  3.6 us
    ppermute x4, waiting for transfers between devices, swap(): return lax.ppermute(x, axis, [(i, i ^ step) for i in range(size)])  1.83 us
  transfers between devices with their start and end apart: 12, of which 5 were waited for; matrix products, arithmetic and copies ran while one was open for 0% of the time, Pallas kernels for 22%

profile of v3, /device:TPU:0, one launch (start us, length us, event | category | flops | bytes accessed | tf_op | source)
XLA Modules:
  0.0 39.6 jit_solution(17888476012867763100)
XLA Ops:
  0.0 0.5 %collective-permute-start = (bf16[128,2048]{1,0:T(8,128)(2,1)}, bf16[128,2048]{1,0:T(8,128)(2,1)S(1)}, u32[]{:S(2)}, u32[]{:S(2)}) collective-permute-start(bf16[128,2048]{1,0:T(8,128)(2,1)} %target.1), channel_id=1, source_target_pairs={{0,8},{8,0},{16,24},{24,16},{1,9},{9,1},{17,25},{25,17},{2,10},{10... | collective-permute-start | bytes 1572872 | tf_op jit(solution)/shard_map/ppermute | solution.py:186
  0.5 2.5 %shard_map.46 = (s32[4,16]{1,0:T(4,128)}, bf16[128,2048]{1,0:T(8,128)(2,1)S(1)}, bf16[4,512,512]{2,1,0:T(8,128)(2,1)S(1)}, s32[8,512]{1,0:T(8,128)S(1)}) custom-call(s32[4,16]{1,0:T(4,128)} %active.1, bf16[128,2048]{1,0:T(8,128)(2,1)} %target.1, bf16[4,512,512]{2,1,0:T(8,128)(2,1)} %pre.1), custom_call_target="tpu_custom_call" | custom-call | flops 5000000000 | tf_op jit(solution)/shard_map/pallas_call | solution.py:18
  3.1 2.6 %collective-permute-start.4 = (bf16[128,1024]{1,0:T(8,128)(2,1)S(1)}, bf16[128,1024]{1,0:T(8,128)(2,1)S(1)}, u32[]{:S(2)}, u32[]{:S(2)}) collective-permute-start(bf16[128,1024]{1,0:T(8,128)(2,1)S(1)} %get-tuple-element.32), channel_id=1, source_target_pairs={{0,16},{8,24},{16,0},{24,8},{1,17},{9,25},{17,1},{25,9},{2,18},{10... | collective-permute-start | bytes 786440 | tf_op jit(solution)/shard_map/ppermute | solution.py:186
  5.7 1.0 %shard_map.48 = (bf16[2048,256]{1,0:T(8,128)(2,1)S(1)}, bf16[2,256,256]{2,1,0:T(8,128)(2,1)S(1)}) custom-call(bf16[2048,2048]{1,0:T(8,128)(2,1)S(1)} %copy-done, s32[8,512]{1,0:T(8,128)S(1)} %get-tuple-element.24.evens, bf16[128,2048]{1,0:T(8,128)(2,1)S(1)} %get-tuple-element.26.rows, bf16[4,512,512]{2,1,0:T(8,128)(2,1)S(1)} %get-tuple-element.27.pre), custom_call_target="tpu_custom_call" | custom-call | tf_op jit(solution)/shard_map/pallas_call | solution.py:18
  6.7 1.5 %collective-permute-start.2 = (bf16[2,256,256]{2,1,0:T(8,128)(2,1)S(1)}, bf16[2,256,256]{2,1,0:T(8,128)(2,1)S(1)}, u32[]{:S(2)}, u32[]{:S(2)}) collective-permute-start(bf16[2,256,256]{2,1,0:T(8,128)(2,1)S(1)} %get-tuple-element.29.rest_0_), channel_id=1, source_target_pairs={{0,1},{1,0},{2,3},{3,2},{4,5},{5,4},{6,7},{7,6},{8,10},{9,11},{10,... | collective-permute-start | bytes 786440 | tf_op jit(solution)/shard_map/ppermute | solution.py:210
  8.3 0.7 %shard_map.49.rest_0_ = bf16[2,256,256]{2,1,0:T(8,128)(2,1)S(1)} custom-call(bf16[2048,2048]{1,0:T(8,128)(2,1)S(1)} %copy-done, bf16[2048,256]{1,0:T(8,128)(2,1)S(1)} %get-tuple-element.28.right, bf16[2,256,256]{2,1,0:T(8,128)(2,1)S(1)} %get-tuple-element.29.rest_0_), custom_call_target="tpu_custom_call" | custom-call | tf_op jit(solution)/shard_map/pallas_call | solution.py:18
  9.0 0.6 %collective-permute-start.1 = (bf16[2,256,256]{2,1,0:T(8,128)(2,1)S(1)}, bf16[2,256,256]{2,1,0:T(8,128)(2,1)S(1)}, u32[]{:S(2)}, u32[]{:S(2)}) collective-permute-start(bf16[2,256,256]{2,1,0:T(8,128)(2,1)S(1)} %shard_map.49.rest_0_), channel_id=1, source_target_pairs={{0,1},{1,0},{2,3},{3,2},{4,5},{5,4},{6,7},{7,6},{8,10},{9,11},{10,... | collective-permute-start | bytes 786440 | tf_op jit(solution)/shard_map/ppermute | solution.py:210
  9.6 1.2 %shard_map.50 = (f32[2,256,256]{2,1,0:T(8,128)S(1)}, f32[2,256,256]{2,1,0:T(8,128)S(1)}) custom-call(bf16[2048,2048]{1,0:T(8,128)(2,1)S(1)} %copy-done, bf16[2048,256]{1,0:T(8,128)(2,1)S(1)} %get-tuple-element.28.right, bf16[2,256,256]{2,1,0:T(8,128)(2,1)S(1)} %shard_map.49.rest_0_), custom_call_target="tpu_custom_call" | custom-call | tf_op jit(solution)/shard_map/pallas_call | solution.py:18
  10.8 1.8 %collective-permute-done.4.x = bf16[128,1024]{1,0:T(8,128)(2,1)S(1)} collective-permute-done((bf16[128,1024]{1,0:T(8,128)(2,1)S(1)}, bf16[128,1024]{1,0:T(8,128)(2,1)S(1)}, u32[]{:S(2)}, u32[]{:S(2)}) %collective-permute-start.4) | collective-permute-done | bytes 262176 | tf_op jit(solution)/shard_map/ppermute | solution.py:186
  12.7 0.5 %collective-permute-start.6 = (bf16[128,512]{1,0:T(8,128)(2,1)S(1)}, bf16[128,512]{1,0:T(8,128)(2,1)S(1)}, u32[]{:S(2)}, u32[]{:S(2)}) collective-permute-start(bf16[128,512]{1,0:T(8,128)(2,1)S(1)} %get-tuple-element.34.rest_1_), channel_id=1, source_target_pairs={{0,8},{8,0},{16,24},{24,16},{1,9},{9,1},{17,25},{25,17},{2,10},{10... | collective-permute-start | bytes 393224 | tf_op jit(solution)/shard_map/ppermute | solution.py:186
  13.3 1.9 %collective-permute-start.3 = (bf16[2,256,256]{2,1,0:T(8,128)(2,1)S(1)}, bf16[2,256,256]{2,1,0:T(8,128)(2,1)S(1)}, u32[]{:S(2)}, u32[]{:S(2)}) collective-permute-start(bf16[2,256,256]{2,1,0:T(8,128)(2,1)S(1)} %shard_map.51), channel_id=1, source_target_pairs={{0,2},{1,3},{2,0},{3,1},{4,6},{5,7},{6,4},{7,5},{8,9},{9,8},{10,11... | collective-permute-start | bytes 786440 | tf_op jit(solution)/shard_map/ppermute | solution.py:210
  15.2 1.0 %shard_map.53 = (bf16[2048,256]{1,0:T(8,128)(2,1)S(1)}, bf16[2,256,256]{2,1,0:T(8,128)(2,1)S(1)}) custom-call(bf16[2048,2048]{1,0:T(8,128)(2,1)S(1)} %copy-done, s32[8,512]{1,0:T(8,128)S(1)} %get-tuple-element.24.evens, bf16[4,512,512]{2,1,0:T(8,128)(2,1)S(1)} %get-tuple-element.27.pre, bf16[128,512]{1,0:T(8,128)(2,1)S(1)} %get-tuple-element.33.rest_0_, ...), custom_call_target="tpu_custom_call" | custom-call | tf_op jit(solution)/shard_map/pallas_call | solution.py:18
  16.2 1.6 %collective-permute-start.9 = (bf16[2,256,256]{2,1,0:T(8,128)(2,1)S(1)}, bf16[2,256,256]{2,1,0:T(8,128)(2,1)S(1)}, u32[]{:S(2)}, u32[]{:S(2)}) collective-permute-start(bf16[2,256,256]{2,1,0:T(8,128)(2,1)S(1)} %get-tuple-element.39.rest_0_), channel_id=1, source_target_pairs={{0,1},{1,0},{2,3},{3,2},{4,5},{5,4},{6,7},{7,6},{8,10},{9,11},{10,... | collective-permute-start | bytes 786440 | tf_op jit(solution)/shard_map/ppermute | solution.py:210
  17.8 0.7 %shard_map.56 = bf16[2,256,256]{2,1,0:T(8,128)(2,1)S(1)} custom-call(bf16[2048,2048]{1,0:T(8,128)(2,1)S(1)} %copy-done, bf16[2048,256]{1,0:T(8,128)(2,1)S(1)} %get-tuple-element.35.right, bf16[2,256,256]{2,1,0:T(8,128)(2,1)S(1)} %get-tuple-element.39.rest_0_, bf16[2,256,256]{2,1,0:T(8,128)(2,1)S(1)} %collective-permute-done.1.rest_0_.rest_1_), custom_call_target="tpu_custom_call" | custom-call | tf_op jit(solution)/shard_map/pallas_call | solution.py:18
  18.5 0.6 %collective-permute-start.8 = (bf16[2,256,256]{2,1,0:T(8,128)(2,1)S(1)}, bf16[2,256,256]{2,1,0:T(8,128)(2,1)S(1)}, u32[]{:S(2)}, u32[]{:S(2)}) collective-permute-start(bf16[2,256,256]{2,1,0:T(8,128)(2,1)S(1)} %shard_map.56), channel_id=1, source_target_pairs={{0,1},{1,0},{2,3},{3,2},{4,5},{5,4},{6,7},{7,6},{8,10},{9,11},{10,... | collective-permute-start | bytes 786440 | tf_op jit(solution)/shard_map/ppermute | solution.py:210
  19.1 1.2 %shard_map.54 = (f32[2,256,256]{2,1,0:T(8,128)S(1)}, f32[2,256,256]{2,1,0:T(8,128)S(1)}) custom-call(bf16[2048,2048]{1,0:T(8,128)(2,1)S(1)} %copy-done, bf16[2048,256]{1,0:T(8,128)(2,1)S(1)} %get-tuple-element.35.right), custom_call_target="tpu_custom_call" | custom-call | tf_op jit(solution)/shard_map/pallas_call | solution.py:18
  20.3 0.5 %collective-permute-done.3.rest_1_ = bf16[2,256,256]{2,1,0:T(8,128)(2,1)S(1)} collective-permute-done((bf16[2,256,256]{2,1,0:T(8,128)(2,1)S(1)}, bf16[2,256,256]{2,1,0:T(8,128)(2,1)S(1)}, u32[]{:S(2)}, u32[]{:S(2)}) %collective-permute-start.3) | collective-permute-done | bytes 262176 | tf_op jit(solution)/shard_map/ppermute | solution.py:210
  20.9 3.1 %collective-permute-start.7 = (bf16[1,256,256]{2,1,0:T(8,128)(2,1)S(1)}, bf16[1,256,256]{2,1,0:T(8,128)(2,1)S(1)}, u32[]{:S(2)}, u32[]{:S(2)}) collective-permute-start(bf16[1,256,256]{2,1,0:T(8,128)(2,1)S(1)} %get-tuple-element.38), channel_id=1, source_target_pairs={{0,4},{1,5},{2,6},{3,7},{4,0},{5,1},{6,2},{7,3},{8,12},{9,13},{10,... | collective-permute-start | bytes 393224 | tf_op jit(solution)/shard_map/ppermute | solution.py:210
  24.1 1.7 %collective-permute-start.10 = (bf16[2,256,256]{2,1,0:T(8,128)(2,1)S(1)}, bf16[2,256,256]{2,1,0:T(8,128)(2,1)S(1)}, u32[]{:S(2)}, u32[]{:S(2)}) collective-permute-start(bf16[2,256,256]{2,1,0:T(8,128)(2,1)S(1)} %shard_map.58), channel_id=1, source_target_pairs={{0,2},{1,3},{2,0},{3,1},{4,6},{5,7},{6,4},{7,5},{8,9},{9,8},{10,11... | collective-permute-start | bytes 786440 | tf_op jit(solution)/shard_map/ppermute | solution.py:210
  25.7 1.8 %collective-permute-done.7.got = bf16[1,256,256]{2,1,0:T(8,128)(2,1)S(1)} collective-permute-done((bf16[1,256,256]{2,1,0:T(8,128)(2,1)S(1)}, bf16[1,256,256]{2,1,0:T(8,128)(2,1)S(1)}, u32[]{:S(2)}, u32[]{:S(2)}) %collective-permute-start.7) | collective-permute-done | bytes 131104 | tf_op jit(solution)/shard_map/ppermute | solution.py:210
  27.6 3.4 %collective-permute-done.10.rest_1_ = bf16[2,256,256]{2,1,0:T(8,128)(2,1)S(1)} collective-permute-done((bf16[2,256,256]{2,1,0:T(8,128)(2,1)S(1)}, bf16[2,256,256]{2,1,0:T(8,128)(2,1)S(1)}, u32[]{:S(2)}, u32[]{:S(2)}) %collective-permute-start.10) | collective-permute-done | bytes 262176 | tf_op jit(solution)/shard_map/ppermute | solution.py:210
  31.0 2.9 %collective-permute-start.11 = (bf16[1,256,256]{2,1,0:T(8,128)(2,1)S(1)}, bf16[1,256,256]{2,1,0:T(8,128)(2,1)S(1)}, u32[]{:S(2)}, u32[]{:S(2)}) collective-permute-start(bf16[1,256,256]{2,1,0:T(8,128)(2,1)S(1)} %get-tuple-element.42), channel_id=1, source_target_pairs={{0,4},{1,5},{2,6},{3,7},{4,0},{5,1},{6,2},{7,3},{8,12},{9,13},{10,... | collective-permute-start | bytes 393224 | tf_op jit(solution)/shard_map/ppermute | solution.py:210
  33.9 4.8 %collective-permute-done.11.got = bf16[1,256,256]{2,1,0:T(8,128)(2,1)S(1)} collective-permute-done((bf16[1,256,256]{2,1,0:T(8,128)(2,1)S(1)}, bf16[1,256,256]{2,1,0:T(8,128)(2,1)S(1)}, u32[]{:S(2)}, u32[]{:S(2)}) %collective-permute-start.11) | collective-permute-done | bytes 131104 | tf_op jit(solution)/shard_map/ppermute | solution.py:210
  38.7 0.9 %shard_map.60 = f32[256,512]{1,0:T(8,128)} custom-call(f32[256,256]{1,0:T(8,128)S(1)} %shard_map.57.rest_2_.near, f32[1,256,256]{2,1,0:T(8,128)S(1)} %get-tuple-element.41.keep, bf16[1,256,256]{2,1,0:T(8,128)(2,1)S(1)} %collective-permute-done.11.got), custom_call_target="tpu_custom_call" | custom-call | tf_op jit(solution)/shard_map/pallas_call | solution.py:18
  (17 shorter events, 0.5 us)
Async XLA Ops:
  0.0 3.0 %collective-permute-start = (bf16[128,2048]{1,0:T(8,128)(2,1)}, bf16[128,2048]{1,0:T(8,128)(2,1)S(1)}, u32[]{:S(2)}, u32[]{:S(2)}) collective-permute-start(bf16[128,2048]{1,0:T(8,128)(2,1)} %target.1), channel_id=1, source_target_pairs={{0,8},{8,0},{16,24},{24,16},{1,9},{9,1},{17,25},{25,17},{2,10},{10... | collective-permute-start | bytes 1572872 | tf_op jit(solution)/shard_map/ppermute | solution.py:186
  0.5 5.2 %copy-start = (bf16[2048,2048]{1,0:T(8,128)(2,1)S(1)}, bf16[2048,2048]{1,0:T(8,128)(2,1)}, u32[]{:S(2)}) copy-start(bf16[2048,2048]{1,0:T(8,128)(2,1)} %pool.11) | copy-start | bytes 25165828
  3.1 9.6 %collective-permute-start.4 = (bf16[128,1024]{1,0:T(8,128)(2,1)S(1)}, bf16[128,1024]{1,0:T(8,128)(2,1)S(1)}, u32[]{:S(2)}, u32[]{:S(2)}) collective-permute-start(bf16[128,1024]{1,0:T(8,128)(2,1)S(1)} %get-tuple-element.32), channel_id=1, source_target_pairs={{0,16},{8,24},{16,0},{24,8},{1,17},{9,25},{17,1},{25,9},{2,18},{10... | collective-permute-start | bytes 786440 | tf_op jit(solution)/shard_map/ppermute | solution.py:186
  6.7 6.5 %collective-permute-start.2 = (bf16[2,256,256]{2,1,0:T(8,128)(2,1)S(1)}, bf16[2,256,256]{2,1,0:T(8,128)(2,1)S(1)}, u32[]{:S(2)}, u32[]{:S(2)}) collective-permute-start(bf16[2,256,256]{2,1,0:T(8,128)(2,1)S(1)} %get-tuple-element.29.rest_0_), channel_id=1, source_target_pairs={{0,1},{1,0},{2,3},{3,2},{4,5},{5,4},{6,7},{7,6},{8,10},{9,11},{10,... | collective-permute-start | bytes 786440 | tf_op jit(solution)/shard_map/ppermute | solution.py:210
  9.0 8.8 %collective-permute-start.1 = (bf16[2,256,256]{2,1,0:T(8,128)(2,1)S(1)}, bf16[2,256,256]{2,1,0:T(8,128)(2,1)S(1)}, u32[]{:S(2)}, u32[]{:S(2)}) collective-permute-start(bf16[2,256,256]{2,1,0:T(8,128)(2,1)S(1)} %shard_map.49.rest_0_), channel_id=1, source_target_pairs={{0,1},{1,0},{2,3},{3,2},{4,5},{5,4},{6,7},{7,6},{8,10},{9,11},{10,... | collective-permute-start | bytes 786440 | tf_op jit(solution)/shard_map/ppermute | solution.py:210
  12.7 2.5 %collective-permute-start.5 = (bf16[128,512]{1,0:T(8,128)(2,1)S(1)}, bf16[128,512]{1,0:T(8,128)(2,1)S(1)}, u32[]{:S(2)}, u32[]{:S(2)}) collective-permute-start(bf16[128,512]{1,0:T(8,128)(2,1)S(1)} %get-tuple-element.33.rest_0_), channel_id=1, source_target_pairs={{0,8},{8,0},{16,24},{24,16},{1,9},{9,1},{17,25},{25,17},{2,10},{10... | collective-permute-start | bytes 393224 | tf_op jit(solution)/shard_map/ppermute | solution.py:186
  12.7 2.4 %collective-permute-start.6 = (bf16[128,512]{1,0:T(8,128)(2,1)S(1)}, bf16[128,512]{1,0:T(8,128)(2,1)S(1)}, u32[]{:S(2)}, u32[]{:S(2)}) collective-permute-start(bf16[128,512]{1,0:T(8,128)(2,1)S(1)} %get-tuple-element.34.rest_1_), channel_id=1, source_target_pairs={{0,8},{8,0},{16,24},{24,16},{1,9},{9,1},{17,25},{25,17},{2,10},{10... | collective-permute-start | bytes 393224 | tf_op jit(solution)/shard_map/ppermute | solution.py:186
  13.3 7.5 %collective-permute-start.3 = (bf16[2,256,256]{2,1,0:T(8,128)(2,1)S(1)}, bf16[2,256,256]{2,1,0:T(8,128)(2,1)S(1)}, u32[]{:S(2)}, u32[]{:S(2)}) collective-permute-start(bf16[2,256,256]{2,1,0:T(8,128)(2,1)S(1)} %shard_map.51), channel_id=1, source_target_pairs={{0,2},{1,3},{2,0},{3,1},{4,6},{5,7},{6,4},{7,5},{8,9},{9,8},{10,11... | collective-permute-start | bytes 786440 | tf_op jit(solution)/shard_map/ppermute | solution.py:210
  16.2 7.9 %collective-permute-start.9 = (bf16[2,256,256]{2,1,0:T(8,128)(2,1)S(1)}, bf16[2,256,256]{2,1,0:T(8,128)(2,1)S(1)}, u32[]{:S(2)}, u32[]{:S(2)}) collective-permute-start(bf16[2,256,256]{2,1,0:T(8,128)(2,1)S(1)} %get-tuple-element.39.rest_0_), channel_id=1, source_target_pairs={{0,1},{1,0},{2,3},{3,2},{4,5},{5,4},{6,7},{7,6},{8,10},{9,11},{10,... | collective-permute-start | bytes 786440 | tf_op jit(solution)/shard_map/ppermute | solution.py:210
  18.5 9.1 %collective-permute-start.8 = (bf16[2,256,256]{2,1,0:T(8,128)(2,1)S(1)}, bf16[2,256,256]{2,1,0:T(8,128)(2,1)S(1)}, u32[]{:S(2)}, u32[]{:S(2)}) collective-permute-start(bf16[2,256,256]{2,1,0:T(8,128)(2,1)S(1)} %shard_map.56), channel_id=1, source_target_pairs={{0,1},{1,0},{2,3},{3,2},{4,5},{5,4},{6,7},{7,6},{8,10},{9,11},{10,... | collective-permute-start | bytes 786440 | tf_op jit(solution)/shard_map/ppermute | solution.py:210
  20.9 6.6 %collective-permute-start.7 = (bf16[1,256,256]{2,1,0:T(8,128)(2,1)S(1)}, bf16[1,256,256]{2,1,0:T(8,128)(2,1)S(1)}, u32[]{:S(2)}, u32[]{:S(2)}) collective-permute-start(bf16[1,256,256]{2,1,0:T(8,128)(2,1)S(1)} %get-tuple-element.38), channel_id=1, source_target_pairs={{0,4},{1,5},{2,6},{3,7},{4,0},{5,1},{6,2},{7,3},{8,12},{9,13},{10,... | collective-permute-start | bytes 393224 | tf_op jit(solution)/shard_map/ppermute | solution.py:210
  24.1 6.9 %collective-permute-start.10 = (bf16[2,256,256]{2,1,0:T(8,128)(2,1)S(1)}, bf16[2,256,256]{2,1,0:T(8,128)(2,1)S(1)}, u32[]{:S(2)}, u32[]{:S(2)}) collective-permute-start(bf16[2,256,256]{2,1,0:T(8,128)(2,1)S(1)} %shard_map.58), channel_id=1, source_target_pairs={{0,2},{1,3},{2,0},{3,1},{4,6},{5,7},{6,4},{7,5},{8,9},{9,8},{10,11... | collective-permute-start | bytes 786440 | tf_op jit(solution)/shard_map/ppermute | solution.py:210
  31.0 7.7 %collective-permute-start.11 = (bf16[1,256,256]{2,1,0:T(8,128)(2,1)S(1)}, bf16[1,256,256]{2,1,0:T(8,128)(2,1)S(1)}, u32[]{:S(2)}, u32[]{:S(2)}) collective-permute-start(bf16[1,256,256]{2,1,0:T(8,128)(2,1)S(1)} %get-tuple-element.42), channel_id=1, source_target_pairs={{0,4},{1,5},{2,6},{3,7},{4,0},{5,1},{6,2},{7,3},{8,12},{9,13},{10,... | collective-permute-start | bytes 393224 | tf_op jit(solution)/shard_map/ppermute | solution.py:210

commit v4 on v3

--- a/solution.py
+++ b/solution.py
@@ -70,8 +70,8 @@
     return pick(panel & 1, at)
 
 
-def load_kernel(group, blocks, active, target, pre, table, target_v, pre_v, even, sems):
-    copies = load([(active, table), (target, target_v), (pre, pre_v)], sems)
+def load_kernel(group, blocks, active, target, table, target_v, even, sems):
+    copies = load([(active, table), (target, target_v)], sems)
     j, panel = place(group)
     base = panel - (panel & 1)
     copies[0].wait()
@@ -187,10 +187,11 @@
 
     sibling = swap(own, "pool", group)
     pool = pltpu.with_memory_space_constraint(pool, pltpu.VMEM)
-    _, own_v, pre_v, evens = call(
+    pre = pltpu.with_memory_space_constraint(pre, pltpu.VMEM)
+    _, own_v, evens = call(
         functools.partial(load_kernel, group, blocks),
-        [(active.shape, active.dtype), (own.shape, BF16), (pre.shape, BF16), ((2 * blocks, bs), active.dtype)],
-        active, own, pre, copies=3, far=(0, 1, 2), flops=5*10**9,
+        [(active.shape, active.dtype), (own.shape, BF16), ((2 * blocks, bs), active.dtype)],
+        active, own, copies=2, far=(0, 1), flops=5*10**9,
     )
     rows, half = call(
         functools.partial(select_kernel, group, blocks, bs), [((PROWS, k), BF16), ((PROWS, k // 2), BF16)],
@@ -227,7 +228,7 @@
 
     right, send = call(
         functools.partial(near_send_kernel, parts, group, scale), [right_out, (shape, BF16)],
-        pool, evens, rows, pre_v, flops=0,
+        pool, evens, rows, pre, flops=0,
     )
     got = exchange(send, 0)
 
@@ -238,20 +239,22 @@
     send2 = more([1], BF16, right, send, flops=0)[0]
     got2 = exchange(send2, 0)
     keep, keep2 = more([2, 3], F32, right, send2, flops=0)
+    near_next = add(keep, got)
     mine = split_after(mine, blocks // 2, keep, flops=0)
     other = [swap(piece, "pool", group) for piece in mine]
     right, far_send = call(
         functools.partial(far_send_kernel, parts, group, scale), [right_out, (shape, BF16)],
-        pool, evens, pre_v, *mine, *other, flops=0,
+        pool, evens, pre, *mine, *other, flops=0,
     )
     far_got = exchange(far_send, 0)
     far_send2 = more([1], BF16, right, far_send, got2)[0]
     far_got2 = exchange(far_send2, 0)
-    got3 = exchange(add(keep, got), 1)
+    got3 = exchange(near_next, 1)
     far_keep, far_keep2 = more([2, 3], F32, right, flops=0)
     near = rest(keep2, [got2, got3], far_keep)
     near_total = call(total_kernel, [((part, 2 * PROWS), F32)], *near, far_got2, flops=10**11)[0]
-    far_got3 = exchange(add(far_keep, far_got, near[0]), 1)
+    far_next = add(far_keep, far_got, near[0])
+    far_got3 = exchange(far_next, 1)
     far = rest(far_keep2, [far_got2, far_got3], near_total)
     out = ((part, 4 * PROWS), F32)
     return call(functools.partial(last_kernel, group), [out], near_total, *far, kind=jax.ShapeDtypeStruct)[0]

time: 39.8 us -> 39.1 us (0.982)
  Pallas kernels: 9.68 us -> 8.95 us
  starting transfers between devices: 17.4 us -> 18.1 us
  waiting for transfers between devices: 12.4 us -> 11.8 us
    pallas_call x15, Pallas kernels: 9.68 us -> 8.95 us  [call(): pl.pallas_call(body, in_specs=specs, out_specs=[VMEM] * len(outs), out_sh...]
    ppermute x8, waiting for transfers between devices: 10.6 us -> 10.1 us  [exchange(): return lax.ppermute(x, ('pool', 'tgt'), pairs)]
    ppermute x8, starting transfers between devices: 13.8 us -> 14.3 us  [exchange(): return lax.ppermute(x, ('pool', 'tgt'), pairs)]
  transfers between devices with their start and end apart: 12 -> 12, of which waited for: 5 -> 5; matrix products, arithmetic and copies ran while one was open for 0% -> 0% of each run, Pallas kernels for 22% -> 20%
where the time goes in v4:
time: 39.1 us; the launch traced here: 39 us
  starting transfers between devices  18.1 us (46%)
  waiting for transfers between devices  11.8 us (30%)
  Pallas kernels  8.95 us (23%)
    ppermute x8, starting transfers between devices, exchange(): return lax.ppermute(x, ('pool', 'tgt'), pairs)  14.3 us
    ppermute x8, waiting for transfers between devices, exchange(): return lax.ppermute(x, ('pool', 'tgt'), pairs)  10.1 us
    pallas_call x15, Pallas kernels, call(): pl.pallas_call(body, in_specs=specs, out_specs=[VMEM] * len(outs), out_sh...  8.95 us
    ppermute x4, starting transfers between devices, swap(): return lax.ppermute(x, axis, [(i, i ^ step) for i in range(size)])  3.87 us
    ppermute x4, waiting for transfers between devices, swap(): return lax.ppermute(x, axis, [(i, i ^ step) for i in range(size)])  1.69 us
  transfers between devices with their start and end apart: 12, of which 5 were waited for; matrix products, arithmetic and copies ran while one was open for 0% of the time, Pallas kernels for 20%

profile of v4, /device:TPU:0, one launch (start us, length us, event | category | flops | bytes accessed | tf_op | source)
XLA Modules:
  0.0 39.0 jit_solution(3853619236532331417)
XLA Ops:
  0.0 0.5 %collective-permute-start = (bf16[128,2048]{1,0:T(8,128)(2,1)}, bf16[128,2048]{1,0:T(8,128)(2,1)S(1)}, u32[]{:S(2)}, u32[]{:S(2)}) collective-permute-start(bf16[128,2048]{1,0:T(8,128)(2,1)} %target.1), channel_id=1, source_target_pairs={{0,8},{8,0},{16,24},{24,16},{1,9},{9,1},{17,25},{25,17},{2,10},{10... | collective-permute-start | bytes 1572872 | tf_op jit(solution)/shard_map/ppermute | solution.py:186
  0.5 1.8 %shard_map.46 = (s32[4,16]{1,0:T(4,128)}, bf16[128,2048]{1,0:T(8,128)(2,1)S(1)}, s32[8,512]{1,0:T(8,128)S(1)}) custom-call(s32[4,16]{1,0:T(4,128)} %active.1, bf16[128,2048]{1,0:T(8,128)(2,1)} %target.1), custom_call_target="tpu_custom_call" | custom-call | flops 5000000000 | tf_op jit(solution)/shard_map/pallas_call | solution.py:18
  2.4 2.8 %collective-permute-start.4 = (bf16[128,1024]{1,0:T(8,128)(2,1)S(1)}, bf16[128,1024]{1,0:T(8,128)(2,1)S(1)}, u32[]{:S(2)}, u32[]{:S(2)}) collective-permute-start(bf16[128,1024]{1,0:T(8,128)(2,1)S(1)} %get-tuple-element.30), channel_id=1, source_target_pairs={{0,16},{8,24},{16,0},{24,8},{1,17},{9,25},{17,1},{25,9},{2,18},{10... | collective-permute-start | bytes 786440 | tf_op jit(solution)/shard_map/ppermute | solution.py:186
  5.3 1.0 %shard_map.48 = (bf16[2048,256]{1,0:T(8,128)(2,1)S(1)}, bf16[2,256,256]{2,1,0:T(8,128)(2,1)S(1)}) custom-call(bf16[2048,2048]{1,0:T(8,128)(2,1)S(1)} %copy-done, s32[8,512]{1,0:T(8,128)S(1)} %get-tuple-element.23.evens, bf16[128,2048]{1,0:T(8,128)(2,1)S(1)} %get-tuple-element.25.rows, bf16[4,512,512]{2,1,0:T(8,128)(2,1)S(1)} %copy-done.1), custom_call_target="tpu_custom_call" | custom-call | tf_op jit(solution)/shard_map/pallas_call | solution.py:18
  6.3 1.9 %collective-permute-start.2 = (bf16[2,256,256]{2,1,0:T(8,128)(2,1)S(1)}, bf16[2,256,256]{2,1,0:T(8,128)(2,1)S(1)}, u32[]{:S(2)}, u32[]{:S(2)}) collective-permute-start(bf16[2,256,256]{2,1,0:T(8,128)(2,1)S(1)} %get-tuple-element.27.rest_0_), channel_id=1, source_target_pairs={{0,1},{1,0},{2,3},{3,2},{4,5},{5,4},{6,7},{7,6},{8,10},{9,11},{10,... | collective-permute-start | bytes 786440 | tf_op jit(solution)/shard_map/ppermute | solution.py:211
  8.2 0.7 %shard_map.49.rest_0_ = bf16[2,256,256]{2,1,0:T(8,128)(2,1)S(1)} custom-call(bf16[2048,2048]{1,0:T(8,128)(2,1)S(1)} %copy-done, bf16[2048,256]{1,0:T(8,128)(2,1)S(1)} %get-tuple-element.26.right, bf16[2,256,256]{2,1,0:T(8,128)(2,1)S(1)} %get-tuple-element.27.rest_0_), custom_call_target="tpu_custom_call" | custom-call | tf_op jit(solution)/shard_map/pallas_call | solution.py:18
  8.9 0.3 collective-permute-start.1
  9.1 1.2 %shard_map.50 = (f32[2,256,256]{2,1,0:T(8,128)S(1)}, f32[2,256,256]{2,1,0:T(8,128)S(1)}) custom-call(bf16[2048,2048]{1,0:T(8,128)(2,1)S(1)} %copy-done, bf16[2048,256]{1,0:T(8,128)(2,1)S(1)} %get-tuple-element.26.right, bf16[2,256,256]{2,1,0:T(8,128)(2,1)S(1)} %shard_map.49.rest_0_), custom_call_target="tpu_custom_call" | custom-call | tf_op jit(solution)/shard_map/pallas_call | solution.py:18
  10.4 1.7 %collective-permute-done.4.x = bf16[128,1024]{1,0:T(8,128)(2,1)S(1)} collective-permute-done((bf16[128,1024]{1,0:T(8,128)(2,1)S(1)}, bf16[128,1024]{1,0:T(8,128)(2,1)S(1)}, u32[]{:S(2)}, u32[]{:S(2)}) %collective-permute-start.4) | collective-permute-done | bytes 262176 | tf_op jit(solution)/shard_map/ppermute | solution.py:186
  12.2 0.5 %collective-permute-start.6 = (bf16[128,512]{1,0:T(8,128)(2,1)S(1)}, bf16[128,512]{1,0:T(8,128)(2,1)S(1)}, u32[]{:S(2)}, u32[]{:S(2)}) collective-permute-start(bf16[128,512]{1,0:T(8,128)(2,1)S(1)} %get-tuple-element.32.rest_1_), channel_id=1, source_target_pairs={{0,8},{8,0},{16,24},{24,16},{1,9},{9,1},{17,25},{25,17},{2,10},{10... | collective-permute-start | bytes 393224 | tf_op jit(solution)/shard_map/ppermute | solution.py:186
  12.8 2.0 %collective-permute-start.3 = (bf16[2,256,256]{2,1,0:T(8,128)(2,1)S(1)}, bf16[2,256,256]{2,1,0:T(8,128)(2,1)S(1)}, u32[]{:S(2)}, u32[]{:S(2)}) collective-permute-start(bf16[2,256,256]{2,1,0:T(8,128)(2,1)S(1)} %shard_map.51), channel_id=1, source_target_pairs={{0,2},{1,3},{2,0},{3,1},{4,6},{5,7},{6,4},{7,5},{8,9},{9,8},{10,11... | collective-permute-start | bytes 786440 | tf_op jit(solution)/shard_map/ppermute | solution.py:211
  14.7 1.0 %shard_map.53 = (bf16[2048,256]{1,0:T(8,128)(2,1)S(1)}, bf16[2,256,256]{2,1,0:T(8,128)(2,1)S(1)}) custom-call(bf16[2048,2048]{1,0:T(8,128)(2,1)S(1)} %copy-done, s32[8,512]{1,0:T(8,128)S(1)} %get-tuple-element.23.evens, bf16[4,512,512]{2,1,0:T(8,128)(2,1)S(1)} %copy-done.1, bf16[128,512]{1,0:T(8,128)(2,1)S(1)} %get-tuple-element.31.rest_0_, ...), custom_call_target="tpu_custom_call" | custom-call | tf_op jit(solution)/shard_map/pallas_call | solution.py:18
  15.8 1.6 %collective-permute-start.9 = (bf16[2,256,256]{2,1,0:T(8,128)(2,1)S(1)}, bf16[2,256,256]{2,1,0:T(8,128)(2,1)S(1)}, u32[]{:S(2)}, u32[]{:S(2)}) collective-permute-start(bf16[2,256,256]{2,1,0:T(8,128)(2,1)S(1)} %get-tuple-element.37.rest_0_), channel_id=1, source_target_pairs={{0,1},{1,0},{2,3},{3,2},{4,5},{5,4},{6,7},{7,6},{8,10},{9,11},{10,... | collective-permute-start | bytes 786440 | tf_op jit(solution)/shard_map/ppermute | solution.py:211
  17.3 0.7 %shard_map.56 = bf16[2,256,256]{2,1,0:T(8,128)(2,1)S(1)} custom-call(bf16[2048,2048]{1,0:T(8,128)(2,1)S(1)} %copy-done, bf16[2048,256]{1,0:T(8,128)(2,1)S(1)} %get-tuple-element.33.right, bf16[2,256,256]{2,1,0:T(8,128)(2,1)S(1)} %get-tuple-element.37.rest_0_, bf16[2,256,256]{2,1,0:T(8,128)(2,1)S(1)} %collective-permute-done.1.rest_0_.rest_1_), custom_call_target="tpu_custom_call" | custom-call | tf_op jit(solution)/shard_map/pallas_call | solution.py:18
  18.0 0.6 %collective-permute-start.8 = (bf16[2,256,256]{2,1,0:T(8,128)(2,1)S(1)}, bf16[2,256,256]{2,1,0:T(8,128)(2,1)S(1)}, u32[]{:S(2)}, u32[]{:S(2)}) collective-permute-start(bf16[2,256,256]{2,1,0:T(8,128)(2,1)S(1)} %shard_map.56), channel_id=1, source_target_pairs={{0,1},{1,0},{2,3},{3,2},{4,5},{5,4},{6,7},{7,6},{8,10},{9,11},{10,... | collective-permute-start | bytes 786440 | tf_op jit(solution)/shard_map/ppermute | solution.py:211
  18.6 1.2 %shard_map.54 = (f32[2,256,256]{2,1,0:T(8,128)S(1)}, f32[2,256,256]{2,1,0:T(8,128)S(1)}) custom-call(bf16[2048,2048]{1,0:T(8,128)(2,1)S(1)} %copy-done, bf16[2048,256]{1,0:T(8,128)(2,1)S(1)} %get-tuple-element.33.right), custom_call_target="tpu_custom_call" | custom-call | tf_op jit(solution)/shard_map/pallas_call | solution.py:18
  19.9 0.5 %collective-permute-done.3.rest_1_ = bf16[2,256,256]{2,1,0:T(8,128)(2,1)S(1)} collective-permute-done((bf16[2,256,256]{2,1,0:T(8,128)(2,1)S(1)}, bf16[2,256,256]{2,1,0:T(8,128)(2,1)S(1)}, u32[]{:S(2)}, u32[]{:S(2)}) %collective-permute-start.3) | collective-permute-done | bytes 262176 | tf_op jit(solution)/shard_map/ppermute | solution.py:211
  20.4 3.4 %collective-permute-start.7 = (bf16[1,256,256]{2,1,0:T(8,128)(2,1)S(1)}, bf16[1,256,256]{2,1,0:T(8,128)(2,1)S(1)}, u32[]{:S(2)}, u32[]{:S(2)}) collective-permute-start(bf16[1,256,256]{2,1,0:T(8,128)(2,1)S(1)} %get-tuple-element.36), channel_id=1, source_target_pairs={{0,4},{1,5},{2,6},{3,7},{4,0},{5,1},{6,2},{7,3},{8,12},{9,13},{10,... | collective-permute-start | bytes 393224 | tf_op jit(solution)/shard_map/ppermute | solution.py:211
  23.9 1.6 %collective-permute-start.10 = (bf16[2,256,256]{2,1,0:T(8,128)(2,1)S(1)}, bf16[2,256,256]{2,1,0:T(8,128)(2,1)S(1)}, u32[]{:S(2)}, u32[]{:S(2)}) collective-permute-start(bf16[2,256,256]{2,1,0:T(8,128)(2,1)S(1)} %shard_map.58), channel_id=1, source_target_pairs={{0,2},{1,3},{2,0},{3,1},{4,6},{5,7},{6,4},{7,5},{8,9},{9,8},{10,11... | collective-permute-start | bytes 786440 | tf_op jit(solution)/shard_map/ppermute | solution.py:211
  25.5 1.6 %collective-permute-done.7.got = bf16[1,256,256]{2,1,0:T(8,128)(2,1)S(1)} collective-permute-done((bf16[1,256,256]{2,1,0:T(8,128)(2,1)S(1)}, bf16[1,256,256]{2,1,0:T(8,128)(2,1)S(1)}, u32[]{:S(2)}, u32[]{:S(2)}) %collective-permute-start.7) | collective-permute-done | bytes 131104 | tf_op jit(solution)/shard_map/ppermute | solution.py:211
  27.1 3.3 %collective-permute-done.10.rest_1_ = bf16[2,256,256]{2,1,0:T(8,128)(2,1)S(1)} collective-permute-done((bf16[2,256,256]{2,1,0:T(8,128)(2,1)S(1)}, bf16[2,256,256]{2,1,0:T(8,128)(2,1)S(1)}, u32[]{:S(2)}, u32[]{:S(2)}) %collective-permute-start.10) | collective-permute-done | bytes 262176 | tf_op jit(solution)/shard_map/ppermute | solution.py:211
  30.5 3.0 %collective-permute-start.11 = (bf16[1,256,256]{2,1,0:T(8,128)(2,1)S(1)}, bf16[1,256,256]{2,1,0:T(8,128)(2,1)S(1)}, u32[]{:S(2)}, u32[]{:S(2)}) collective-permute-start(bf16[1,256,256]{2,1,0:T(8,128)(2,1)S(1)} %get-tuple-element.40), channel_id=1, source_target_pairs={{0,4},{1,5},{2,6},{3,7},{4,0},{5,1},{6,2},{7,3},{8,12},{9,13},{10,... | collective-permute-start | bytes 393224 | tf_op jit(solution)/shard_map/ppermute | solution.py:211
  33.5 4.6 %collective-permute-done.11.got = bf16[1,256,256]{2,1,0:T(8,128)(2,1)S(1)} collective-permute-done((bf16[1,256,256]{2,1,0:T(8,128)(2,1)S(1)}, bf16[1,256,256]{2,1,0:T(8,128)(2,1)S(1)}, u32[]{:S(2)}, u32[]{:S(2)}) %collective-permute-start.11) | collective-permute-done | bytes 131104 | tf_op jit(solution)/shard_map/ppermute | solution.py:211
  38.1 0.9 %shard_map.60 = f32[256,512]{1,0:T(8,128)} custom-call(f32[256,256]{1,0:T(8,128)S(1)} %shard_map.57.rest_2_.near, f32[1,256,256]{2,1,0:T(8,128)S(1)} %get-tuple-element.39.keep, bf16[1,256,256]{2,1,0:T(8,128)(2,1)S(1)} %collective-permute-done.11.got), custom_call_target="tpu_custom_call" | custom-call | tf_op jit(solution)/shard_map/pallas_call | solution.py:18
  (19 shorter events, 0.5 us)
Async XLA Ops:
  0.0 5.3 %copy-start = (bf16[2048,2048]{1,0:T(8,128)(2,1)S(1)}, bf16[2048,2048]{1,0:T(8,128)(2,1)}, u32[]{:S(2)}) copy-start(bf16[2048,2048]{1,0:T(8,128)(2,1)} %pool.11) | copy-start | bytes 25165828
  0.0 5.3 %copy-start.1 = (bf16[4,512,512]{2,1,0:T(8,128)(2,1)S(1)}, bf16[4,512,512]{2,1,0:T(8,128)(2,1)}, u32[]{:S(2)}) copy-start(bf16[4,512,512]{2,1,0:T(8,128)(2,1)} %pre.3) | copy-start | bytes 6291460
  0.0 2.3 %collective-permute-start = (bf16[128,2048]{1,0:T(8,128)(2,1)}, bf16[128,2048]{1,0:T(8,128)(2,1)S(1)}, u32[]{:S(2)}, u32[]{:S(2)}) collective-permute-start(bf16[128,2048]{1,0:T(8,128)(2,1)} %target.1), channel_id=1, source_target_pairs={{0,8},{8,0},{16,24},{24,16},{1,9},{9,1},{17,25},{25,17},{2,10},{10... | collective-permute-start | bytes 1572872 | tf_op jit(solution)/shard_map/ppermute | solution.py:186
  2.4 9.6 %collective-permute-start.4 = (bf16[128,1024]{1,0:T(8,128)(2,1)S(1)}, bf16[128,1024]{1,0:T(8,128)(2,1)S(1)}, u32[]{:S(2)}, u32[]{:S(2)}) collective-permute-start(bf16[128,1024]{1,0:T(8,128)(2,1)S(1)} %get-tuple-element.30), channel_id=1, source_target_pairs={{0,16},{8,24},{16,0},{24,8},{1,17},{9,25},{17,1},{25,9},{2,18},{10... | collective-permute-start | bytes 786440 | tf_op jit(solution)/shard_map/ppermute | solution.py:186
  6.3 6.4 %collective-permute-start.2 = (bf16[2,256,256]{2,1,0:T(8,128)(2,1)S(1)}, bf16[2,256,256]{2,1,0:T(8,128)(2,1)S(1)}, u32[]{:S(2)}, u32[]{:S(2)}) collective-permute-start(bf16[2,256,256]{2,1,0:T(8,128)(2,1)S(1)} %get-tuple-element.27.rest_0_), channel_id=1, source_target_pairs={{0,1},{1,0},{2,3},{3,2},{4,5},{5,4},{6,7},{7,6},{8,10},{9,11},{10,... | collective-permute-start | bytes 786440 | tf_op jit(solution)/shard_map/ppermute | solution.py:211
  8.9 8.4 %collective-permute-start.1 = (bf16[2,256,256]{2,1,0:T(8,128)(2,1)S(1)}, bf16[2,256,256]{2,1,0:T(8,128)(2,1)S(1)}, u32[]{:S(2)}, u32[]{:S(2)}) collective-permute-start(bf16[2,256,256]{2,1,0:T(8,128)(2,1)S(1)} %shard_map.49.rest_0_), channel_id=1, source_target_pairs={{0,1},{1,0},{2,3},{3,2},{4,5},{5,4},{6,7},{7,6},{8,10},{9,11},{10,... | collective-permute-start | bytes 786440 | tf_op jit(solution)/shard_map/ppermute | solution.py:211
  12.1 2.7 %collective-permute-start.5 = (bf16[128,512]{1,0:T(8,128)(2,1)S(1)}, bf16[128,512]{1,0:T(8,128)(2,1)S(1)}, u32[]{:S(2)}, u32[]{:S(2)}) collective-permute-start(bf16[128,512]{1,0:T(8,128)(2,1)S(1)} %get-tuple-element.31.rest_0_), channel_id=1, source_target_pairs={{0,8},{8,0},{16,24},{24,16},{1,9},{9,1},{17,25},{25,17},{2,10},{10... | collective-permute-start | bytes 393224 | tf_op jit(solution)/shard_map/ppermute | solution.py:186
  12.2 2.6 %collective-permute-start.6 = (bf16[128,512]{1,0:T(8,128)(2,1)S(1)}, bf16[128,512]{1,0:T(8,128)(2,1)S(1)}, u32[]{:S(2)}, u32[]{:S(2)}) collective-permute-start(bf16[128,512]{1,0:T(8,128)(2,1)S(1)} %get-tuple-element.32.rest_1_), channel_id=1, source_target_pairs={{0,8},{8,0},{16,24},{24,16},{1,9},{9,1},{17,25},{25,17},{2,10},{10... | collective-permute-start | bytes 393224 | tf_op jit(solution)/shard_map/ppermute | solution.py:186
  12.8 7.6 %collective-permute-start.3 = (bf16[2,256,256]{2,1,0:T(8,128)(2,1)S(1)}, bf16[2,256,256]{2,1,0:T(8,128)(2,1)S(1)}, u32[]{:S(2)}, u32[]{:S(2)}) collective-permute-start(bf16[2,256,256]{2,1,0:T(8,128)(2,1)S(1)} %shard_map.51), channel_id=1, source_target_pairs={{0,2},{1,3},{2,0},{3,1},{4,6},{5,7},{6,4},{7,5},{8,9},{9,8},{10,11... | collective-permute-start | bytes 786440 | tf_op jit(solution)/shard_map/ppermute | solution.py:211
  15.8 8.1 %collective-permute-start.9 = (bf16[2,256,256]{2,1,0:T(8,128)(2,1)S(1)}, bf16[2,256,256]{2,1,0:T(8,128)(2,1)S(1)}, u32[]{:S(2)}, u32[]{:S(2)}) collective-permute-start(bf16[2,256,256]{2,1,0:T(8,128)(2,1)S(1)} %get-tuple-element.37.rest_0_), channel_id=1, source_target_pairs={{0,1},{1,0},{2,3},{3,2},{4,5},{5,4},{6,7},{7,6},{8,10},{9,11},{10,... | collective-permute-start | bytes 786440 | tf_op jit(solution)/shard_map/ppermute | solution.py:211
  18.0 9.1 %collective-permute-start.8 = (bf16[2,256,256]{2,1,0:T(8,128)(2,1)S(1)}, bf16[2,256,256]{2,1,0:T(8,128)(2,1)S(1)}, u32[]{:S(2)}, u32[]{:S(2)}) collective-permute-start(bf16[2,256,256]{2,1,0:T(8,128)(2,1)S(1)} %shard_map.56), channel_id=1, source_target_pairs={{0,1},{1,0},{2,3},{3,2},{4,5},{5,4},{6,7},{7,6},{8,10},{9,11},{10,... | collective-permute-start | bytes 786440 | tf_op jit(solution)/shard_map/ppermute | solution.py:211
  20.4 6.7 %collective-permute-start.7 = (bf16[1,256,256]{2,1,0:T(8,128)(2,1)S(1)}, bf16[1,256,256]{2,1,0:T(8,128)(2,1)S(1)}, u32[]{:S(2)}, u32[]{:S(2)}) collective-permute-start(bf16[1,256,256]{2,1,0:T(8,128)(2,1)S(1)} %get-tuple-element.36), channel_id=1, source_target_pairs={{0,4},{1,5},{2,6},{3,7},{4,0},{5,1},{6,2},{7,3},{8,12},{9,13},{10,... | collective-permute-start | bytes 393224 | tf_op jit(solution)/shard_map/ppermute | solution.py:211
  23.9 6.6 %collective-permute-start.10 = (bf16[2,256,256]{2,1,0:T(8,128)(2,1)S(1)}, bf16[2,256,256]{2,1,0:T(8,128)(2,1)S(1)}, u32[]{:S(2)}, u32[]{:S(2)}) collective-permute-start(bf16[2,256,256]{2,1,0:T(8,128)(2,1)S(1)} %shard_map.58), channel_id=1, source_target_pairs={{0,2},{1,3},{2,0},{3,1},{4,6},{5,7},{6,4},{7,5},{8,9},{9,8},{10,11... | collective-permute-start | bytes 786440 | tf_op jit(solution)/shard_map/ppermute | solution.py:211
  30.5 7.6 %collective-permute-start.11 = (bf16[1,256,256]{2,1,0:T(8,128)(2,1)S(1)}, bf16[1,256,256]{2,1,0:T(8,128)(2,1)S(1)}, u32[]{:S(2)}, u32[]{:S(2)}) collective-permute-start(bf16[1,256,256]{2,1,0:T(8,128)(2,1)S(1)} %get-tuple-element.40), channel_id=1, source_target_pairs={{0,4},{1,5},{2,6},{3,7},{4,0},{5,1},{6,2},{7,3},{8,12},{9,13},{10,... | collective-permute-start | bytes 393224 | tf_op jit(solution)/shard_map/ppermute | solution.py:211

commit v5 on v4

--- a/solution.py
+++ b/solution.py
@@ -48,21 +48,21 @@
     return copies
 
 
-def order_of(parts, core):
+def order_of(parts, far, core):
     bits = list(range(parts.bit_length() - 1))
-    return ([0, 1, 2] if core == 0 else [1, 0, 2]) + bits[3:]
+    return [[[0, 1, 2], [1, 0, 2]], [[0, 1, 2], [1, 0, 2]]][far][core] + bits[3:]
 
 
 def pick(core, values):
     return jnp.where(core == 1, values[1], values[0])
 
 
-def row_block(parts, group, n):
+def row_block(parts, group, far, n):
     j, panel = place(group)
     away, away2, i = n < parts // 2, n % (parts // 2) < parts // 4, n % (parts // 4)
     at = []
     for core in range(2):
-        first, second, *left = order_of(parts, core)
+        first, second, *left = order_of(parts, far, core)
         value = (((j >> first) & 1) ^ away) << first | (((j >> second) & 1) ^ away2) << second
         for t, bit in enumerate(sorted(left)):
             value = value | ((i >> t) & 1) << bit
@@ -111,7 +111,7 @@
 def near_send_kernel(parts, group, scale, pool, evens, rows, pre, right, send):
     bs = pre.shape[1]
     condition(scale, pre, evens[: pre.shape[0], :], lambda b: rows[:, b * bs : (b + 1) * bs], right)
-    scores(parts, group, 0, pool, right, send)
+    scores(parts, group, 0, 0, pool, right, send)
 
 
 def far_send_kernel(parts, group, scale, pool, evens, pre, *rest):
@@ -124,36 +124,44 @@
         return jnp.where(core == b // depth, rest[b % depth][...], rest[depth + b % depth][...])
 
     condition(scale, pre, evens[blocks : 2 * blocks, :], rows_at, right)
-    scores(parts, group, 0, pool, right, send)
-
-
-def scores(parts, group, quarter, pool, right, out):
+    scores(parts, group, 1, 0, pool, right, send)
+
+
+def scores(parts, group, far, quarter, pool, right, out):
     count, rows = out.shape[:2]
     for n in range(count):
-        start = pl.multiple_of(row_block(parts, group, quarter * count + n) * rows, rows)
+        start = pl.multiple_of(row_block(parts, group, far, quarter * count + n) * rows, rows)
         value = jnp.dot(pool[pl.ds(start, rows), :], right[...], preferred_element_type=F32)
         out[n] = value.astype(out.dtype)
 
 
-def scores_kernel(parts, group, quarters, pool, right, *rest):
+def scores_kernel(parts, group, far, quarters, pool, right, *rest):
     for quarter, out in zip(quarters, rest[-len(quarters) :]):
-        scores(parts, group, quarter, pool, right, out)
+        scores(parts, group, far, quarter, pool, right, out)
 
 
 def add_kernel(keep, got, *rest):
     rest[-1][...] = (keep[...] + got[...].astype(F32)).astype(BF16)
 
 
-def halve_kernel(parts, group, step, gots, keep, *rest):
+def add_two_kernel(keep, got, *rest):
+    for n, out in enumerate(rest[-2:]):
+        columns = slice(n * PROWS, (n + 1) * PROWS)
+        out[...] = (keep[:, :, columns] + got[:, :, columns].astype(F32)).astype(BF16)
+
+
+def halve_kernel(parts, group, far, step, gots, begin, keep, *rest):
     send, home = rest[-2:]
     j, panel = place(group)
-    bits = [sorted(order_of(parts, core)[2:])[step - 2] for core in range(2)]
+    bits = [sorted(order_of(parts, far, core)[2:])[step - 2] for core in range(2)]
     value = (j >> pick(panel & 1, bits)) & 1
     for i in range(send.shape[0]):
         for out, at in ((send, 2 * i + 1 - value), (home, 2 * i + value)):
-            total = keep[at]
+            width = out.shape[2]
+            total = keep[at, :, begin : begin + width]
             for got in rest[:gots]:
-                total = total + got[at].astype(F32)
+                start = begin if got.shape[2] > width else 0
+                total = total + got[at, :, start : start + width].astype(F32)
             out[i] = total.astype(out.dtype)
 
 
@@ -161,12 +169,15 @@
     rest[-1][...] = keep[0] + got[0].astype(F32)
 
 
-def last_kernel(group, near, keep, got, out):
+def last_kernel(group, near, keep, got, keep2, got2, out):
     pair = place(group)[1] >> 1
     width = near.shape[1]
-    far = keep[0] + got[0].astype(F32)
-    out[:, :width] = jnp.where(pair == 1, far, near[...])
-    out[:, width:] = jnp.where(pair == 1, near[...], far)
+    out[:, :width] = near[...]
+    out[:, width:] = near[...]
+    start = pl.multiple_of((1 - pair) * width, width)
+    half = keep.shape[2]
+    out[:, pl.ds(start, half)] = keep[0] + got[0].astype(F32)
+    out[:, pl.ds(pl.multiple_of(start + half, half), half)] = keep2[0] + got2[0].astype(F32)
 
 
 def local(tgt_size, pool_size, pool, target, pre, active):
@@ -202,10 +213,10 @@
     right_out = ((k, 2 * PROWS), BF16)
     flops = 30 * m * k * PROWS
 
-    def exchange(x, step):
+    def exchange(x, step, far):
         pairs = []
         for p in range(pool_size):
-            bit = order_of(parts, (p // group) & 1)
+            bit = order_of(parts, far, (p // group) & 1)
             bit = bit[step] if step < 2 else sorted(bit[2:])[step - 2]
             pairs += [(p * parts + j, p * parts + (j ^ (1 << bit))) for j in range(parts)]
         return lax.ppermute(x, ("pool", "tgt"), pairs)
@@ -213,15 +224,15 @@
     def add(keep, got, *others):
         return call(add_kernel, [(shape, BF16)], keep, got, *others)[0]
 
-    def rest(keep, gots, *others):
+    def rest(far, keep, gots, *others, begin=0, width=2 * PROWS):
         step = 2
         while True:
-            half_shape = (keep.shape[0] // 2,) + keep.shape[1:]
+            half_shape = (keep.shape[0] // 2, keep.shape[1], width)
             send, keep = call(
-                functools.partial(halve_kernel, parts, group, step, len(gots)),
+                functools.partial(halve_kernel, parts, group, far, step, len(gots), begin),
                 [(half_shape, BF16), (half_shape, F32)], keep, *gots, *others,
             )
-            others, gots = (), [exchange(send, step)]
+            others, gots, begin = (), [exchange(send, step, far)], 0
             step += 1
             if keep.shape[0] == 1:
                 return keep, gots[0]
@@ -230,15 +241,15 @@
         functools.partial(near_send_kernel, parts, group, scale), [right_out, (shape, BF16)],
         pool, evens, rows, pre, flops=0,
     )
-    got = exchange(send, 0)
-
-    def more(quarters, dtype, right, *others, flops=0):
-        body = functools.partial(scores_kernel, parts, group, quarters)
+    got = exchange(send, 0, 0)
+
+    def more(far, quarters, dtype, right, *others, flops=0):
+        body = functools.partial(scores_kernel, parts, group, far, quarters)
         return call(body, [(shape, dtype)] * len(quarters), pool, right, *others, flops=flops)
 
-    send2 = more([1], BF16, right, send, flops=0)[0]
-    got2 = exchange(send2, 0)
-    keep, keep2 = more([2, 3], F32, right, send2, flops=0)
+    send2 = more(0, [1], BF16, right, send, flops=0)[0]
+    got2 = exchange(send2, 0, 0)
+    keep, keep2 = more(0, [2, 3], F32, right, send2, flops=0)
     near_next = add(keep, got)
     mine = split_after(mine, blocks // 2, keep, flops=0)
     other = [swap(piece, "pool", group) for piece in mine]
@@ -246,16 +257,18 @@
         functools.partial(far_send_kernel, parts, group, scale), [right_out, (shape, BF16)],
         pool, evens, pre, *mine, *other, flops=0,
     )
-    far_got = exchange(far_send, 0)
-    far_send2 = more([1], BF16, right, far_send, got2)[0]
-    far_got2 = exchange(far_send2, 0)
-    got3 = exchange(near_next, 1)
-    far_keep, far_keep2 = more([2, 3], F32, right, flops=0)
-    near = rest(keep2, [got2, got3], far_keep)
+    far_got = exchange(far_send, 0, 1)
+    far_send2 = more(1, [1], BF16, right, far_send, got2)[0]
+    far_got2 = exchange(far_send2, 0, 1)
+    got3 = exchange(near_next, 1, 0)
+    far_keep, far_keep2 = more(1, [2, 3], F32, right, flops=0)
+    near = rest(0, keep2, [got2, got3], far_keep)
     near_total = call(total_kernel, [((part, 2 * PROWS), F32)], *near, far_got2, flops=10**11)[0]
-    far_next = add(far_keep, far_got, near[0])
-    far_got3 = exchange(far_next, 1)
-    far = rest(far_keep2, [far_got2, far_got3], near_total)
+    far = []
+    narrow = (shape[0], shape[1], PROWS)
+    for begin, far_next in zip((0, PROWS), call(add_two_kernel, [(narrow, BF16)] * 2, far_keep, far_got, near[0])):
+        gots = [far_got2, exchange(far_next, 1, 1)]
+        far += rest(1, far_keep2, gots, near_total, begin=begin, width=PROWS)
     out = ((part, 4 * PROWS), F32)
     return call(functools.partial(last_kernel, group), [out], near_total, *far, kind=jax.ShapeDtypeStruct)[0]
 

time: 39.1 us -> 38.6 us (0.987)
  waiting for transfers between devices: 11.8 us -> 9.35 us
  starting transfers between devices: 18.1 us -> 20 us
    ppermute x8 -> x10, waiting for transfers between devices: 10.1 us -> 7.66 us  [exchange(): return lax.ppermute(x, ('pool', 'tgt'), pairs)]
    ppermute x8 -> x10, starting transfers between devices: 14.3 us -> 16.1 us  [exchange(): return lax.ppermute(x, ('pool', 'tgt'), pairs)]
    pallas_call x15 -> x16, Pallas kernels: 8.95 us -> 8.96 us  [call(): pl.pallas_call(body, in_specs=specs, out_specs=[VMEM] * len(outs), out_sh...]
  transfers between devices with their start and end apart: 12 -> 14, of which waited for: 5 -> 6; matrix products, arithmetic and copies ran while one was open for 0% -> 0% of each run, Pallas kernels for 20% -> 21%
where the time goes in v5:
time: 38.6 us; the launch traced here: 38.4 us
  starting transfers between devices  20 us (52%)
  waiting for transfers between devices  9.35 us (24%)
  Pallas kernels  8.96 us (23%)
    ppermute x10, starting transfers between devices, exchange(): return lax.ppermute(x, ('pool', 'tgt'), pairs)  16.1 us
    pallas_call x16, Pallas kernels, call(): pl.pallas_call(body, in_specs=specs, out_specs=[VMEM] * len(outs), out_sh...  8.96 us
    ppermute x10, waiting for transfers between devices, exchange(): return lax.ppermute(x, ('pool', 'tgt'), pairs)  7.66 us
    ppermute x4, starting transfers between devices, swap(): return lax.ppermute(x, axis, [(i, i ^ step) for i in range(size)])  3.87 us
    ppermute x4, waiting for transfers between devices, swap(): return lax.ppermute(x, axis, [(i, i ^ step) for i in range(size)])  1.69 us
  transfers between devices with their start and end apart: 14, of which 6 were waited for; matrix products, arithmetic and copies ran while one was open for 0% of the time, Pallas kernels for 21%

profile of v5, /device:TPU:0, one launch (start us, length us, event | category | flops | bytes accessed | tf_op | source)
XLA Modules:
  0.0 38.4 jit_solution(2373708366904619421)
XLA Ops:
  0.5 1.8 %shard_map.46 = (s32[4,16]{1,0:T(4,128)}, bf16[128,2048]{1,0:T(8,128)(2,1)S(1)}, s32[8,512]{1,0:T(8,128)S(1)}) custom-call(s32[4,16]{1,0:T(4,128)} %active.1, bf16[128,2048]{1,0:T(8,128)(2,1)} %target.1), custom_call_target="tpu_custom_call" | custom-call | flops 5000000000 | tf_op jit(solution)/shard_map/pallas_call | solution.py:18
  2.4 2.8 %collective-permute-start.4 = (bf16[128,1024]{1,0:T(8,128)(2,1)S(1)}, bf16[128,1024]{1,0:T(8,128)(2,1)S(1)}, u32[]{:S(2)}, u32[]{:S(2)}) collective-permute-start(bf16[128,1024]{1,0:T(8,128)(2,1)S(1)} %get-tuple-element.34), channel_id=1, source_target_pairs={{0,16},{8,24},{16,0},{24,8},{1,17},{9,25},{17,1},{25,9},{2,18},{10... | collective-permute-start | bytes 786440 | tf_op jit(solution)/shard_map/ppermute | solution.py:197
  5.3 1.0 %shard_map.48 = (bf16[2048,256]{1,0:T(8,128)(2,1)S(1)}, bf16[2,256,256]{2,1,0:T(8,128)(2,1)S(1)}) custom-call(bf16[2048,2048]{1,0:T(8,128)(2,1)S(1)} %copy-done, s32[8,512]{1,0:T(8,128)S(1)} %get-tuple-element.27.evens, bf16[128,2048]{1,0:T(8,128)(2,1)S(1)} %get-tuple-element.29.rows, bf16[4,512,512]{2,1,0:T(8,128)(2,1)S(1)} %copy-done.1), custom_call_target="tpu_custom_call" | custom-call | tf_op jit(solution)/shard_map/pallas_call | solution.py:18
  6.3 1.9 %collective-permute-start.2 = (bf16[2,256,256]{2,1,0:T(8,128)(2,1)S(1)}, bf16[2,256,256]{2,1,0:T(8,128)(2,1)S(1)}, u32[]{:S(2)}, u32[]{:S(2)}) collective-permute-start(bf16[2,256,256]{2,1,0:T(8,128)(2,1)S(1)} %get-tuple-element.31.rest_0_), channel_id=1, source_target_pairs={{0,1},{1,0},{2,3},{3,2},{4,5},{5,4},{6,7},{7,6},{8,10},{9,11},{10,... | collective-permute-start | bytes 786440 | tf_op jit(solution)/shard_map/ppermute | solution.py:222
  8.2 0.7 %shard_map.49.rest_0_ = bf16[2,256,256]{2,1,0:T(8,128)(2,1)S(1)} custom-call(bf16[2048,2048]{1,0:T(8,128)(2,1)S(1)} %copy-done, bf16[2048,256]{1,0:T(8,128)(2,1)S(1)} %get-tuple-element.30.right, bf16[2,256,256]{2,1,0:T(8,128)(2,1)S(1)} %get-tuple-element.31.rest_0_), custom_call_target="tpu_custom_call" | custom-call | tf_op jit(solution)/shard_map/pallas_call | solution.py:18
  9.1 1.2 %shard_map.50 = (f32[2,256,256]{2,1,0:T(8,128)S(1)}, f32[2,256,256]{2,1,0:T(8,128)S(1)}) custom-call(bf16[2048,2048]{1,0:T(8,128)(2,1)S(1)} %copy-done, bf16[2048,256]{1,0:T(8,128)(2,1)S(1)} %get-tuple-element.30.right, bf16[2,256,256]{2,1,0:T(8,128)(2,1)S(1)} %shard_map.49.rest_0_), custom_call_target="tpu_custom_call" | custom-call | tf_op jit(solution)/shard_map/pallas_call | solution.py:18
  10.4 1.7 %collective-permute-done.4.x = bf16[128,1024]{1,0:T(8,128)(2,1)S(1)} collective-permute-done((bf16[128,1024]{1,0:T(8,128)(2,1)S(1)}, bf16[128,1024]{1,0:T(8,128)(2,1)S(1)}, u32[]{:S(2)}, u32[]{:S(2)}) %collective-permute-start.4) | collective-permute-done | bytes 262176 | tf_op jit(solution)/shard_map/ppermute | solution.py:197
  12.2 0.5 %collective-permute-start.6 = (bf16[128,512]{1,0:T(8,128)(2,1)S(1)}, bf16[128,512]{1,0:T(8,128)(2,1)S(1)}, u32[]{:S(2)}, u32[]{:S(2)}) collective-permute-start(bf16[128,512]{1,0:T(8,128)(2,1)S(1)} %get-tuple-element.36.rest_1_), channel_id=1, source_target_pairs={{0,8},{8,0},{16,24},{24,16},{1,9},{9,1},{17,25},{25,17},{2,10},{10... | collective-permute-start | bytes 393224 | tf_op jit(solution)/shard_map/ppermute | solution.py:197
  12.8 2.0 %collective-permute-start.3 = (bf16[2,256,256]{2,1,0:T(8,128)(2,1)S(1)}, bf16[2,256,256]{2,1,0:T(8,128)(2,1)S(1)}, u32[]{:S(2)}, u32[]{:S(2)}) collective-permute-start(bf16[2,256,256]{2,1,0:T(8,128)(2,1)S(1)} %shard_map.51), channel_id=1, source_target_pairs={{0,2},{1,3},{2,0},{3,1},{4,6},{5,7},{6,4},{7,5},{8,9},{9,8},{10,11... | collective-permute-start | bytes 786440 | tf_op jit(solution)/shard_map/ppermute | solution.py:222
  14.7 1.0 %shard_map.53 = (bf16[2048,256]{1,0:T(8,128)(2,1)S(1)}, bf16[2,256,256]{2,1,0:T(8,128)(2,1)S(1)}) custom-call(bf16[2048,2048]{1,0:T(8,128)(2,1)S(1)} %copy-done, s32[8,512]{1,0:T(8,128)S(1)} %get-tuple-element.27.evens, bf16[4,512,512]{2,1,0:T(8,128)(2,1)S(1)} %copy-done.1, bf16[128,512]{1,0:T(8,128)(2,1)S(1)} %get-tuple-element.35.rest_0_, ...), custom_call_target="tpu_custom_call" | custom-call | tf_op jit(solution)/shard_map/pallas_call | solution.py:18
  15.8 1.6 %collective-permute-start.9 = (bf16[2,256,256]{2,1,0:T(8,128)(2,1)S(1)}, bf16[2,256,256]{2,1,0:T(8,128)(2,1)S(1)}, u32[]{:S(2)}, u32[]{:S(2)}) collective-permute-start(bf16[2,256,256]{2,1,0:T(8,128)(2,1)S(1)} %get-tuple-element.41.rest_0_), channel_id=1, source_target_pairs={{0,1},{1,0},{2,3},{3,2},{4,5},{5,4},{6,7},{7,6},{8,10},{9,11},{10,... | collective-permute-start | bytes 786440 | tf_op jit(solution)/shard_map/ppermute | solution.py:222
  17.3 0.7 %shard_map.56 = bf16[2,256,256]{2,1,0:T(8,128)(2,1)S(1)} custom-call(bf16[2048,2048]{1,0:T(8,128)(2,1)S(1)} %copy-done, bf16[2048,256]{1,0:T(8,128)(2,1)S(1)} %get-tuple-element.37.right, bf16[2,256,256]{2,1,0:T(8,128)(2,1)S(1)} %get-tuple-element.41.rest_0_, bf16[2,256,256]{2,1,0:T(8,128)(2,1)S(1)} %collective-permute-done.1.rest_0_.rest_1_), custom_call_target="tpu_custom_call" | custom-call | tf_op jit(solution)/shard_map/pallas_call | solution.py:18
  18.0 0.6 %collective-permute-start.8 = (bf16[2,256,256]{2,1,0:T(8,128)(2,1)S(1)}, bf16[2,256,256]{2,1,0:T(8,128)(2,1)S(1)}, u32[]{:S(2)}, u32[]{:S(2)}) collective-permute-start(bf16[2,256,256]{2,1,0:T(8,128)(2,1)S(1)} %shard_map.56), channel_id=1, source_target_pairs={{0,1},{1,0},{2,3},{3,2},{4,5},{5,4},{6,7},{7,6},{8,10},{9,11},{10,... | collective-permute-start | bytes 786440 | tf_op jit(solution)/shard_map/ppermute | solution.py:222
  18.6 1.2 %shard_map.54 = (f32[2,256,256]{2,1,0:T(8,128)S(1)}, f32[2,256,256]{2,1,0:T(8,128)S(1)}) custom-call(bf16[2048,2048]{1,0:T(8,128)(2,1)S(1)} %copy-done, bf16[2048,256]{1,0:T(8,128)(2,1)S(1)} %get-tuple-element.37.right), custom_call_target="tpu_custom_call" | custom-call | tf_op jit(solution)/shard_map/pallas_call | solution.py:18
  19.9 0.5 %collective-permute-done.3.rest_1_ = bf16[2,256,256]{2,1,0:T(8,128)(2,1)S(1)} collective-permute-done((bf16[2,256,256]{2,1,0:T(8,128)(2,1)S(1)}, bf16[2,256,256]{2,1,0:T(8,128)(2,1)S(1)}, u32[]{:S(2)}, u32[]{:S(2)}) %collective-permute-start.3) | collective-permute-done | bytes 262176 | tf_op jit(solution)/shard_map/ppermute | solution.py:222
  20.4 3.4 %collective-permute-start.7 = (bf16[1,256,256]{2,1,0:T(8,128)(2,1)S(1)}, bf16[1,256,256]{2,1,0:T(8,128)(2,1)S(1)}, u32[]{:S(2)}, u32[]{:S(2)}) collective-permute-start(bf16[1,256,256]{2,1,0:T(8,128)(2,1)S(1)} %get-tuple-element.40), channel_id=1, source_target_pairs={{0,4},{1,5},{2,6},{3,7},{4,0},{5,1},{6,2},{7,3},{8,12},{9,13},{10,... | collective-permute-start | bytes 393224 | tf_op jit(solution)/shard_map/ppermute | solution.py:222
  23.9 1.6 %collective-permute-start.10 = (bf16[2,256,128]{2,1,0:T(8,128)(2,1)S(1)}, bf16[2,256,128]{2,1,0:T(8,128)(2,1)S(1)}, u32[]{:S(2)}, u32[]{:S(2)}) collective-permute-start(bf16[2,256,128]{2,1,0:T(8,128)(2,1)S(1)} %get-tuple-element.43), channel_id=1, source_target_pairs={{0,2},{1,3},{2,0},{3,1},{4,6},{5,7},{6,4},{7,5},{8,9},{9,8},{10,11... | collective-permute-start | bytes 393224 | tf_op jit(solution)/shard_map/ppermute | solution.py:222
  26.0 1.1 %collective-permute-done.7.got = bf16[1,256,256]{2,1,0:T(8,128)(2,1)S(1)} collective-permute-done((bf16[1,256,256]{2,1,0:T(8,128)(2,1)S(1)}, bf16[1,256,256]{2,1,0:T(8,128)(2,1)S(1)}, u32[]{:S(2)}, u32[]{:S(2)}) %collective-permute-start.7) | collective-permute-done | bytes 131104 | tf_op jit(solution)/shard_map/ppermute | solution.py:222
  27.1 1.9 %collective-permute-done.10.rest_1_ = bf16[2,256,128]{2,1,0:T(8,128)(2,1)S(1)} collective-permute-done((bf16[2,256,128]{2,1,0:T(8,128)(2,1)S(1)}, bf16[2,256,128]{2,1,0:T(8,128)(2,1)S(1)}, u32[]{:S(2)}, u32[]{:S(2)}) %collective-permute-start.10) | collective-permute-done | bytes 131104 | tf_op jit(solution)/shard_map/ppermute | solution.py:222
  29.1 3.0 %collective-permute-start.11 = (bf16[1,256,128]{2,1,0:T(8,128)(2,1)S(1)}, bf16[1,256,128]{2,1,0:T(8,128)(2,1)S(1)}, u32[]{:S(2)}, u32[]{:S(2)}) collective-permute-start(bf16[1,256,128]{2,1,0:T(8,128)(2,1)S(1)} %get-tuple-element.45), channel_id=1, source_target_pairs={{0,4},{1,5},{2,6},{3,7},{4,0},{5,1},{6,2},{7,3},{8,12},{9,13},{10,... | collective-permute-start | bytes 196616 | tf_op jit(solution)/shard_map/ppermute | solution.py:222
  32.1 1.4 %collective-permute-start.13 = (bf16[1,256,128]{2,1,0:T(8,128)(2,1)S(1)}, bf16[1,256,128]{2,1,0:T(8,128)(2,1)S(1)}, u32[]{:S(2)}, u32[]{:S(2)}) collective-permute-start(bf16[1,256,128]{2,1,0:T(8,128)(2,1)S(1)} %get-tuple-element.48), channel_id=1, source_target_pairs={{0,4},{1,5},{2,6},{3,7},{4,0},{5,1},{6,2},{7,3},{8,12},{9,13},{10,... | collective-permute-start | bytes 196616 | tf_op jit(solution)/shard_map/ppermute | solution.py:222
  33.5 3.4 %collective-permute-done.11.got = bf16[1,256,128]{2,1,0:T(8,128)(2,1)S(1)} collective-permute-done((bf16[1,256,128]{2,1,0:T(8,128)(2,1)S(1)}, bf16[1,256,128]{2,1,0:T(8,128)(2,1)S(1)}, u32[]{:S(2)}, u32[]{:S(2)}) %collective-permute-start.11) | collective-permute-done | bytes 65568 | tf_op jit(solution)/shard_map/ppermute | solution.py:222
  36.8 0.7 %collective-permute-done.13.got2 = bf16[1,256,128]{2,1,0:T(8,128)(2,1)S(1)} collective-permute-done((bf16[1,256,128]{2,1,0:T(8,128)(2,1)S(1)}, bf16[1,256,128]{2,1,0:T(8,128)(2,1)S(1)}, u32[]{:S(2)}, u32[]{:S(2)}) %collective-permute-start.13) | collective-permute-done | bytes 65568 | tf_op jit(solution)/shard_map/ppermute | solution.py:222
  37.5 0.9 %shard_map.61 = f32[256,512]{1,0:T(8,128)} custom-call(f32[256,256]{1,0:T(8,128)S(1)} %shard_map.57.rest_2_.near, f32[1,256,128]{2,1,0:T(8,128)S(1)} %get-tuple-element.44.keep, bf16[1,256,128]{2,1,0:T(8,128)(2,1)S(1)} %collective-permute-done.11.got, f32[1,256,128]{2,1,0:T(8,128)S(1)} %get-tuple-element.47.keep2, ...), custom_call_target="tpu_custom_call" | custom-call | tf_op jit(solution)/shard_map/pallas_call | solution.py:18
  (24 shorter events, 1.7 us)
Async XLA Ops:
  0.0 5.3 %copy-start = (bf16[2048,2048]{1,0:T(8,128)(2,1)S(1)}, bf16[2048,2048]{1,0:T(8,128)(2,1)}, u32[]{:S(2)}) copy-start(bf16[2048,2048]{1,0:T(8,128)(2,1)} %pool.11) | copy-start | bytes 25165828
  0.0 5.3 %copy-start.1 = (bf16[4,512,512]{2,1,0:T(8,128)(2,1)S(1)}, bf16[4,512,512]{2,1,0:T(8,128)(2,1)}, u32[]{:S(2)}) copy-start(bf16[4,512,512]{2,1,0:T(8,128)(2,1)} %pre.3) | copy-start | bytes 6291460
  0.0 2.3 %collective-permute-start = (bf16[128,2048]{1,0:T(8,128)(2,1)}, bf16[128,2048]{1,0:T(8,128)(2,1)S(1)}, u32[]{:S(2)}, u32[]{:S(2)}) collective-permute-start(bf16[128,2048]{1,0:T(8,128)(2,1)} %target.1), channel_id=1, source_target_pairs={{0,8},{8,0},{16,24},{24,16},{1,9},{9,1},{17,25},{25,17},{2,10},{10... | collective-permute-start | bytes 1572872 | tf_op jit(solution)/shard_map/ppermute | solution.py:197
  2.4 9.6 %collective-permute-start.4 = (bf16[128,1024]{1,0:T(8,128)(2,1)S(1)}, bf16[128,1024]{1,0:T(8,128)(2,1)S(1)}, u32[]{:S(2)}, u32[]{:S(2)}) collective-permute-start(bf16[128,1024]{1,0:T(8,128)(2,1)S(1)} %get-tuple-element.34), channel_id=1, source_target_pairs={{0,16},{8,24},{16,0},{24,8},{1,17},{9,25},{17,1},{25,9},{2,18},{10... | collective-permute-start | bytes 786440 | tf_op jit(solution)/shard_map/ppermute | solution.py:197
  6.3 6.4 %collective-permute-start.2 = (bf16[2,256,256]{2,1,0:T(8,128)(2,1)S(1)}, bf16[2,256,256]{2,1,0:T(8,128)(2,1)S(1)}, u32[]{:S(2)}, u32[]{:S(2)}) collective-permute-start(bf16[2,256,256]{2,1,0:T(8,128)(2,1)S(1)} %get-tuple-element.31.rest_0_), channel_id=1, source_target_pairs={{0,1},{1,0},{2,3},{3,2},{4,5},{5,4},{6,7},{7,6},{8,10},{9,11},{10,... | collective-permute-start | bytes 786440 | tf_op jit(solution)/shard_map/ppermute | solution.py:222
  8.9 8.4 %collective-permute-start.1 = (bf16[2,256,256]{2,1,0:T(8,128)(2,1)S(1)}, bf16[2,256,256]{2,1,0:T(8,128)(2,1)S(1)}, u32[]{:S(2)}, u32[]{:S(2)}) collective-permute-start(bf16[2,256,256]{2,1,0:T(8,128)(2,1)S(1)} %shard_map.49.rest_0_), channel_id=1, source_target_pairs={{0,1},{1,0},{2,3},{3,2},{4,5},{5,4},{6,7},{7,6},{8,10},{9,11},{10,... | collective-permute-start | bytes 786440 | tf_op jit(solution)/shard_map/ppermute | solution.py:222
  12.1 2.7 %collective-permute-start.5 = (bf16[128,512]{1,0:T(8,128)(2,1)S(1)}, bf16[128,512]{1,0:T(8,128)(2,1)S(1)}, u32[]{:S(2)}, u32[]{:S(2)}) collective-permute-start(bf16[128,512]{1,0:T(8,128)(2,1)S(1)} %get-tuple-element.35.rest_0_), channel_id=1, source_target_pairs={{0,8},{8,0},{16,24},{24,16},{1,9},{9,1},{17,25},{25,17},{2,10},{10... | collective-permute-start | bytes 393224 | tf_op jit(solution)/shard_map/ppermute | solution.py:197
  12.2 2.6 %collective-permute-start.6 = (bf16[128,512]{1,0:T(8,128)(2,1)S(1)}, bf16[128,512]{1,0:T(8,128)(2,1)S(1)}, u32[]{:S(2)}, u32[]{:S(2)}) collective-permute-start(bf16[128,512]{1,0:T(8,128)(2,1)S(1)} %get-tuple-element.36.rest_1_), channel_id=1, source_target_pairs={{0,8},{8,0},{16,24},{24,16},{1,9},{9,1},{17,25},{25,17},{2,10},{10... | collective-permute-start | bytes 393224 | tf_op jit(solution)/shard_map/ppermute | solution.py:197
  12.8 7.6 %collective-permute-start.3 = (bf16[2,256,256]{2,1,0:T(8,128)(2,1)S(1)}, bf16[2,256,256]{2,1,0:T(8,128)(2,1)S(1)}, u32[]{:S(2)}, u32[]{:S(2)}) collective-permute-start(bf16[2,256,256]{2,1,0:T(8,128)(2,1)S(1)} %shard_map.51), channel_id=1, source_target_pairs={{0,2},{1,3},{2,0},{3,1},{4,6},{5,7},{6,4},{7,5},{8,9},{9,8},{10,11... | collective-permute-start | bytes 786440 | tf_op jit(solution)/shard_map/ppermute | solution.py:222
  15.8 8.1 %collective-permute-start.9 = (bf16[2,256,256]{2,1,0:T(8,128)(2,1)S(1)}, bf16[2,256,256]{2,1,0:T(8,128)(2,1)S(1)}, u32[]{:S(2)}, u32[]{:S(2)}) collective-permute-start(bf16[2,256,256]{2,1,0:T(8,128)(2,1)S(1)} %get-tuple-element.41.rest_0_), channel_id=1, source_target_pairs={{0,1},{1,0},{2,3},{3,2},{4,5},{5,4},{6,7},{7,6},{8,10},{9,11},{10,... | collective-permute-start | bytes 786440 | tf_op jit(solution)/shard_map/ppermute | solution.py:222
  18.0 9.1 %collective-permute-start.8 = (bf16[2,256,256]{2,1,0:T(8,128)(2,1)S(1)}, bf16[2,256,256]{2,1,0:T(8,128)(2,1)S(1)}, u32[]{:S(2)}, u32[]{:S(2)}) collective-permute-start(bf16[2,256,256]{2,1,0:T(8,128)(2,1)S(1)} %shard_map.56), channel_id=1, source_target_pairs={{0,1},{1,0},{2,3},{3,2},{4,5},{5,4},{6,7},{7,6},{8,10},{9,11},{10,... | collective-permute-start | bytes 786440 | tf_op jit(solution)/shard_map/ppermute | solution.py:222
  20.4 6.7 %collective-permute-start.7 = (bf16[1,256,256]{2,1,0:T(8,128)(2,1)S(1)}, bf16[1,256,256]{2,1,0:T(8,128)(2,1)S(1)}, u32[]{:S(2)}, u32[]{:S(2)}) collective-permute-start(bf16[1,256,256]{2,1,0:T(8,128)(2,1)S(1)} %get-tuple-element.40), channel_id=1, source_target_pairs={{0,4},{1,5},{2,6},{3,7},{4,0},{5,1},{6,2},{7,3},{8,12},{9,13},{10,... | collective-permute-start | bytes 393224 | tf_op jit(solution)/shard_map/ppermute | solution.py:222
  23.9 5.2 %collective-permute-start.10 = (bf16[2,256,128]{2,1,0:T(8,128)(2,1)S(1)}, bf16[2,256,128]{2,1,0:T(8,128)(2,1)S(1)}, u32[]{:S(2)}, u32[]{:S(2)}) collective-permute-start(bf16[2,256,128]{2,1,0:T(8,128)(2,1)S(1)} %get-tuple-element.43), channel_id=1, source_target_pairs={{0,2},{1,3},{2,0},{3,1},{4,6},{5,7},{6,4},{7,5},{8,9},{9,8},{10,11... | collective-permute-start | bytes 393224 | tf_op jit(solution)/shard_map/ppermute | solution.py:222
  25.5 6.6 %collective-permute-start.12 = (bf16[2,256,128]{2,1,0:T(8,128)(2,1)S(1)}, bf16[2,256,128]{2,1,0:T(8,128)(2,1)S(1)}, u32[]{:S(2)}, u32[]{:S(2)}) collective-permute-start(bf16[2,256,128]{2,1,0:T(8,128)(2,1)S(1)} %get-tuple-element.46), channel_id=1, source_target_pairs={{0,2},{1,3},{2,0},{3,1},{4,6},{5,7},{6,4},{7,5},{8,9},{9,8},{10,11... | collective-permute-start | bytes 393224 | tf_op jit(solution)/shard_map/ppermute | solution.py:222
  29.1 7.8 %collective-permute-start.11 = (bf16[1,256,128]{2,1,0:T(8,128)(2,1)S(1)}, bf16[1,256,128]{2,1,0:T(8,128)(2,1)S(1)}, u32[]{:S(2)}, u32[]{:S(2)}) collective-permute-start(bf16[1,256,128]{2,1,0:T(8,128)(2,1)S(1)} %get-tuple-element.45), channel_id=1, source_target_pairs={{0,4},{1,5},{2,6},{3,7},{4,0},{5,1},{6,2},{7,3},{8,12},{9,13},{10,... | collective-permute-start | bytes 196616 | tf_op jit(solution)/shard_map/ppermute | solution.py:222
  32.1 5.4 %collective-permute-start.13 = (bf16[1,256,128]{2,1,0:T(8,128)(2,1)S(1)}, bf16[1,256,128]{2,1,0:T(8,128)(2,1)S(1)}, u32[]{:S(2)}, u32[]{:S(2)}) collective-permute-start(bf16[1,256,128]{2,1,0:T(8,128)(2,1)S(1)} %get-tuple-element.48), channel_id=1, source_target_pairs={{0,4},{1,5},{2,6},{3,7},{4,0},{5,1},{6,2},{7,3},{8,12},{9,13},{10,... | collective-permute-start | bytes 196616 | tf_op jit(solution)/shard_map/ppermute | solution.py:222

commit v6 on v5

--- a/solution.py
+++ b/solution.py
@@ -171,13 +171,25 @@
 
 def last_kernel(group, near, keep, got, keep2, got2, out):
     pair = place(group)[1] >> 1
-    width = near.shape[1]
-    out[:, :width] = near[...]
-    out[:, width:] = near[...]
+    count, width, half = out.shape[0], near.shape[1], keep.shape[2]
+    rows = pl.ds(pl.multiple_of(pl.program_id(0) * count, count), count)
+    out[:, pl.ds(pl.multiple_of(pair * width, width), width)] = near[rows, :]
     start = pl.multiple_of((1 - pair) * width, width)
-    half = keep.shape[2]
-    out[:, pl.ds(start, half)] = keep[0] + got[0].astype(F32)
-    out[:, pl.ds(pl.multiple_of(start + half, half), half)] = keep2[0] + got2[0].astype(F32)
+    out[:, pl.ds(start, half)] = keep[0, rows, :] + got[0, rows, :].astype(F32)
+    start = pl.multiple_of(start + half, half)
+    out[:, pl.ds(start, half)] = keep2[0, rows, :] + got2[0, rows, :].astype(F32)
+
+
+def last(group, part, *args, steps=2):
+    return pl.pallas_call(
+        functools.partial(last_kernel, group),
+        grid=(steps,),
+        in_specs=[VMEM] * len(args),
+        out_specs=pl.BlockSpec((part // steps, 4 * PROWS), lambda n: (n, 0)),
+        out_shape=jax.ShapeDtypeStruct((part, 4 * PROWS), F32),
+        compiler_params=pltpu.CompilerParams(vmem_limit_bytes=24 * 2**20),
+        cost_estimate=pl.CostEstimate(flops=0, bytes_accessed=0, transcendentals=0),
+    )(*args)
 
 
 def local(tgt_size, pool_size, pool, target, pre, active):
@@ -269,8 +281,7 @@
     for begin, far_next in zip((0, PROWS), call(add_two_kernel, [(narrow, BF16)] * 2, far_keep, far_got, near[0])):
         gots = [far_got2, exchange(far_next, 1, 1)]
         far += rest(1, far_keep2, gots, near_total, begin=begin, width=PROWS)
-    out = ((part, 4 * PROWS), F32)
-    return call(functools.partial(last_kernel, group), [out], near_total, *far, kind=jax.ShapeDtypeStruct)[0]
+    return last(group, part, near_total, *far)
 
 
 def solution(mesh):

time: 38.6 us -> 38.5 us (level)
    pallas_call x16 -> x15, Pallas kernels: 8.96 us -> 8.1 us  [call(): pl.pallas_call(body, in_specs=specs, out_specs=[VMEM] * len(outs), out_sh...]
    pallas_call x0 -> x1, Pallas kernels: none -> 0.82 us  [last(): pl.pallas_call(functools.partial(last_kernel, group), grid=(steps,), in_s...]
where the time goes in v6:
time: 38.5 us; the launch traced here: 38.4 us
  starting transfers between devices  20 us (52%)
  waiting for transfers between devices  9.35 us (24%)
  Pallas kernels  8.93 us (23%)
    ppermute x10, starting transfers between devices, exchange(): return lax.ppermute(x, ('pool', 'tgt'), pairs)  16.1 us
    pallas_call x15, Pallas kernels, call(): pl.pallas_call(body, in_specs=specs, out_specs=[VMEM] * len(outs), out_sh...  8.1 us
    ppermute x10, waiting for transfers between devices, exchange(): return lax.ppermute(x, ('pool', 'tgt'), pairs)  7.66 us
    ppermute x4, starting transfers between devices, swap(): return lax.ppermute(x, axis, [(i, i ^ step) for i in range(size)])  3.87 us
    ppermute x4, waiting for transfers between devices, swap(): return lax.ppermute(x, axis, [(i, i ^ step) for i in range(size)])  1.69 us
    pallas_call x1, Pallas kernels, last(): pl.pallas_call(functools.partial(last_kernel, group), grid=(steps,), in_s...  0.82 us
  transfers between devices with their start and end apart: 14, of which 6 were waited for; matrix products, arithmetic and copies ran while one was open for 0% of the time, Pallas kernels for 21%

profile of v6, /device:TPU:0, one launch (start us, length us, event | category | flops | bytes accessed | tf_op | source)
XLA Modules:
  0.0 38.4 jit_solution(10130243003312713374)
XLA Ops:
  0.5 1.8 %shard_map.46 = (s32[4,16]{1,0:T(4,128)}, bf16[128,2048]{1,0:T(8,128)(2,1)S(1)}, s32[8,512]{1,0:T(8,128)S(1)}) custom-call(s32[4,16]{1,0:T(4,128)} %active.1, bf16[128,2048]{1,0:T(8,128)(2,1)} %target.1), custom_call_target="tpu_custom_call" | custom-call | flops 5000000000 | tf_op jit(solution)/shard_map/pallas_call | solution.py:18
  2.4 2.8 %collective-permute-start.4 = (bf16[128,1024]{1,0:T(8,128)(2,1)S(1)}, bf16[128,1024]{1,0:T(8,128)(2,1)S(1)}, u32[]{:S(2)}, u32[]{:S(2)}) collective-permute-start(bf16[128,1024]{1,0:T(8,128)(2,1)S(1)} %get-tuple-element.34), channel_id=1, source_target_pairs={{0,16},{8,24},{16,0},{24,8},{1,17},{9,25},{17,1},{25,9},{2,18},{10... | collective-permute-start | bytes 786440 | tf_op jit(solution)/shard_map/ppermute | solution.py:209
  5.3 1.0 %shard_map.48 = (bf16[2048,256]{1,0:T(8,128)(2,1)S(1)}, bf16[2,256,256]{2,1,0:T(8,128)(2,1)S(1)}) custom-call(bf16[2048,2048]{1,0:T(8,128)(2,1)S(1)} %copy-done, s32[8,512]{1,0:T(8,128)S(1)} %get-tuple-element.27.evens, bf16[128,2048]{1,0:T(8,128)(2,1)S(1)} %get-tuple-element.29.rows, bf16[4,512,512]{2,1,0:T(8,128)(2,1)S(1)} %copy-done.1), custom_call_target="tpu_custom_call" | custom-call | tf_op jit(solution)/shard_map/pallas_call | solution.py:18
  6.3 1.9 %collective-permute-start.2 = (bf16[2,256,256]{2,1,0:T(8,128)(2,1)S(1)}, bf16[2,256,256]{2,1,0:T(8,128)(2,1)S(1)}, u32[]{:S(2)}, u32[]{:S(2)}) collective-permute-start(bf16[2,256,256]{2,1,0:T(8,128)(2,1)S(1)} %get-tuple-element.31.rest_0_), channel_id=1, source_target_pairs={{0,1},{1,0},{2,3},{3,2},{4,5},{5,4},{6,7},{7,6},{8,10},{9,11},{10,... | collective-permute-start | bytes 786440 | tf_op jit(solution)/shard_map/ppermute | solution.py:234
  8.2 0.7 %shard_map.49.rest_0_ = bf16[2,256,256]{2,1,0:T(8,128)(2,1)S(1)} custom-call(bf16[2048,2048]{1,0:T(8,128)(2,1)S(1)} %copy-done, bf16[2048,256]{1,0:T(8,128)(2,1)S(1)} %get-tuple-element.30.right, bf16[2,256,256]{2,1,0:T(8,128)(2,1)S(1)} %get-tuple-element.31.rest_0_), custom_call_target="tpu_custom_call" | custom-call | tf_op jit(solution)/shard_map/pallas_call | solution.py:18
  9.1 1.2 %shard_map.50 = (f32[2,256,256]{2,1,0:T(8,128)S(1)}, f32[2,256,256]{2,1,0:T(8,128)S(1)}) custom-call(bf16[2048,2048]{1,0:T(8,128)(2,1)S(1)} %copy-done, bf16[2048,256]{1,0:T(8,128)(2,1)S(1)} %get-tuple-element.30.right, bf16[2,256,256]{2,1,0:T(8,128)(2,1)S(1)} %shard_map.49.rest_0_), custom_call_target="tpu_custom_call" | custom-call | tf_op jit(solution)/shard_map/pallas_call | solution.py:18
  10.4 1.7 %collective-permute-done.4.x = bf16[128,1024]{1,0:T(8,128)(2,1)S(1)} collective-permute-done((bf16[128,1024]{1,0:T(8,128)(2,1)S(1)}, bf16[128,1024]{1,0:T(8,128)(2,1)S(1)}, u32[]{:S(2)}, u32[]{:S(2)}) %collective-permute-start.4) | collective-permute-done | bytes 262176 | tf_op jit(solution)/shard_map/ppermute | solution.py:209
  12.2 0.5 %collective-permute-start.6 = (bf16[128,512]{1,0:T(8,128)(2,1)S(1)}, bf16[128,512]{1,0:T(8,128)(2,1)S(1)}, u32[]{:S(2)}, u32[]{:S(2)}) collective-permute-start(bf16[128,512]{1,0:T(8,128)(2,1)S(1)} %get-tuple-element.36.rest_1_), channel_id=1, source_target_pairs={{0,8},{8,0},{16,24},{24,16},{1,9},{9,1},{17,25},{25,17},{2,10},{10... | collective-permute-start | bytes 393224 | tf_op jit(solution)/shard_map/ppermute | solution.py:209
  12.8 2.0 %collective-permute-start.3 = (bf16[2,256,256]{2,1,0:T(8,128)(2,1)S(1)}, bf16[2,256,256]{2,1,0:T(8,128)(2,1)S(1)}, u32[]{:S(2)}, u32[]{:S(2)}) collective-permute-start(bf16[2,256,256]{2,1,0:T(8,128)(2,1)S(1)} %shard_map.51), channel_id=1, source_target_pairs={{0,2},{1,3},{2,0},{3,1},{4,6},{5,7},{6,4},{7,5},{8,9},{9,8},{10,11... | collective-permute-start | bytes 786440 | tf_op jit(solution)/shard_map/ppermute | solution.py:234
  14.7 1.0 %shard_map.53 = (bf16[2048,256]{1,0:T(8,128)(2,1)S(1)}, bf16[2,256,256]{2,1,0:T(8,128)(2,1)S(1)}) custom-call(bf16[2048,2048]{1,0:T(8,128)(2,1)S(1)} %copy-done, s32[8,512]{1,0:T(8,128)S(1)} %get-tuple-element.27.evens, bf16[4,512,512]{2,1,0:T(8,128)(2,1)S(1)} %copy-done.1, bf16[128,512]{1,0:T(8,128)(2,1)S(1)} %get-tuple-element.35.rest_0_, ...), custom_call_target="tpu_custom_call" | custom-call | tf_op jit(solution)/shard_map/pallas_call | solution.py:18
  15.8 1.6 %collective-permute-start.9 = (bf16[2,256,256]{2,1,0:T(8,128)(2,1)S(1)}, bf16[2,256,256]{2,1,0:T(8,128)(2,1)S(1)}, u32[]{:S(2)}, u32[]{:S(2)}) collective-permute-start(bf16[2,256,256]{2,1,0:T(8,128)(2,1)S(1)} %get-tuple-element.41.rest_0_), channel_id=1, source_target_pairs={{0,1},{1,0},{2,3},{3,2},{4,5},{5,4},{6,7},{7,6},{8,10},{9,11},{10,... | collective-permute-start | bytes 786440 | tf_op jit(solution)/shard_map/ppermute | solution.py:234
  17.3 0.7 %shard_map.56 = bf16[2,256,256]{2,1,0:T(8,128)(2,1)S(1)} custom-call(bf16[2048,2048]{1,0:T(8,128)(2,1)S(1)} %copy-done, bf16[2048,256]{1,0:T(8,128)(2,1)S(1)} %get-tuple-element.37.right, bf16[2,256,256]{2,1,0:T(8,128)(2,1)S(1)} %get-tuple-element.41.rest_0_, bf16[2,256,256]{2,1,0:T(8,128)(2,1)S(1)} %collective-permute-done.1.rest_0_.rest_1_), custom_call_target="tpu_custom_call" | custom-call | tf_op jit(solution)/shard_map/pallas_call | solution.py:18
  18.0 0.6 %collective-permute-start.8 = (bf16[2,256,256]{2,1,0:T(8,128)(2,1)S(1)}, bf16[2,256,256]{2,1,0:T(8,128)(2,1)S(1)}, u32[]{:S(2)}, u32[]{:S(2)}) collective-permute-start(bf16[2,256,256]{2,1,0:T(8,128)(2,1)S(1)} %shard_map.56), channel_id=1, source_target_pairs={{0,1},{1,0},{2,3},{3,2},{4,5},{5,4},{6,7},{7,6},{8,10},{9,11},{10,... | collective-permute-start | bytes 786440 | tf_op jit(solution)/shard_map/ppermute | solution.py:234
  18.6 1.2 %shard_map.54 = (f32[2,256,256]{2,1,0:T(8,128)S(1)}, f32[2,256,256]{2,1,0:T(8,128)S(1)}) custom-call(bf16[2048,2048]{1,0:T(8,128)(2,1)S(1)} %copy-done, bf16[2048,256]{1,0:T(8,128)(2,1)S(1)} %get-tuple-element.37.right), custom_call_target="tpu_custom_call" | custom-call | tf_op jit(solution)/shard_map/pallas_call | solution.py:18
  19.9 0.5 %collective-permute-done.3.rest_1_ = bf16[2,256,256]{2,1,0:T(8,128)(2,1)S(1)} collective-permute-done((bf16[2,256,256]{2,1,0:T(8,128)(2,1)S(1)}, bf16[2,256,256]{2,1,0:T(8,128)(2,1)S(1)}, u32[]{:S(2)}, u32[]{:S(2)}) %collective-permute-start.3) | collective-permute-done | bytes 262176 | tf_op jit(solution)/shard_map/ppermute | solution.py:234
  20.4 3.4 %collective-permute-start.7 = (bf16[1,256,256]{2,1,0:T(8,128)(2,1)S(1)}, bf16[1,256,256]{2,1,0:T(8,128)(2,1)S(1)}, u32[]{:S(2)}, u32[]{:S(2)}) collective-permute-start(bf16[1,256,256]{2,1,0:T(8,128)(2,1)S(1)} %get-tuple-element.40), channel_id=1, source_target_pairs={{0,4},{1,5},{2,6},{3,7},{4,0},{5,1},{6,2},{7,3},{8,12},{9,13},{10,... | collective-permute-start | bytes 393224 | tf_op jit(solution)/shard_map/ppermute | solution.py:234
  23.9 1.6 %collective-permute-start.10 = (bf16[2,256,128]{2,1,0:T(8,128)(2,1)S(1)}, bf16[2,256,128]{2,1,0:T(8,128)(2,1)S(1)}, u32[]{:S(2)}, u32[]{:S(2)}) collective-permute-start(bf16[2,256,128]{2,1,0:T(8,128)(2,1)S(1)} %get-tuple-element.43), channel_id=1, source_target_pairs={{0,2},{1,3},{2,0},{3,1},{4,6},{5,7},{6,4},{7,5},{8,9},{9,8},{10,11... | collective-permute-start | bytes 393224 | tf_op jit(solution)/shard_map/ppermute | solution.py:234
  26.0 1.1 %collective-permute-done.7.got = bf16[1,256,256]{2,1,0:T(8,128)(2,1)S(1)} collective-permute-done((bf16[1,256,256]{2,1,0:T(8,128)(2,1)S(1)}, bf16[1,256,256]{2,1,0:T(8,128)(2,1)S(1)}, u32[]{:S(2)}, u32[]{:S(2)}) %collective-permute-start.7) | collective-permute-done | bytes 131104 | tf_op jit(solution)/shard_map/ppermute | solution.py:234
  27.1 1.9 %collective-permute-done.10.rest_1_ = bf16[2,256,128]{2,1,0:T(8,128)(2,1)S(1)} collective-permute-done((bf16[2,256,128]{2,1,0:T(8,128)(2,1)S(1)}, bf16[2,256,128]{2,1,0:T(8,128)(2,1)S(1)}, u32[]{:S(2)}, u32[]{:S(2)}) %collective-permute-start.10) | collective-permute-done | bytes 131104 | tf_op jit(solution)/shard_map/ppermute | solution.py:234
  29.1 3.0 %collective-permute-start.11 = (bf16[1,256,128]{2,1,0:T(8,128)(2,1)S(1)}, bf16[1,256,128]{2,1,0:T(8,128)(2,1)S(1)}, u32[]{:S(2)}, u32[]{:S(2)}) collective-permute-start(bf16[1,256,128]{2,1,0:T(8,128)(2,1)S(1)} %get-tuple-element.45), channel_id=1, source_target_pairs={{0,4},{1,5},{2,6},{3,7},{4,0},{5,1},{6,2},{7,3},{8,12},{9,13},{10,... | collective-permute-start | bytes 196616 | tf_op jit(solution)/shard_map/ppermute | solution.py:234
  32.1 1.4 %collective-permute-start.13 = (bf16[1,256,128]{2,1,0:T(8,128)(2,1)S(1)}, bf16[1,256,128]{2,1,0:T(8,128)(2,1)S(1)}, u32[]{:S(2)}, u32[]{:S(2)}) collective-permute-start(bf16[1,256,128]{2,1,0:T(8,128)(2,1)S(1)} %get-tuple-element.48), channel_id=1, source_target_pairs={{0,4},{1,5},{2,6},{3,7},{4,0},{5,1},{6,2},{7,3},{8,12},{9,13},{10,... | collective-permute-start | bytes 196616 | tf_op jit(solution)/shard_map/ppermute | solution.py:234
  33.5 3.4 %collective-permute-done.11.got = bf16[1,256,128]{2,1,0:T(8,128)(2,1)S(1)} collective-permute-done((bf16[1,256,128]{2,1,0:T(8,128)(2,1)S(1)}, bf16[1,256,128]{2,1,0:T(8,128)(2,1)S(1)}, u32[]{:S(2)}, u32[]{:S(2)}) %collective-permute-start.11) | collective-permute-done | bytes 65568 | tf_op jit(solution)/shard_map/ppermute | solution.py:234
  36.8 0.7 %collective-permute-done.13.got2 = bf16[1,256,128]{2,1,0:T(8,128)(2,1)S(1)} collective-permute-done((bf16[1,256,128]{2,1,0:T(8,128)(2,1)S(1)}, bf16[1,256,128]{2,1,0:T(8,128)(2,1)S(1)}, u32[]{:S(2)}, u32[]{:S(2)}) %collective-permute-start.13) | collective-permute-done | bytes 65568 | tf_op jit(solution)/shard_map/ppermute | solution.py:234
  37.5 0.8 %shard_map.61 = f32[256,512]{1,0:T(8,128)} custom-call(f32[256,256]{1,0:T(8,128)S(1)} %shard_map.57.rest_2_.near, f32[1,256,128]{2,1,0:T(8,128)S(1)} %get-tuple-element.44.keep, bf16[1,256,128]{2,1,0:T(8,128)(2,1)S(1)} %collective-permute-done.11.got, f32[1,256,128]{2,1,0:T(8,128)S(1)} %get-tuple-element.47.keep2, ...), custom_call_target="tpu_custom_call" | custom-call | tf_op jit(solution)/shard_map/pallas_call | solution.py:184
  (24 shorter events, 1.7 us)
Async XLA Ops:
  0.0 5.3 %copy-start = (bf16[2048,2048]{1,0:T(8,128)(2,1)S(1)}, bf16[2048,2048]{1,0:T(8,128)(2,1)}, u32[]{:S(2)}) copy-start(bf16[2048,2048]{1,0:T(8,128)(2,1)} %pool.11) | copy-start | bytes 25165828
  0.0 5.3 %copy-start.1 = (bf16[4,512,512]{2,1,0:T(8,128)(2,1)S(1)}, bf16[4,512,512]{2,1,0:T(8,128)(2,1)}, u32[]{:S(2)}) copy-start(bf16[4,512,512]{2,1,0:T(8,128)(2,1)} %pre.3) | copy-start | bytes 6291460
  0.0 2.3 %collective-permute-start = (bf16[128,2048]{1,0:T(8,128)(2,1)}, bf16[128,2048]{1,0:T(8,128)(2,1)S(1)}, u32[]{:S(2)}, u32[]{:S(2)}) collective-permute-start(bf16[128,2048]{1,0:T(8,128)(2,1)} %target.1), channel_id=1, source_target_pairs={{0,8},{8,0},{16,24},{24,16},{1,9},{9,1},{17,25},{25,17},{2,10},{10... | collective-permute-start | bytes 1572872 | tf_op jit(solution)/shard_map/ppermute | solution.py:209
  2.4 9.6 %collective-permute-start.4 = (bf16[128,1024]{1,0:T(8,128)(2,1)S(1)}, bf16[128,1024]{1,0:T(8,128)(2,1)S(1)}, u32[]{:S(2)}, u32[]{:S(2)}) collective-permute-start(bf16[128,1024]{1,0:T(8,128)(2,1)S(1)} %get-tuple-element.34), channel_id=1, source_target_pairs={{0,16},{8,24},{16,0},{24,8},{1,17},{9,25},{17,1},{25,9},{2,18},{10... | collective-permute-start | bytes 786440 | tf_op jit(solution)/shard_map/ppermute | solution.py:209
  6.3 6.4 %collective-permute-start.2 = (bf16[2,256,256]{2,1,0:T(8,128)(2,1)S(1)}, bf16[2,256,256]{2,1,0:T(8,128)(2,1)S(1)}, u32[]{:S(2)}, u32[]{:S(2)}) collective-permute-start(bf16[2,256,256]{2,1,0:T(8,128)(2,1)S(1)} %get-tuple-element.31.rest_0_), channel_id=1, source_target_pairs={{0,1},{1,0},{2,3},{3,2},{4,5},{5,4},{6,7},{7,6},{8,10},{9,11},{10,... | collective-permute-start | bytes 786440 | tf_op jit(solution)/shard_map/ppermute | solution.py:234
  8.9 8.4 %collective-permute-start.1 = (bf16[2,256,256]{2,1,0:T(8,128)(2,1)S(1)}, bf16[2,256,256]{2,1,0:T(8,128)(2,1)S(1)}, u32[]{:S(2)}, u32[]{:S(2)}) collective-permute-start(bf16[2,256,256]{2,1,0:T(8,128)(2,1)S(1)} %shard_map.49.rest_0_), channel_id=1, source_target_pairs={{0,1},{1,0},{2,3},{3,2},{4,5},{5,4},{6,7},{7,6},{8,10},{9,11},{10,... | collective-permute-start | bytes 786440 | tf_op jit(solution)/shard_map/ppermute | solution.py:234
  12.1 2.7 %collective-permute-start.5 = (bf16[128,512]{1,0:T(8,128)(2,1)S(1)}, bf16[128,512]{1,0:T(8,128)(2,1)S(1)}, u32[]{:S(2)}, u32[]{:S(2)}) collective-permute-start(bf16[128,512]{1,0:T(8,128)(2,1)S(1)} %get-tuple-element.35.rest_0_), channel_id=1, source_target_pairs={{0,8},{8,0},{16,24},{24,16},{1,9},{9,1},{17,25},{25,17},{2,10},{10... | collective-permute-start | bytes 393224 | tf_op jit(solution)/shard_map/ppermute | solution.py:209
  12.2 2.6 %collective-permute-start.6 = (bf16[128,512]{1,0:T(8,128)(2,1)S(1)}, bf16[128,512]{1,0:T(8,128)(2,1)S(1)}, u32[]{:S(2)}, u32[]{:S(2)}) collective-permute-start(bf16[128,512]{1,0:T(8,128)(2,1)S(1)} %get-tuple-element.36.rest_1_), channel_id=1, source_target_pairs={{0,8},{8,0},{16,24},{24,16},{1,9},{9,1},{17,25},{25,17},{2,10},{10... | collective-permute-start | bytes 393224 | tf_op jit(solution)/shard_map/ppermute | solution.py:209
  12.8 7.6 %collective-permute-start.3 = (bf16[2,256,256]{2,1,0:T(8,128)(2,1)S(1)}, bf16[2,256,256]{2,1,0:T(8,128)(2,1)S(1)}, u32[]{:S(2)}, u32[]{:S(2)}) collective-permute-start(bf16[2,256,256]{2,1,0:T(8,128)(2,1)S(1)} %shard_map.51), channel_id=1, source_target_pairs={{0,2},{1,3},{2,0},{3,1},{4,6},{5,7},{6,4},{7,5},{8,9},{9,8},{10,11... | collective-permute-start | bytes 786440 | tf_op jit(solution)/shard_map/ppermute | solution.py:234
  15.8 8.1 %collective-permute-start.9 = (bf16[2,256,256]{2,1,0:T(8,128)(2,1)S(1)}, bf16[2,256,256]{2,1,0:T(8,128)(2,1)S(1)}, u32[]{:S(2)}, u32[]{:S(2)}) collective-permute-start(bf16[2,256,256]{2,1,0:T(8,128)(2,1)S(1)} %get-tuple-element.41.rest_0_), channel_id=1, source_target_pairs={{0,1},{1,0},{2,3},{3,2},{4,5},{5,4},{6,7},{7,6},{8,10},{9,11},{10,... | collective-permute-start | bytes 786440 | tf_op jit(solution)/shard_map/ppermute | solution.py:234
  18.0 9.1 %collective-permute-start.8 = (bf16[2,256,256]{2,1,0:T(8,128)(2,1)S(1)}, bf16[2,256,256]{2,1,0:T(8,128)(2,1)S(1)}, u32[]{:S(2)}, u32[]{:S(2)}) collective-permute-start(bf16[2,256,256]{2,1,0:T(8,128)(2,1)S(1)} %shard_map.56), channel_id=1, source_target_pairs={{0,1},{1,0},{2,3},{3,2},{4,5},{5,4},{6,7},{7,6},{8,10},{9,11},{10,... | collective-permute-start | bytes 786440 | tf_op jit(solution)/shard_map/ppermute | solution.py:234
  20.4 6.7 %collective-permute-start.7 = (bf16[1,256,256]{2,1,0:T(8,128)(2,1)S(1)}, bf16[1,256,256]{2,1,0:T(8,128)(2,1)S(1)}, u32[]{:S(2)}, u32[]{:S(2)}) collective-permute-start(bf16[1,256,256]{2,1,0:T(8,128)(2,1)S(1)} %get-tuple-element.40), channel_id=1, source_target_pairs={{0,4},{1,5},{2,6},{3,7},{4,0},{5,1},{6,2},{7,3},{8,12},{9,13},{10,... | collective-permute-start | bytes 393224 | tf_op jit(solution)/shard_map/ppermute | solution.py:234
  23.9 5.2 %collective-permute-start.10 = (bf16[2,256,128]{2,1,0:T(8,128)(2,1)S(1)}, bf16[2,256,128]{2,1,0:T(8,128)(2,1)S(1)}, u32[]{:S(2)}, u32[]{:S(2)}) collective-permute-start(bf16[2,256,128]{2,1,0:T(8,128)(2,1)S(1)} %get-tuple-element.43), channel_id=1, source_target_pairs={{0,2},{1,3},{2,0},{3,1},{4,6},{5,7},{6,4},{7,5},{8,9},{9,8},{10,11... | collective-permute-start | bytes 393224 | tf_op jit(solution)/shard_map/ppermute | solution.py:234
  25.5 6.6 %collective-permute-start.12 = (bf16[2,256,128]{2,1,0:T(8,128)(2,1)S(1)}, bf16[2,256,128]{2,1,0:T(8,128)(2,1)S(1)}, u32[]{:S(2)}, u32[]{:S(2)}) collective-permute-start(bf16[2,256,128]{2,1,0:T(8,128)(2,1)S(1)} %get-tuple-element.46), channel_id=1, source_target_pairs={{0,2},{1,3},{2,0},{3,1},{4,6},{5,7},{6,4},{7,5},{8,9},{9,8},{10,11... | collective-permute-start | bytes 393224 | tf_op jit(solution)/shard_map/ppermute | solution.py:234
  29.1 7.8 %collective-permute-start.11 = (bf16[1,256,128]{2,1,0:T(8,128)(2,1)S(1)}, bf16[1,256,128]{2,1,0:T(8,128)(2,1)S(1)}, u32[]{:S(2)}, u32[]{:S(2)}) collective-permute-start(bf16[1,256,128]{2,1,0:T(8,128)(2,1)S(1)} %get-tuple-element.45), channel_id=1, source_target_pairs={{0,4},{1,5},{2,6},{3,7},{4,0},{5,1},{6,2},{7,3},{8,12},{9,13},{10,... | collective-permute-start | bytes 196616 | tf_op jit(solution)/shard_map/ppermute | solution.py:234
  32.1 5.4 %collective-permute-start.13 = (bf16[1,256,128]{2,1,0:T(8,128)(2,1)S(1)}, bf16[1,256,128]{2,1,0:T(8,128)(2,1)S(1)}, u32[]{:S(2)}, u32[]{:S(2)}) collective-permute-start(bf16[1,256,128]{2,1,0:T(8,128)(2,1)S(1)} %get-tuple-element.48), channel_id=1, source_target_pairs={{0,4},{1,5},{2,6},{3,7},{4,0},{5,1},{6,2},{7,3},{8,12},{9,13},{10,... | collective-permute-start | bytes 196616 | tf_op jit(solution)/shard_map/ppermute | solution.py:234

commit v7 on v5

--- a/solution.py
+++ b/solution.py
@@ -165,8 +165,9 @@
             out[i] = total.astype(out.dtype)
 
 
-def total_kernel(keep, got, *rest):
-    rest[-1][...] = keep[0] + got[0].astype(F32)
+def total_kernel(keep, got, keep2, got2, *rest):
+    rest[-1][:, :PROWS] = keep[0] + got[0].astype(F32)
+    rest[-1][:, PROWS:] = keep2[0] + got2[0].astype(F32)
 
 
 def last_kernel(group, near, keep, got, keep2, got2, out):
@@ -250,7 +251,8 @@
     send2 = more(0, [1], BF16, right, send, flops=0)[0]
     got2 = exchange(send2, 0, 0)
     keep, keep2 = more(0, [2, 3], F32, right, send2, flops=0)
-    near_next = add(keep, got)
+    narrow = (shape[0], shape[1], PROWS)
+    near_next = call(add_two_kernel, [(narrow, BF16)] * 2, keep, got)
     mine = split_after(mine, blocks // 2, keep, flops=0)
     other = [swap(piece, "pool", group) for piece in mine]
     right, far_send = call(
@@ -260,13 +262,15 @@
     far_got = exchange(far_send, 0, 1)
     far_send2 = more(1, [1], BF16, right, far_send, got2)[0]
     far_got2 = exchange(far_send2, 0, 1)
-    got3 = exchange(near_next, 1, 0)
-    far_keep, far_keep2 = more(1, [2, 3], F32, right, flops=0)
-    near = rest(0, keep2, [got2, got3], far_keep)
+    got3 = [exchange(piece, 1, 0) for piece in near_next]
+    far_keep, far_keep2 = more(1, [2, 3], F32, right, flops=10**10)
+    near = []
+    for n, piece in enumerate(got3):
+        near += rest(0, keep2, [got2, piece], far_keep, begin=n * PROWS, width=PROWS)
     near_total = call(total_kernel, [((part, 2 * PROWS), F32)], *near, far_got2, flops=10**11)[0]
     far = []
     narrow = (shape[0], shape[1], PROWS)
-    for begin, far_next in zip((0, PROWS), call(add_two_kernel, [(narrow, BF16)] * 2, far_keep, far_got, near[0])):
+    for begin, far_next in zip((0, PROWS), call(add_two_kernel, [(narrow, BF16)] * 2, far_keep, far_got, near[0], near[2])):
         gots = [far_got2, exchange(far_next, 1, 1)]
         far += rest(1, far_keep2, gots, near_total, begin=begin, width=PROWS)
     out = ((part, 4 * PROWS), F32)

time: 38.6 us -> 38.6 us (level)
  starting transfers between devices: 20 us -> 18.5 us
  waiting for transfers between devices: 9.35 us -> 10.8 us
    ppermute x10 -> x12, waiting for transfers between devices: 7.66 us -> 9.15 us  [exchange(): return lax.ppermute(x, ('pool', 'tgt'), pairs)]
    ppermute x10 -> x12, starting transfers between devices: 16.1 us -> 14.7 us  [exchange(): return lax.ppermute(x, ('pool', 'tgt'), pairs)]
    pallas_call x16 -> x17, Pallas kernels: 8.96 us -> 8.98 us  [call(): pl.pallas_call(body, in_specs=specs, out_specs=[VMEM] * len(outs), out_sh...]
  transfers between devices with their start and end apart: 14 -> 16, of which waited for: 6 -> 6; matrix products, arithmetic and copies ran while one was open for 0% -> 0% of each run, Pallas kernels for 21% -> 21%
where the time goes in v7:
time: 38.6 us; the launch traced here: 38.5 us
  starting transfers between devices  18.5 us (48%)
  waiting for transfers between devices  10.8 us (28%)
  Pallas kernels  8.98 us (23%)
    ppermute x12, starting transfers between devices, exchange(): return lax.ppermute(x, ('pool', 'tgt'), pairs)  14.7 us
    ppermute x12, waiting for transfers between devices, exchange(): return lax.ppermute(x, ('pool', 'tgt'), pairs)  9.15 us
    pallas_call x17, Pallas kernels, call(): pl.pallas_call(body, in_specs=specs, out_specs=[VMEM] * len(outs), out_sh...  8.98 us
    ppermute x4, starting transfers between devices, swap(): return lax.ppermute(x, axis, [(i, i ^ step) for i in range(size)])  3.87 us
    ppermute x4, waiting for transfers between devices, swap(): return lax.ppermute(x, axis, [(i, i ^ step) for i in range(size)])  1.69 us
  transfers between devices with their start and end apart: 16, of which 6 were waited for; matrix products, arithmetic and copies ran while one was open for 0% of the time, Pallas kernels for 21%

profile of v7, /device:TPU:0, one launch (start us, length us, event | category | flops | bytes accessed | tf_op | source)
XLA Modules:
  0.0 38.5 jit_solution(11571762171542103836)
XLA Ops:
  0.0 0.5 %collective-permute-start = (bf16[128,2048]{1,0:T(8,128)(2,1)}, bf16[128,2048]{1,0:T(8,128)(2,1)S(1)}, u32[]{:S(2)}, u32[]{:S(2)}) collective-permute-start(bf16[128,2048]{1,0:T(8,128)(2,1)} %target.1), channel_id=1, source_target_pairs={{0,8},{8,0},{16,24},{24,16},{1,9},{9,1},{17,25},{25,17},{2,10},{10... | collective-permute-start | bytes 1572872 | tf_op jit(solution)/shard_map/ppermute | solution.py:198
  0.5 1.8 %shard_map.46 = (s32[4,16]{1,0:T(4,128)}, bf16[128,2048]{1,0:T(8,128)(2,1)S(1)}, s32[8,512]{1,0:T(8,128)S(1)}) custom-call(s32[4,16]{1,0:T(4,128)} %active.1, bf16[128,2048]{1,0:T(8,128)(2,1)} %target.1), custom_call_target="tpu_custom_call" | custom-call | flops 5000000000 | tf_op jit(solution)/shard_map/pallas_call | solution.py:18
  2.4 2.8 %collective-permute-start.4 = (bf16[128,1024]{1,0:T(8,128)(2,1)S(1)}, bf16[128,1024]{1,0:T(8,128)(2,1)S(1)}, u32[]{:S(2)}, u32[]{:S(2)}) collective-permute-start(bf16[128,1024]{1,0:T(8,128)(2,1)S(1)} %get-tuple-element.39), channel_id=1, source_target_pairs={{0,16},{8,24},{16,0},{24,8},{1,17},{9,25},{17,1},{25,9},{2,18},{10... | collective-permute-start | bytes 786440 | tf_op jit(solution)/shard_map/ppermute | solution.py:198
  5.3 1.0 %shard_map.48 = (bf16[2048,256]{1,0:T(8,128)(2,1)S(1)}, bf16[2,256,256]{2,1,0:T(8,128)(2,1)S(1)}) custom-call(bf16[2048,2048]{1,0:T(8,128)(2,1)S(1)} %copy-done, s32[8,512]{1,0:T(8,128)S(1)} %get-tuple-element.31.evens, bf16[128,2048]{1,0:T(8,128)(2,1)S(1)} %get-tuple-element.33.rows, bf16[4,512,512]{2,1,0:T(8,128)(2,1)S(1)} %copy-done.1), custom_call_target="tpu_custom_call" | custom-call | tf_op jit(solution)/shard_map/pallas_call | solution.py:18
  6.3 1.9 %collective-permute-start.2 = (bf16[2,256,256]{2,1,0:T(8,128)(2,1)S(1)}, bf16[2,256,256]{2,1,0:T(8,128)(2,1)S(1)}, u32[]{:S(2)}, u32[]{:S(2)}) collective-permute-start(bf16[2,256,256]{2,1,0:T(8,128)(2,1)S(1)} %get-tuple-element.35.rest_0_), channel_id=1, source_target_pairs={{0,1},{1,0},{2,3},{3,2},{4,5},{5,4},{6,7},{7,6},{8,10},{9,11},{10,... | collective-permute-start | bytes 786440 | tf_op jit(solution)/shard_map/ppermute | solution.py:223
  8.2 0.7 %shard_map.49.rest_0_ = bf16[2,256,256]{2,1,0:T(8,128)(2,1)S(1)} custom-call(bf16[2048,2048]{1,0:T(8,128)(2,1)S(1)} %copy-done, bf16[2048,256]{1,0:T(8,128)(2,1)S(1)} %get-tuple-element.34.right, bf16[2,256,256]{2,1,0:T(8,128)(2,1)S(1)} %get-tuple-element.35.rest_0_), custom_call_target="tpu_custom_call" | custom-call | tf_op jit(solution)/shard_map/pallas_call | solution.py:18
  9.1 1.2 %shard_map.50 = (f32[2,256,256]{2,1,0:T(8,128)S(1)}, f32[2,256,256]{2,1,0:T(8,128)S(1)}) custom-call(bf16[2048,2048]{1,0:T(8,128)(2,1)S(1)} %copy-done, bf16[2048,256]{1,0:T(8,128)(2,1)S(1)} %get-tuple-element.34.right, bf16[2,256,256]{2,1,0:T(8,128)(2,1)S(1)} %shard_map.49.rest_0_), custom_call_target="tpu_custom_call" | custom-call | tf_op jit(solution)/shard_map/pallas_call | solution.py:18
  10.4 1.7 %collective-permute-done.4.x = bf16[128,1024]{1,0:T(8,128)(2,1)S(1)} collective-permute-done((bf16[128,1024]{1,0:T(8,128)(2,1)S(1)}, bf16[128,1024]{1,0:T(8,128)(2,1)S(1)}, u32[]{:S(2)}, u32[]{:S(2)}) %collective-permute-start.4) | collective-permute-done | bytes 262176 | tf_op jit(solution)/shard_map/ppermute | solution.py:198
  12.2 0.5 %collective-permute-start.6 = (bf16[128,512]{1,0:T(8,128)(2,1)S(1)}, bf16[128,512]{1,0:T(8,128)(2,1)S(1)}, u32[]{:S(2)}, u32[]{:S(2)}) collective-permute-start(bf16[128,512]{1,0:T(8,128)(2,1)S(1)} %get-tuple-element.41.rest_1_), channel_id=1, source_target_pairs={{0,8},{8,0},{16,24},{24,16},{1,9},{9,1},{17,25},{25,17},{2,10},{10... | collective-permute-start | bytes 393224 | tf_op jit(solution)/shard_map/ppermute | solution.py:198
  12.8 2.0 %collective-permute-start.3 = (bf16[2,256,128]{2,1,0:T(8,128)(2,1)S(1)}, bf16[2,256,128]{2,1,0:T(8,128)(2,1)S(1)}, u32[]{:S(2)}, u32[]{:S(2)}) collective-permute-start(bf16[2,256,128]{2,1,0:T(8,128)(2,1)S(1)} %get-tuple-element.38), channel_id=1, source_target_pairs={{0,2},{1,3},{2,0},{3,1},{4,6},{5,7},{6,4},{7,5},{8,9},{9,8},{10,11... | collective-permute-start | bytes 393224 | tf_op jit(solution)/shard_map/ppermute | solution.py:223
  14.9 1.0 %shard_map.53 = (bf16[2048,256]{1,0:T(8,128)(2,1)S(1)}, bf16[2,256,256]{2,1,0:T(8,128)(2,1)S(1)}) custom-call(bf16[2048,2048]{1,0:T(8,128)(2,1)S(1)} %copy-done, s32[8,512]{1,0:T(8,128)S(1)} %get-tuple-element.31.evens, bf16[4,512,512]{2,1,0:T(8,128)(2,1)S(1)} %copy-done.1, bf16[128,512]{1,0:T(8,128)(2,1)S(1)} %get-tuple-element.40.rest_0_, ...), custom_call_target="tpu_custom_call" | custom-call | tf_op jit(solution)/shard_map/pallas_call | solution.py:18
  15.9 1.9 %collective-permute-start.11 = (bf16[2,256,256]{2,1,0:T(8,128)(2,1)S(1)}, bf16[2,256,256]{2,1,0:T(8,128)(2,1)S(1)}, u32[]{:S(2)}, u32[]{:S(2)}) collective-permute-start(bf16[2,256,256]{2,1,0:T(8,128)(2,1)S(1)} %get-tuple-element.49.rest_0_), channel_id=1, source_target_pairs={{0,1},{1,0},{2,3},{3,2},{4,5},{5,4},{6,7},{7,6},{8,10},{9,11},{10,... | collective-permute-start | bytes 786440 | tf_op jit(solution)/shard_map/ppermute | solution.py:223
  17.8 0.7 %shard_map.57 = bf16[2,256,256]{2,1,0:T(8,128)(2,1)S(1)} custom-call(bf16[2048,2048]{1,0:T(8,128)(2,1)S(1)} %copy-done, bf16[2048,256]{1,0:T(8,128)(2,1)S(1)} %get-tuple-element.42.right, bf16[2,256,256]{2,1,0:T(8,128)(2,1)S(1)} %get-tuple-element.49.rest_0_, bf16[2,256,256]{2,1,0:T(8,128)(2,1)S(1)} %collective-permute-done.1.rest_0_.rest_1_), custom_call_target="tpu_custom_call" | custom-call | tf_op jit(solution)/shard_map/pallas_call | solution.py:18
  18.7 1.2 %shard_map.54 = (f32[2,256,256]{2,1,0:T(8,128)S(1)}, f32[2,256,256]{2,1,0:T(8,128)S(1)}) custom-call(bf16[2048,2048]{1,0:T(8,128)(2,1)S(1)} %copy-done, bf16[2048,256]{1,0:T(8,128)(2,1)S(1)} %get-tuple-element.42.right), custom_call_target="tpu_custom_call" | custom-call | flops 10000000000 | tf_op jit(solution)/shard_map/pallas_call | solution.py:18
  20.0 1.1 %collective-permute-done.8.rest_1_ = bf16[2,256,128]{2,1,0:T(8,128)(2,1)S(1)} collective-permute-done((bf16[2,256,128]{2,1,0:T(8,128)(2,1)S(1)}, bf16[2,256,128]{2,1,0:T(8,128)(2,1)S(1)}, u32[]{:S(2)}, u32[]{:S(2)}) %collective-permute-start.8) | collective-permute-done | bytes 131104 | tf_op jit(solution)/shard_map/ppermute | solution.py:223
  21.2 2.7 %collective-permute-start.9 = (bf16[1,256,128]{2,1,0:T(8,128)(2,1)S(1)}, bf16[1,256,128]{2,1,0:T(8,128)(2,1)S(1)}, u32[]{:S(2)}, u32[]{:S(2)}) collective-permute-start(bf16[1,256,128]{2,1,0:T(8,128)(2,1)S(1)} %get-tuple-element.48), channel_id=1, source_target_pairs={{0,4},{1,5},{2,6},{3,7},{4,0},{5,1},{6,2},{7,3},{8,12},{9,13},{10,... | collective-permute-start | bytes 196616 | tf_op jit(solution)/shard_map/ppermute | solution.py:223
  24.3 1.3 %collective-permute-start.12 = (bf16[2,256,128]{2,1,0:T(8,128)(2,1)S(1)}, bf16[2,256,128]{2,1,0:T(8,128)(2,1)S(1)}, u32[]{:S(2)}, u32[]{:S(2)}) collective-permute-start(bf16[2,256,128]{2,1,0:T(8,128)(2,1)S(1)} %get-tuple-element.51), channel_id=1, source_target_pairs={{0,2},{1,3},{2,0},{3,1},{4,6},{5,7},{6,4},{7,5},{8,9},{9,8},{10,11... | collective-permute-start | bytes 393224 | tf_op jit(solution)/shard_map/ppermute | solution.py:223
  25.6 0.8 %collective-permute-start.14 = (bf16[2,256,128]{2,1,0:T(8,128)(2,1)S(1)}, bf16[2,256,128]{2,1,0:T(8,128)(2,1)S(1)}, u32[]{:S(2)}, u32[]{:S(2)}) collective-permute-start(bf16[2,256,128]{2,1,0:T(8,128)(2,1)S(1)} %get-tuple-element.54), channel_id=1, source_target_pairs={{0,2},{1,3},{2,0},{3,1},{4,6},{5,7},{6,4},{7,5},{8,9},{9,8},{10,11... | collective-permute-start | bytes 393224 | tf_op jit(solution)/shard_map/ppermute | solution.py:223
  26.8 4.1 %collective-permute-done.7.got = bf16[1,256,128]{2,1,0:T(8,128)(2,1)S(1)} collective-permute-done((bf16[1,256,128]{2,1,0:T(8,128)(2,1)S(1)}, bf16[1,256,128]{2,1,0:T(8,128)(2,1)S(1)}, u32[]{:S(2)}, u32[]{:S(2)}) %collective-permute-start.7) | collective-permute-done | bytes 65568 | tf_op jit(solution)/shard_map/ppermute | solution.py:223
  31.0 1.2 %collective-permute-start.13 = (bf16[1,256,128]{2,1,0:T(8,128)(2,1)S(1)}, bf16[1,256,128]{2,1,0:T(8,128)(2,1)S(1)}, u32[]{:S(2)}, u32[]{:S(2)}) collective-permute-start(bf16[1,256,128]{2,1,0:T(8,128)(2,1)S(1)} %get-tuple-element.53), channel_id=1, source_target_pairs={{0,4},{1,5},{2,6},{3,7},{4,0},{5,1},{6,2},{7,3},{8,12},{9,13},{10,... | collective-permute-start | bytes 196616 | tf_op jit(solution)/shard_map/ppermute | solution.py:223
  32.2 1.9 %collective-permute-start.15 = (bf16[1,256,128]{2,1,0:T(8,128)(2,1)S(1)}, bf16[1,256,128]{2,1,0:T(8,128)(2,1)S(1)}, u32[]{:S(2)}, u32[]{:S(2)}) collective-permute-start(bf16[1,256,128]{2,1,0:T(8,128)(2,1)S(1)} %get-tuple-element.56), channel_id=1, source_target_pairs={{0,4},{1,5},{2,6},{3,7},{4,0},{5,1},{6,2},{7,3},{8,12},{9,13},{10,... | collective-permute-start | bytes 196616 | tf_op jit(solution)/shard_map/ppermute | solution.py:223
  34.1 2.8 %collective-permute-done.13.got = bf16[1,256,128]{2,1,0:T(8,128)(2,1)S(1)} collective-permute-done((bf16[1,256,128]{2,1,0:T(8,128)(2,1)S(1)}, bf16[1,256,128]{2,1,0:T(8,128)(2,1)S(1)}, u32[]{:S(2)}, u32[]{:S(2)}) %collective-permute-start.13) | collective-permute-done | bytes 65568 | tf_op jit(solution)/shard_map/ppermute | solution.py:223
  36.9 0.7 %collective-permute-done.15.got2 = bf16[1,256,128]{2,1,0:T(8,128)(2,1)S(1)} collective-permute-done((bf16[1,256,128]{2,1,0:T(8,128)(2,1)S(1)}, bf16[1,256,128]{2,1,0:T(8,128)(2,1)S(1)}, u32[]{:S(2)}, u32[]{:S(2)}) %collective-permute-start.15) | collective-permute-done | bytes 65568 | tf_op jit(solution)/shard_map/ppermute | solution.py:223
  37.6 0.9 %shard_map.62 = f32[256,512]{1,0:T(8,128)} custom-call(f32[256,256]{1,0:T(8,128)S(1)} %shard_map.58.rest_2_.near, f32[1,256,128]{2,1,0:T(8,128)S(1)} %get-tuple-element.52.keep, bf16[1,256,128]{2,1,0:T(8,128)(2,1)S(1)} %collective-permute-done.13.got, f32[1,256,128]{2,1,0:T(8,128)S(1)} %get-tuple-element.55.keep2, ...), custom_call_target="tpu_custom_call" | custom-call | tf_op jit(solution)/shard_map/pallas_call | solution.py:18
  (29 shorter events, 2.0 us)
Async XLA Ops:
  0.0 5.3 %copy-start = (bf16[2048,2048]{1,0:T(8,128)(2,1)S(1)}, bf16[2048,2048]{1,0:T(8,128)(2,1)}, u32[]{:S(2)}) copy-start(bf16[2048,2048]{1,0:T(8,128)(2,1)} %pool.11) | copy-start | bytes 25165828
  0.0 5.3 %copy-start.1 = (bf16[4,512,512]{2,1,0:T(8,128)(2,1)S(1)}, bf16[4,512,512]{2,1,0:T(8,128)(2,1)}, u32[]{:S(2)}) copy-start(bf16[4,512,512]{2,1,0:T(8,128)(2,1)} %pre.3) | copy-start | bytes 6291460
  0.0 2.3 %collective-permute-start = (bf16[128,2048]{1,0:T(8,128)(2,1)}, bf16[128,2048]{1,0:T(8,128)(2,1)S(1)}, u32[]{:S(2)}, u32[]{:S(2)}) collective-permute-start(bf16[128,2048]{1,0:T(8,128)(2,1)} %target.1), channel_id=1, source_target_pairs={{0,8},{8,0},{16,24},{24,16},{1,9},{9,1},{17,25},{25,17},{2,10},{10... | collective-permute-start | bytes 1572872 | tf_op jit(solution)/shard_map/ppermute | solution.py:198
  2.4 9.6 %collective-permute-start.4 = (bf16[128,1024]{1,0:T(8,128)(2,1)S(1)}, bf16[128,1024]{1,0:T(8,128)(2,1)S(1)}, u32[]{:S(2)}, u32[]{:S(2)}) collective-permute-start(bf16[128,1024]{1,0:T(8,128)(2,1)S(1)} %get-tuple-element.39), channel_id=1, source_target_pairs={{0,16},{8,24},{16,0},{24,8},{1,17},{9,25},{17,1},{25,9},{2,18},{10... | collective-permute-start | bytes 786440 | tf_op jit(solution)/shard_map/ppermute | solution.py:198
  6.3 6.4 %collective-permute-start.2 = (bf16[2,256,256]{2,1,0:T(8,128)(2,1)S(1)}, bf16[2,256,256]{2,1,0:T(8,128)(2,1)S(1)}, u32[]{:S(2)}, u32[]{:S(2)}) collective-permute-start(bf16[2,256,256]{2,1,0:T(8,128)(2,1)S(1)} %get-tuple-element.35.rest_0_), channel_id=1, source_target_pairs={{0,1},{1,0},{2,3},{3,2},{4,5},{5,4},{6,7},{7,6},{8,10},{9,11},{10,... | collective-permute-start | bytes 786440 | tf_op jit(solution)/shard_map/ppermute | solution.py:223
  8.9 8.9 %collective-permute-start.1 = (bf16[2,256,256]{2,1,0:T(8,128)(2,1)S(1)}, bf16[2,256,256]{2,1,0:T(8,128)(2,1)S(1)}, u32[]{:S(2)}, u32[]{:S(2)}) collective-permute-start(bf16[2,256,256]{2,1,0:T(8,128)(2,1)S(1)} %shard_map.49.rest_0_), channel_id=1, source_target_pairs={{0,1},{1,0},{2,3},{3,2},{4,5},{5,4},{6,7},{7,6},{8,10},{9,11},{10,... | collective-permute-start | bytes 786440 | tf_op jit(solution)/shard_map/ppermute | solution.py:223
  12.1 2.8 %collective-permute-start.5 = (bf16[128,512]{1,0:T(8,128)(2,1)S(1)}, bf16[128,512]{1,0:T(8,128)(2,1)S(1)}, u32[]{:S(2)}, u32[]{:S(2)}) collective-permute-start(bf16[128,512]{1,0:T(8,128)(2,1)S(1)} %get-tuple-element.40.rest_0_), channel_id=1, source_target_pairs={{0,8},{8,0},{16,24},{24,16},{1,9},{9,1},{17,25},{25,17},{2,10},{10... | collective-permute-start | bytes 393224 | tf_op jit(solution)/shard_map/ppermute | solution.py:198
  12.2 2.7 %collective-permute-start.6 = (bf16[128,512]{1,0:T(8,128)(2,1)S(1)}, bf16[128,512]{1,0:T(8,128)(2,1)S(1)}, u32[]{:S(2)}, u32[]{:S(2)}) collective-permute-start(bf16[128,512]{1,0:T(8,128)(2,1)S(1)} %get-tuple-element.41.rest_1_), channel_id=1, source_target_pairs={{0,8},{8,0},{16,24},{24,16},{1,9},{9,1},{17,25},{25,17},{2,10},{10... | collective-permute-start | bytes 393224 | tf_op jit(solution)/shard_map/ppermute | solution.py:198
  12.8 11.0 %collective-permute-start.3 = (bf16[2,256,128]{2,1,0:T(8,128)(2,1)S(1)}, bf16[2,256,128]{2,1,0:T(8,128)(2,1)S(1)}, u32[]{:S(2)}, u32[]{:S(2)}) collective-permute-start(bf16[2,256,128]{2,1,0:T(8,128)(2,1)S(1)} %get-tuple-element.38), channel_id=1, source_target_pairs={{0,2},{1,3},{2,0},{3,1},{4,6},{5,7},{6,4},{7,5},{8,9},{9,8},{10,11... | collective-permute-start | bytes 393224 | tf_op jit(solution)/shard_map/ppermute | solution.py:223
  14.7 6.4 %collective-permute-start.8 = (bf16[2,256,128]{2,1,0:T(8,128)(2,1)S(1)}, bf16[2,256,128]{2,1,0:T(8,128)(2,1)S(1)}, u32[]{:S(2)}, u32[]{:S(2)}) collective-permute-start(bf16[2,256,128]{2,1,0:T(8,128)(2,1)S(1)} %get-tuple-element.46), channel_id=1, source_target_pairs={{0,2},{1,3},{2,0},{3,1},{4,6},{5,7},{6,4},{7,5},{8,9},{9,8},{10,11... | collective-permute-start | bytes 393224 | tf_op jit(solution)/shard_map/ppermute | solution.py:223
  15.9 8.4 %collective-permute-start.11 = (bf16[2,256,256]{2,1,0:T(8,128)(2,1)S(1)}, bf16[2,256,256]{2,1,0:T(8,128)(2,1)S(1)}, u32[]{:S(2)}, u32[]{:S(2)}) collective-permute-start(bf16[2,256,256]{2,1,0:T(8,128)(2,1)S(1)} %get-tuple-element.49.rest_0_), channel_id=1, source_target_pairs={{0,1},{1,0},{2,3},{3,2},{4,5},{5,4},{6,7},{7,6},{8,10},{9,11},{10,... | collective-permute-start | bytes 786440 | tf_op jit(solution)/shard_map/ppermute | solution.py:223
  18.5 12.4 %collective-permute-start.10 = (bf16[2,256,256]{2,1,0:T(8,128)(2,1)S(1)}, bf16[2,256,256]{2,1,0:T(8,128)(2,1)S(1)}, u32[]{:S(2)}, u32[]{:S(2)}) collective-permute-start(bf16[2,256,256]{2,1,0:T(8,128)(2,1)S(1)} %shard_map.57), channel_id=1, source_target_pairs={{0,1},{1,0},{2,3},{3,2},{4,5},{5,4},{6,7},{7,6},{8,10},{9,11},{10,... | collective-permute-start | bytes 786440 | tf_op jit(solution)/shard_map/ppermute | solution.py:223
  21.2 5.6 %collective-permute-start.9 = (bf16[1,256,128]{2,1,0:T(8,128)(2,1)S(1)}, bf16[1,256,128]{2,1,0:T(8,128)(2,1)S(1)}, u32[]{:S(2)}, u32[]{:S(2)}) collective-permute-start(bf16[1,256,128]{2,1,0:T(8,128)(2,1)S(1)} %get-tuple-element.48), channel_id=1, source_target_pairs={{0,4},{1,5},{2,6},{3,7},{4,0},{5,1},{6,2},{7,3},{8,12},{9,13},{10,... | collective-permute-start | bytes 196616 | tf_op jit(solution)/shard_map/ppermute | solution.py:223
  23.9 7.0 %collective-permute-start.7 = (bf16[1,256,128]{2,1,0:T(8,128)(2,1)S(1)}, bf16[1,256,128]{2,1,0:T(8,128)(2,1)S(1)}, u32[]{:S(2)}, u32[]{:S(2)}) collective-permute-start(bf16[1,256,128]{2,1,0:T(8,128)(2,1)S(1)} %get-tuple-element.45), channel_id=1, source_target_pairs={{0,4},{1,5},{2,6},{3,7},{4,0},{5,1},{6,2},{7,3},{8,12},{9,13},{10,... | collective-permute-start | bytes 196616 | tf_op jit(solution)/shard_map/ppermute | solution.py:223
  24.3 6.6 %collective-permute-start.12 = (bf16[2,256,128]{2,1,0:T(8,128)(2,1)S(1)}, bf16[2,256,128]{2,1,0:T(8,128)(2,1)S(1)}, u32[]{:S(2)}, u32[]{:S(2)}) collective-permute-start(bf16[2,256,128]{2,1,0:T(8,128)(2,1)S(1)} %get-tuple-element.51), channel_id=1, source_target_pairs={{0,2},{1,3},{2,0},{3,1},{4,6},{5,7},{6,4},{7,5},{8,9},{9,8},{10,11... | collective-permute-start | bytes 393224 | tf_op jit(solution)/shard_map/ppermute | solution.py:223
  25.6 6.5 %collective-permute-start.14 = (bf16[2,256,128]{2,1,0:T(8,128)(2,1)S(1)}, bf16[2,256,128]{2,1,0:T(8,128)(2,1)S(1)}, u32[]{:S(2)}, u32[]{:S(2)}) collective-permute-start(bf16[2,256,128]{2,1,0:T(8,128)(2,1)S(1)} %get-tuple-element.54), channel_id=1, source_target_pairs={{0,2},{1,3},{2,0},{3,1},{4,6},{5,7},{6,4},{7,5},{8,9},{9,8},{10,11... | collective-permute-start | bytes 393224 | tf_op jit(solution)/shard_map/ppermute | solution.py:223
  31.0 5.9 %collective-permute-start.13 = (bf16[1,256,128]{2,1,0:T(8,128)(2,1)S(1)}, bf16[1,256,128]{2,1,0:T(8,128)(2,1)S(1)}, u32[]{:S(2)}, u32[]{:S(2)}) collective-permute-start(bf16[1,256,128]{2,1,0:T(8,128)(2,1)S(1)} %get-tuple-element.53), channel_id=1, source_target_pairs={{0,4},{1,5},{2,6},{3,7},{4,0},{5,1},{6,2},{7,3},{8,12},{9,13},{10,... | collective-permute-start | bytes 196616 | tf_op jit(solution)/shard_map/ppermute | solution.py:223
  32.2 5.4 %collective-permute-start.15 = (bf16[1,256,128]{2,1,0:T(8,128)(2,1)S(1)}, bf16[1,256,128]{2,1,0:T(8,128)(2,1)S(1)}, u32[]{:S(2)}, u32[]{:S(2)}) collective-permute-start(bf16[1,256,128]{2,1,0:T(8,128)(2,1)S(1)} %get-tuple-element.56), channel_id=1, source_target_pairs={{0,4},{1,5},{2,6},{3,7},{4,0},{5,1},{6,2},{7,3},{8,12},{9,13},{10,... | collective-permute-start | bytes 196616 | tf_op jit(solution)/shard_map/ppermute | solution.py:223
